TPU v7x, 32 devices: a whole 2x2x4 slice. The times are simulated.
32 devices in a mesh: dp: 8 (over z, x), tensor: 4 (over y, core).
Axes of the slice: x: 2, y: 2, z: 4, core: 2. Of those that a mesh axis runs over, the one named last changes fastest.
Arguments:
- tokens: bfloat16 [4096, 2048], P('dp'), may hold values from -6 to 6
- norm_attn: float32 [2048], replicated, may hold values from 0.5 to 1.5
- w_query: bfloat16 [2048, 2048], P(None, 'tensor'), may hold values from -0.125 to 0.125
- key_weight: bfloat16 [2048, 1024], P(None, 'tensor'), may hold values from -0.125 to 0.125
- value_weight: bfloat16 [2048, 1024], P(None, 'tensor'), may hold values from -0.125 to 0.125
- query_gain: float32 [128], replicated, may hold values from 0.5 to 1.5
- key_gain: float32 [128], replicated, may hold values from 0.5 to 1.5
- w_out: bfloat16 [2048, 2048], P('tensor'), may hold values from -2 to 2
- norm_mlp: float32 [2048], replicated, may hold values from 0.5 to 1.5
- w_gate: bfloat16 [2048, 6144], P(None, 'tensor'), may hold values from -0.125 to 0.125
- w_up: bfloat16 [2048, 6144], P(None, 'tensor'), may hold values from -0.125 to 0.125
- w_down: bfloat16 [6144, 2048], P('tensor'), may hold values from -0.078125 to 0.078125
- out_grad: bfloat16 [4096, 2048], P('dp'), may hold values from -6 to 6
- prefix_len: int32 [1], replicated, may hold values from 409 to 2048
Outputs:
- block_out: bfloat16 [4096, 2048], P('dp')
- tokens_grad: float32 [4096, 2048], P('dp')
- norm_attn_grad: float32 [2048], P('dp')
- w_query_grad: float32 [2048, 2048], P('dp', 'tensor')
- w_key_grad: float32 [2048, 1024], P('dp', 'tensor')
- w_value_grad: float32 [2048, 1024], P('dp', 'tensor')
- query_gain_grad: float32 [128], replicated
- key_gain_grad: float32 [128], replicated
- w_out_grad: float32 [2048, 2048], P('tensor', 'dp')
- norm_mlp_grad: float32 [2048], P('dp')
- w_gate_grad: float32 [2048, 6144], P('dp', 'tensor')
- w_up_grad: float32 [2048, 6144], P('dp', 'tensor')
- w_down_grad: float32 [6144, 2048], P('tensor', 'dp')
Inputs may be any that keep to these rules, and one draw needn't show every extreme that they name: `prefix_len`: leading tokens of each sequence that see one another in both directions.
All inputs are finite; a program needn't handle non-finite values.
Results may differ from a plain program's by a relative error of at most 0.024.
Values may be sent and summed in bfloat16 or wider, within the bound.
A program may use at most 256 MiB of HBM per device.

v0:
```python
import math

import jax
import jax.numpy as jnp
from jax import lax
from jax.sharding import PartitionSpec as P

GROUP = 8


norm_eps = 1e-06
rope_base = 1000000.0
masked_score = -1e30


def rms_scale(value_rows_all, norm_gain):
    return (
        value_rows_all
        * lax.rsqrt(jnp.mean(value_rows_all * value_rows_all, axis=-1, keepdims=True) + norm_eps)
        * norm_gain
    )


def rope_tables(positions, head_width):
    counter = jnp.arange(head_width // 2, dtype=jnp.float32)
    frequency = rope_base ** (-2.0 * counter / head_width)
    angles = positions.astype(jnp.float32)[:, None] * frequency[None, :]
    return (jnp.cos(angles)[:, None, :], jnp.sin(angles)[:, None, :])


def rope_apply(value_rows_all, cosine_table, sine_table):
    half_width = value_rows_all.shape[-1] // 2
    first_half = value_rows_all[..., :half_width]
    second_half = value_rows_all[..., half_width:]
    return jnp.concatenate(
        [
            first_half * cosine_table - second_half * sine_table,
            second_half * cosine_table + first_half * sine_table,
        ],
        axis=-1,
    )


def shards(
    tokens,
    norm_attn,
    w_query,
    key_weight,
    value_weight,
    query_gain,
    key_gain,
    w_out,
    norm_mlp,
    w_gate,
    w_up,
    w_down,
    out_grad,
    prefix_len,
):
    tok_rows = tokens.shape[0]
    head_width = query_gain.shape[0]
    q_heads = w_query.shape[1] // head_width
    kv_heads = key_weight.shape[1] // head_width
    repeat = q_heads // kv_heads
    kv_width = kv_heads * head_width
    group_size = GROUP
    seq_len = group_size * tok_rows
    scores_scale = 1.0 / math.sqrt(head_width)
    device = lax.axis_index("dp")
    seq_index = device // group_size
    member = device % group_size
    prefix = jnp.sum(jnp.where(jnp.arange(prefix_len.shape[0]) == seq_index, prefix_len, 0))
    positions = member * tok_rows + jnp.arange(tok_rows)
    last_pos = member * tok_rows + tok_rows - 1
    cosine_table, sine_table = rope_tables(positions, head_width)
    xfloat = tokens.astype(jnp.float32)
    h_one_f, attn_norm_pull = jax.vjp(rms_scale, xfloat, norm_attn)
    hidden_first = h_one_f.astype(jnp.bfloat16)
    q_proj = jnp.dot(hidden_first, w_query, preferred_element_type=jnp.float32)
    key_projected = jnp.dot(hidden_first, key_weight, preferred_element_type=jnp.float32)
    value_projected = jnp.dot(hidden_first, value_weight, preferred_element_type=jnp.float32)

    def heads_in(q_part, k_part, q_norm_gain, k_norm_gain):
        q_rot = rope_apply(
            rms_scale(q_part.reshape(tok_rows, q_heads, head_width), q_norm_gain),
            cosine_table,
            sine_table,
        )
        k_rot = rope_apply(
            rms_scale(k_part.reshape(tok_rows, kv_heads, head_width), k_norm_gain),
            cosine_table,
            sine_table,
        )
        return (q_rot, k_rot)

    (q_rot, k_rot), heads_pull = jax.vjp(heads_in, q_proj, key_projected, query_gain, key_gain)
    query_back = (
        q_rot.astype(jnp.bfloat16)
        .reshape(tok_rows, kv_heads, repeat, head_width)
        .transpose(1, 2, 0, 3)
    )
    kv_local = jnp.concatenate(
        [
            k_rot.astype(jnp.bfloat16).reshape(tok_rows, kv_width),
            value_projected.astype(jnp.bfloat16),
        ],
        axis=1,
    )

    def visible(first_row, row_count):
        key_pos = first_row + jnp.arange(row_count)
        return (key_pos[None, :] <= positions[:, None]) | (key_pos[None, :] < prefix)

    def needed(first_row):
        return (first_row <= last_pos) | (first_row < prefix)

    def split_block(kv_block):
        row_count = kv_block.shape[0]
        key_portion = kv_block[:, :kv_width].reshape(row_count, kv_heads, head_width)
        value_portion = kv_block[:, kv_width:].reshape(row_count, kv_heads, head_width)
        return (key_portion, value_portion)

    def forward_work(flash_state, kv_block, first_row):
        row_top, denom_sum, weighted_sum = flash_state
        key_portion, value_portion = split_block(kv_block)
        attention_scores = (
            jnp.einsum(
                "xfmu,axu->xfma", query_back, key_portion, preferred_element_type=jnp.float32
            )
            * scores_scale
        )
        allowed = visible(first_row, kv_block.shape[0])
        attention_scores = jnp.where(allowed, attention_scores, masked_score)
        new_top = jnp.maximum(row_top, jnp.max(attention_scores, axis=-1))
        weights = jnp.where(allowed, jnp.exp(attention_scores - new_top[..., None]), 0.0)
        rescale = jnp.exp(row_top - new_top)
        denom_sum = denom_sum * rescale + jnp.sum(weights, axis=-1)
        weighted_sum = weighted_sum * rescale[..., None] + jnp.einsum(
            "opwk,koz->opwz",
            weights.astype(jnp.bfloat16),
            value_portion,
            preferred_element_type=jnp.float32,
        )
        return (new_top, denom_sum, weighted_sum)

    flash_state = (
        jnp.full((kv_heads, repeat, tok_rows), masked_score, jnp.float32),
        jnp.zeros((kv_heads, repeat, tok_rows), jnp.float32),
        jnp.zeros((kv_heads, repeat, tok_rows, head_width), jnp.float32),
    )
    kv_all = lax.all_gather(kv_local, "dp", axis=0, tiled=True)
    kv_own = lax.dynamic_slice_in_dim(kv_all, seq_index * seq_len, seq_len, 0)
    fold_flash_state = flash_state
    row_count = kv_own.shape[0]
    block_row_list = math.gcd(row_count, 512)
    blocks = kv_own.reshape(row_count // block_row_list, block_row_list, kv_own.shape[1])
    starts = 0 + block_row_list * jnp.arange(row_count // block_row_list)

    def one_block(carry_state, scan_item):
        kv_block, block_start = scan_item
        return (
            lax.cond(
                needed(block_start),
                lambda state_in: forward_work(state_in, kv_block, block_start),
                lambda state_in: state_in,
                carry_state,
            ),
            None,
        )

    fold_flash_state, unused = lax.scan(one_block, fold_flash_state, (blocks, starts))
    flash_state = fold_flash_state
    row_top, denom_sum, weighted_sum = flash_state
    heads_f = weighted_sum / denom_sum[..., None]
    log_total = row_top + jnp.log(denom_sum)
    heads_b = (
        heads_f.transpose(2, 0, 1, 3).reshape(tok_rows, q_heads * head_width).astype(jnp.bfloat16)
    )
    attn = lax.psum(
        jnp.dot(heads_b, w_out, preferred_element_type=jnp.float32).astype(jnp.bfloat16), "tensor"
    ).astype(jnp.float32)
    middle = xfloat + attn
    h_two_f, mlp_norm_pull = jax.vjp(rms_scale, middle, norm_mlp)
    h_two = h_two_f.astype(jnp.bfloat16)
    gate_proj = jnp.dot(h_two, w_gate, preferred_element_type=jnp.float32)
    up_proj = jnp.dot(h_two, w_up, preferred_element_type=jnp.float32)

    def swiglu(gate_part, up_part):
        return jax.nn.silu(gate_part) * up_part

    hidden_f, swiglu_pull = jax.vjp(swiglu, gate_proj, up_proj)
    hidden = hidden_f.astype(jnp.bfloat16)
    mlp_out = lax.psum(
        jnp.dot(hidden, w_down, preferred_element_type=jnp.float32).astype(jnp.bfloat16), "tensor"
    ).astype(jnp.float32)
    block_out = (middle + mlp_out).astype(jnp.bfloat16)
    w_down_grad = jnp.dot(hidden.T, out_grad, preferred_element_type=jnp.float32)
    d_hidden = jnp.dot(out_grad, w_down.T, preferred_element_type=jnp.float32)
    d_gate_f, d_up_f = swiglu_pull(d_hidden)
    d_gate = d_gate_f.astype(jnp.bfloat16)
    d_up = d_up_f.astype(jnp.bfloat16)
    w_gate_grad = jnp.dot(h_two.T, d_gate, preferred_element_type=jnp.float32)
    w_up_grad = jnp.dot(h_two.T, d_up, preferred_element_type=jnp.float32)
    d_h_two = lax.psum(
        (
            jnp.dot(d_gate, w_gate.T, preferred_element_type=jnp.float32)
            + jnp.dot(d_up, w_up.T, preferred_element_type=jnp.float32)
        ).astype(jnp.bfloat16),
        "tensor",
    ).astype(jnp.float32)
    d_middle_part, norm_mlp_grad = mlp_norm_pull(d_h_two)
    d_middle = out_grad.astype(jnp.float32) + d_middle_part
    d_attn = d_middle.astype(jnp.bfloat16)
    w_out_grad = jnp.dot(heads_b.T, d_attn, preferred_element_type=jnp.float32)
    d_heads = jnp.dot(d_attn, w_out.T, preferred_element_type=jnp.float32).astype(jnp.bfloat16)
    heads_grouped_grad = d_heads.reshape(tok_rows, kv_heads, repeat, head_width).transpose(
        1, 2, 0, 3
    )
    row_delta = jnp.sum(heads_grouped_grad.astype(jnp.float32) * heads_f, axis=-1)

    def backward_work(dq_acc, kv_block, first_row):
        row_count = kv_block.shape[0]
        key_portion, value_portion = split_block(kv_block)
        attention_scores = (
            jnp.einsum(
                "xfmu,axu->xfma", query_back, key_portion, preferred_element_type=jnp.float32
            )
            * scores_scale
        )
        allowed = visible(first_row, row_count)
        probabilities = jnp.where(allowed, jnp.exp(attention_scores - log_total[..., None]), 0.0)
        probabilities_back = probabilities.astype(jnp.bfloat16)
        d_chances = jnp.einsum(
            "xfmu,axu->xfma", heads_grouped_grad, value_portion, preferred_element_type=jnp.float32
        )
        scores_gradient = (probabilities * (d_chances - row_delta[..., None])).astype(jnp.bfloat16)
        dq_acc = (
            dq_acc
            + jnp.einsum(
                "opwk,koz->opwz", scores_gradient, key_portion, preferred_element_type=jnp.float32
            )
            * scores_scale
        )
        d_keys = (
            jnp.einsum(
                "qnob,qnop->bqp", scores_gradient, query_back, preferred_element_type=jnp.float32
            )
            * scores_scale
        )
        d_vals = jnp.einsum(
            "qnob,qnop->bqp",
            probabilities_back,
            heads_grouped_grad,
            preferred_element_type=jnp.float32,
        )
        return (
            dq_acc,
            jnp.concatenate(
                [d_keys.reshape(row_count, kv_width), d_vals.reshape(row_count, kv_width)], axis=1
            ),
        )

    dq_start = jnp.zeros((kv_heads, repeat, tok_rows, head_width), jnp.float32)
    dq_acc = dq_start
    row_count = kv_own.shape[0]
    block_row_list = math.gcd(row_count, 512)
    blocks = kv_own.reshape(row_count // block_row_list, block_row_list, kv_own.shape[1])
    starts = 0 + block_row_list * jnp.arange(row_count // block_row_list)
    empty_term = jnp.zeros((block_row_list, 2 * kv_width), jnp.float32)

    def one_block(carry_acc, scan_item):
        kv_block, block_start = scan_item
        return lax.cond(
            needed(block_start),
            lambda acc_in: backward_work(acc_in, kv_block, block_start),
            lambda acc_in: (acc_in, empty_term),
            carry_acc,
        )

    dq_acc, kv_terms = lax.scan(one_block, dq_acc, (blocks, starts))
    dq_acc, own_term = (dq_acc, kv_terms.reshape(row_count, 2 * kv_width))
    spread = jnp.zeros((kv_all.shape[0], 2 * kv_width), jnp.float32)
    spread = lax.dynamic_update_slice_in_dim(spread, own_term, seq_index * seq_len, 0)
    kv_grad = lax.psum_scatter(
        spread.astype(jnp.bfloat16), "dp", scatter_dimension=0, tiled=True
    ).astype(jnp.float32)
    dq_rows = dq_acc.transpose(2, 0, 1, 3).reshape(tok_rows, q_heads, head_width)
    dk_rows = kv_grad[:, :kv_width].reshape(tok_rows, kv_heads, head_width)
    d_q_proj_f, d_k_proj_f, query_gain_part, key_gain_part = heads_pull((dq_rows, dk_rows))
    d_q_proj = d_q_proj_f.astype(jnp.bfloat16)
    d_k_proj = d_k_proj_f.astype(jnp.bfloat16)
    d_v_proj = kv_grad[:, kv_width:].astype(jnp.bfloat16)
    w_query_grad = jnp.dot(hidden_first.T, d_q_proj, preferred_element_type=jnp.float32)
    w_key_grad = jnp.dot(hidden_first.T, d_k_proj, preferred_element_type=jnp.float32)
    w_value_grad = jnp.dot(hidden_first.T, d_v_proj, preferred_element_type=jnp.float32)
    d_h_one = lax.psum(
        (
            jnp.dot(d_q_proj, w_query.T, preferred_element_type=jnp.float32)
            + jnp.dot(d_k_proj, key_weight.T, preferred_element_type=jnp.float32)
            + jnp.dot(d_v_proj, value_weight.T, preferred_element_type=jnp.float32)
        ).astype(jnp.bfloat16),
        "tensor",
    ).astype(jnp.float32)
    d_input_part, norm_attn_grad = attn_norm_pull(d_h_one)
    tokens_grad = d_middle + d_input_part
    query_gain_grad, key_gain_grad = lax.psum((query_gain_part, key_gain_part), ("dp", "tensor"))
    summed = (
        lax.psum_scatter(
            norm_attn_grad.astype(jnp.bfloat16), "dp", scatter_dimension=0, tiled=True
        ).astype(jnp.float32),
        lax.psum_scatter(
            w_query_grad.astype(jnp.bfloat16), "dp", scatter_dimension=0, tiled=True
        ).astype(jnp.float32),
        lax.psum_scatter(
            w_key_grad.astype(jnp.bfloat16), "dp", scatter_dimension=0, tiled=True
        ).astype(jnp.float32),
        lax.psum_scatter(
            w_value_grad.astype(jnp.bfloat16), "dp", scatter_dimension=0, tiled=True
        ).astype(jnp.float32),
        lax.psum_scatter(
            w_out_grad.astype(jnp.bfloat16), "dp", scatter_dimension=1, tiled=True
        ).astype(jnp.float32),
        lax.psum_scatter(
            norm_mlp_grad.astype(jnp.bfloat16), "dp", scatter_dimension=0, tiled=True
        ).astype(jnp.float32),
        lax.psum_scatter(
            w_gate_grad.astype(jnp.bfloat16), "dp", scatter_dimension=0, tiled=True
        ).astype(jnp.float32),
        lax.psum_scatter(
            w_up_grad.astype(jnp.bfloat16), "dp", scatter_dimension=0, tiled=True
        ).astype(jnp.float32),
        lax.psum_scatter(
            w_down_grad.astype(jnp.bfloat16), "dp", scatter_dimension=1, tiled=True
        ).astype(jnp.float32),
    )
    return (
        block_out,
        tokens_grad,
        summed[0],
        summed[1],
        summed[2],
        summed[3],
        query_gain_grad,
        key_gain_grad,
        summed[4],
        summed[5],
        summed[6],
        summed[7],
        summed[8],
    )


def solution(mesh):
    placed = (
        P("dp", None),
        P(),
        P(None, "tensor"),
        P(None, "tensor"),
        P(None, "tensor"),
        P(),
        P(),
        P("tensor", None),
        P(),
        P(None, "tensor"),
        P(None, "tensor"),
        P("tensor", None),
        P("dp", None),
        P(),
    )
    return jax.shard_map(
        shards,
        mesh=mesh,
        in_specs=placed,
        out_specs=(
            P("dp", None),
            P("dp", None),
            P("dp"),
            P("dp", "tensor"),
            P("dp", "tensor"),
            P("dp", "tensor"),
            P(),
            P(),
            P("tensor", "dp"),
            P("dp"),
            P("dp", "tensor"),
            P("dp", "tensor"),
            P("tensor", "dp"),
        ),
        check_vma=False,
    )
```

profile of v0, /device:TPU:0, one launch (start us, length us, event | category | flops | bytes accessed | tf_op | source)
XLA Modules:
  0.0 1261.5 jit_solution(1204481988051319848)
XLA Ops:
  21.3 72.2 %all-gather.2.cloned.1.call-done = bf16[4096,512]{0,1:T(8,128)(2,1)} async-done(((bf16[512,512]{0,1:T(8,128)(2,1)}), bf16[4096,512]{0,1:T(8,128)(2,1)}) %all-gather.2.cloned.1.call-update) | async-done | bytes 4194320 | tf_op jit(solution)/shard_map/all_gather | solution.py:151
  99.1 38.2 %while.31 = (s32[]{:T(128)}, f32[2,2,512]{2,1,0:T(2,128)S(1)}, f32[2,2,512]{2,1,0:T(2,128)S(1)}, f32[2,2,512,128]{3,2,1,0:T(8,128)}, s32[8]{0:T(128)S(1)}, /*ind...) while((s32[]{:T(128)}, f32[2,2,512]{2,1,0:T(2,128)S(1)}, ...), condition=%wide.region_8.9_spmd.clone, body=%wide.region_3.0_spmd.clone.sunk | while | flops 551557120 | bytes 27407720 | solution.py:171
  101.0 7.6 conditional.6
  110.6 7.6 conditional.6
  120.1 7.6 conditional.6
  144.1 87.4 %all-reduce.13.cloned.1.call-done = bf16[512,2048]{1,0:T(8,128)(2,1)} async-done(((bf16[512,2048]{1,0:T(8,128)(2,1)}), bf16[512,2048]{1,0:T(8,128)(2,1)}) %all-reduce.13.cloned.1.call-update) | async-done | bytes 2097168 | tf_op jit(solution)/shard_map/psum | solution.py:179
  236.2 8.7 fusion.67
  244.9 5.1 fusion.68
  250.0 9.8 multiply_convert_fusion.1
  259.8 5.4 fusion.69
  270.4 51.1 %all-reduce.15.cloned.1.call-done = bf16[512,2048]{1,0:T(8,128)(2,1)} async-done(((bf16[512,2048]{1,0:T(8,128)(2,1)}), bf16[512,2048]{1,0:T(8,128)(2,1)}) %all-reduce.15.cloned.1.call-update) | async-done | bytes 2097168 | tf_op jit(solution)/shard_map/psum | solution.py:204
  332.2 54.5 %while.32 = (s32[]{:T(128)}, f32[2,2,512,128]{3,2,1,0:T(8,128)}, bf16[8,512,512]{2,1,0:T(8,128)(2,1)}, s32[8]{0:T(128)S(1)}, s32[]{:T(128)}, /*index=5*/s32[]{:T...) while((s32[]{:T(128)}, f32[2,2,512,128]{3,2,1,0:T(8,128)}, ...), condition=%wide.region_18.19_spmd.clone, body=%wide.region_15.18_spmd.clone.sunk | while | flops 1355024384 | bytes 32544572 | solution.py:280
  334.1 10.2 conditional.7
  347.2 10.2 conditional.7
  360.4 10.2 conditional.7
  388.3 6.4 convolution_convert_fusion.3
  408.6 117.1 %reduce-scatter.9.cloned.1.call-done = bf16[512,512]{1,0:T(8,128)(2,1)} async-done(((bf16[4096,512]{1,0:T(8,128)(2,1)}), bf16[512,512]{1,0:T(8,128)(2,1)}) %reduce-scatter.9.cloned.1.call-update) | async-done | bytes 524304 | tf_op jit(solution)/shard_map/reduce_scatter | solution.py:284
  534.4 8.3 convolution_convert_fusion.5
  548.6 8.2 convolution_convert_fusion.2
  556.9 8.2 convolution_convert_fusion.1
  565.2 8.1 convolution_convert_fusion
  575.2 22.4 %reduce-scatter.17.cloned.1.call-done = bf16[512,256]{1,0:T(8,128)(2,1)} async-done(((bf16[512,2048]{1,0:T(8,128)(2,1)}), bf16[512,256]{1,0:T(8,128)(2,1)}) %reduce-scatter.17.cloned.1.call-update) | async-done | bytes 262160 | tf_op jit(solution)/shard_map/reduce_scatter | solution.py:320
  599.4 68.7 %reduce-scatter.11.cloned.1.call-done = bf16[256,512]{1,0:T(8,128)(2,1)} async-done(((bf16[2048,512]{1,0:T(8,128)(2,1)}), bf16[256,512]{1,0:T(8,128)(2,1)}) %reduce-scatter.11.cloned.1.call-update) | async-done | bytes 262160 | tf_op jit(solution)/shard_map/reduce_scatter | solution.py:311
  669.9 40.2 %all-reduce.6 = (f32[128]{0:T(128)}, f32[128]{0:T(128)}) all-reduce(f32[128]{0:T(128)S(1)} %get-tuple-element.380, f32[128]{0:T(128)S(1)} %get-tuple-element.382), channel_id=1, replica_groups=mesh['dp'=8,'tensor'=4] {'dp','tensor'}, use_global_device_ids=true, to_apply=%region_30.31 | all-reduce | flops 256 | bytes 2048 | tf_op jit(solution)/shard_map/psum | solution.py:306
  710.1 24.7 %reduce-scatter.13.cloned.1.call-done = bf16[256,256]{1,0:T(8,128)(2,1)} async-done(((bf16[2048,256]{1,0:T(8,128)(2,1)}), bf16[256,256]{1,0:T(8,128)(2,1)}) %reduce-scatter.13.cloned.1.call-update) | async-done | bytes 131088 | tf_op jit(solution)/shard_map/reduce_scatter | solution.py:314
  736.4 64.3 %reduce-scatter.15.cloned.1.call-done = bf16[256,256]{1,0:T(8,128)(2,1)} async-done(((bf16[2048,256]{1,0:T(8,128)(2,1)}), bf16[256,256]{1,0:T(8,128)(2,1)}) %reduce-scatter.15.cloned.1.call-update) | async-done | bytes 131088 | tf_op jit(solution)/shard_map/reduce_scatter | solution.py:317
  802.3 86.3 %all-reduce.17.cloned.1.call-done = (bf16[512,2048]{1,0:T(8,128)(2,1)}, bf16[512,2048]{1,0:T(8,128)(2,1)}) async-done(((bf16[512,2048]{1,0:T(8,128)(2,1)}, bf16[512,2048]{1,0:T(8,128)(2,1)}), (bf16[512,2048]{1,0:T(8,128)(2,1)}, bf16[512,2048]{1,0:T(8,128)(2,1)})) %all-reduce.17.cloned.1.call-update) | async-done | bytes 4194320 | tf_op jit(solution)/shard_map/psum | solution.py:193
  891.9 22.3 %all-reduce.7 = (bf16[2048]{0:T(1024)(128)(2,1)S(1)}, bf16[2048]{0:T(1024)(128)(2,1)S(1)}) all-reduce(bf16[2048]{0:T(1024)(128)(2,1)S(1)} %get-tuple-element.378, bf16[2048]{0:T(1024)(128)(2,1)S(1)} %get-tuple-element.376), channel_id=3, replica_groups=mesh['dp'=8,'tensor'=4] {'dp'}, use_global_device_ids=true, to_apply=%region_25.26.clone | all-reduce | flops 4096 | bytes 16384
  914.9 8.4 fusion.34
  923.3 86.7 %reduce-scatter.19.cloned.1.call-done = bf16[256,1536]{1,0:T(8,128)(2,1)} async-done(((bf16[2048,1536]{1,0:T(8,128)(2,1)}), bf16[256,1536]{1,0:T(8,128)(2,1)}) %reduce-scatter.19.cloned.1.call-update) | async-done | bytes 786448 | tf_op jit(solution)/shard_map/reduce_scatter | solution.py:326
  1012.5 118.3 %reduce-scatter.21.cloned.1.call-done = bf16[256,1536]{1,0:T(8,128)(2,1)} async-done(((bf16[2048,1536]{1,0:T(8,128)(2,1)}), bf16[256,1536]{1,0:T(8,128)(2,1)}) %reduce-scatter.21.cloned.1.call-update) | async-done | bytes 786448 | tf_op jit(solution)/shard_map/reduce_scatter | solution.py:329
  1133.3 118.6 %reduce-scatter.23.cloned.1.call-done = bf16[1536,256]{1,0:T(8,128)(2,1)} async-done(((bf16[1536,2048]{1,0:T(8,128)(2,1)}), bf16[1536,256]{1,0:T(8,128)(2,1)}) %reduce-scatter.23.cloned.1.call-update) | async-done | bytes 786448 | tf_op jit(solution)/shard_map/reduce_scatter | solution.py:332
  (323 shorter events, 166.6 us)
Async XLA Ops:
  7.2 134.1 %copy-start = (bf16[512,2048]{1,0:T(8,128)(2,1)S(1)}, bf16[512,2048]{1,0:T(8,128)(2,1)}, u32[]{:S(2)}) copy-start(bf16[512,2048]{1,0:T(8,128)(2,1)} %param.29) | copy-start | bytes 6291460
  7.2 5.8 copy-start.28
  7.2 5.8 copy-start.20
  7.2 86.3 %all-gather.2.cloned.1.call-start = ((), (), s32[]{:S(2)}) async-start(), calls=%async_computation.8 | async-start | bytes 4718592 | tf_op jit(solution)/shard_map/all_gather | solution.py:151
  7.3 5.7 copy-start.2
  9.6 6.1 copy-start.30
  15.6 215.9 %all-reduce.13.cloned.1.call-start = ((), (), s32[]{:S(2)}) async-start(), calls=%async_computation.9 | async-start | bytes 4194304 | tf_op jit(solution)/shard_map/psum | solution.py:179
  143.9 90.8 %copy-start.25 = (f32[2048]{0:T(1024)S(1)}, f32[2048]{0:T(1024)}, u32[]{:S(2)}) copy-start(f32[2048]{0:T(1024)} %param.30) | copy-start | bytes 24580
  143.9 177.7 %all-reduce.15.cloned.1.call-start = ((), (), s32[]{:S(2)}) async-start(), calls=%async_computation.10 | async-start | bytes 4194304 | tf_op jit(solution)/shard_map/psum | solution.py:204
  235.0 9.9 slice-start.2
  236.2 8.7 copy-start.17
  236.2 8.7 slice-start.3
  244.9 14.9 %slice-start = ((s8[6291456]{0:T(1024)(128)(4,1)}), s8[4194304]{0:T(1024)(128)(4,1)S(1)}, s32[]{:S(2)}) async-start(s8[6291456]{0:T(1024)(128)(4,1)} %bitcast.174), calls=%async_computation.20 | async-start | bytes 8388608
  250.0 9.8 slice-start.1
  259.8 5.4 copy-start.40
  269.9 255.8 %reduce-scatter.9.cloned.1.call-start = ((), (), s32[]{:S(2)}) async-start(), calls=%async_computation.11 | async-start | bytes 4718592 | tf_op jit(solution)/shard_map/reduce_scatter | solution.py:284
  386.7 210.9 %reduce-scatter.17.cloned.1.call-start = ((), (), s32[]{:S(2)}) async-start(), calls=%async_computation.15 | async-start | bytes 2359296 | tf_op jit(solution)/shard_map/reduce_scatter | solution.py:320
  394.7 273.4 %reduce-scatter.11.cloned.1.call-start = ((), (), s32[]{:S(2)}) async-start(), calls=%async_computation.12 | async-start | bytes 2359296 | tf_op jit(solution)/shard_map/reduce_scatter | solution.py:311
  394.9 9.3 copy-start.10
  408.5 120.3 %copy-start.13 = (f32[512,256]{0,1:T(8,128)S(1)}, f32[512,256]{0,1:T(8,128)}, u32[]{:S(2)}) copy-start(f32[512,256]{0,1:T(8,128)} %copy-done.12) | copy-start | bytes 1572868
  408.5 120.3 %copy-start.27 = (f32[512,2]{0,1:T(2,128)S(1)}, f32[512,2]{0,1:T(2,128)}, u32[]{:S(2)}) copy-start(f32[512,2]{0,1:T(2,128)} %copy-done.26) | copy-start | bytes 12292
  408.5 120.3 %copy-start.37 = (f32[128]{0:T(128)S(1)}, f32[128]{0:T(128)}, u32[]{:S(2)}) copy-start(f32[128]{0:T(128)} %param.28) | copy-start | bytes 1540
  408.6 120.5 %copy-start.35 = (f32[512,2]{0,1:T(2,128)S(1)}, f32[512,2]{0,1:T(2,128)}, u32[]{:S(2)}) copy-start(f32[512,2]{0,1:T(2,128)} %copy-done.34) | copy-start | bytes 12292
  408.6 326.2 %reduce-scatter.13.cloned.1.call-start = ((), (), s32[]{:S(2)}) async-start(), calls=%async_computation.13 | async-start | bytes 1179648 | tf_op jit(solution)/shard_map/reduce_scatter | solution.py:314
  531.3 269.5 %reduce-scatter.15.cloned.1.call-start = ((), (), s32[]{:S(2)}) async-start(), calls=%async_computation.14 | async-start | bytes 1179648 | tf_op jit(solution)/shard_map/reduce_scatter | solution.py:317
  534.3 354.3 %all-reduce.17.cloned.1.call-start = ((), (), s32[]{:S(2)}) async-start(), calls=%async_computation.19 | async-start | bytes 8388608 | tf_op jit(solution)/shard_map/psum | solution.py:193
  534.4 8.3 copy-start.22
  548.4 461.7 %reduce-scatter.19.cloned.1.call-start = ((), (), s32[]{:S(2)}) async-start(), calls=%async_computation.16 | async-start | bytes 7077888 | tf_op jit(solution)/shard_map/reduce_scatter | solution.py:326
  556.9 573.9 %reduce-scatter.21.cloned.1.call-start = ((), (), s32[]{:S(2)}) async-start(), calls=%async_computation.17 | async-start | bytes 7077888 | tf_op jit(solution)/shard_map/reduce_scatter | solution.py:329
  565.1 686.7 %reduce-scatter.23.cloned.1.call-start = ((), (), s32[]{:S(2)}) async-start(), calls=%async_computation.18 | async-start | bytes 7077888 | tf_op jit(solution)/shard_map/reduce_scatter | solution.py:332
  573.4 341.5 %copy-start.33 = (f32[512]{0:T(512)S(1)}, f32[512]{0:T(512)}, u32[]{:S(2)}) copy-start(f32[512]{0:T(512)} %copy-done.32) | copy-start | bytes 6148
  914.9 339.3 %copy-start.1 = (bf16[512,2048]{1,0:T(8,128)(2,1)S(1)}, bf16[512,2048]{1,0:T(8,128)(2,1)}, u32[]{:S(2)}) copy-start(bf16[512,2048]{1,0:T(8,128)(2,1)} %param.29) | copy-start | bytes 6291460
  (31 other events, 74.7 us)
Sparse Core Ops, SparseCore 0:
  15.7 77.6 all-gather.1
  144.0 87.4 all-reduce.12
  270.1 51.4 all-reduce.14
  386.9 138.8 reduce-scatter.8
  529.6 67.9 reduce-scatter.16
  601.4 66.6 reduce-scatter.10
  671.9 62.8 reduce-scatter.12
  738.2 62.5 reduce-scatter.14
  803.9 84.6 all-reduce.16
  892.0 117.9 reduce-scatter.18
  1013.6 117.1 reduce-scatter.20
  1134.3 117.5 reduce-scatter.22
where the time goes:
time: 1270 us; the launch traced here: 1260 us
  waiting for transfers between devices  918 us (72%)
  matrix products  130 us (10%)
  blocking collectives  62.5 us (5%)
  other arithmetic  58.4 us (5%)
  local copies, waits for them, and re-layouts  52.7 us (4%)
  loops' own time  21.8 us (2%)
  between operations  16.6 us (1%)
    reduce_scatter x1, waiting for transfers between devices, shards(): lax.psum_scatter(w_down_grad.astype(jnp.bfloat16), 'dp', scatter_dimensio...  119 us
    reduce_scatter x1, waiting for transfers between devices, shards(): lax.psum_scatter(w_up_grad.astype(jnp.bfloat16), 'dp', scatter_dimension=...  118 us
    reduce_scatter x1, waiting for transfers between devices, shards(): lax.psum_scatter(spread.astype(jnp.bfloat16), 'dp', scatter_dimension=0,...  117 us
    psum x1, waiting for transfers between devices, shards(): lax.psum(jnp.dot(heads_b, w_out, preferred_element_type=jnp.float32).asty...  87.4 us
    reduce_scatter x1, waiting for transfers between devices, shards(): lax.psum_scatter(w_gate_grad.astype(jnp.bfloat16), 'dp', scatter_dimensio...  86.7 us
    psum x1, waiting for transfers between devices, shards(): lax.psum(jnp.dot(hidden, w_down, preferred_element_type=jnp.float32).asty...  86.3 us
    all_gather x1, waiting for transfers between devices, shards(): kv_all = lax.all_gather(kv_local, 'dp', axis=0, tiled=True)  72.2 us
    reduce_scatter x1, waiting for transfers between devices, shards(): lax.psum_scatter(w_query_grad.astype(jnp.bfloat16), 'dp', scatter_dimensi...  68.7 us
  transfers between devices with their start and end apart: 12, of which 12 were waited for; matrix products, arithmetic and copies ran while one was open for 7% of the time, Pallas kernels for 0%

commit v1 on v0

v1 whole, which is shorter than its diff:
```python
import functools
import math

import jax
import jax.numpy as jnp
from jax import lax
from jax.experimental import pallas as pl
from jax.experimental.pallas import tpu as pltpu
from jax.sharding import PartitionSpec as P

F32 = jnp.float32
BF16 = jnp.bfloat16
EPS = 1e-06
ROPE_BASE = 1000000.0
MAX_PREFIX = 2048
VMEM_LIMIT = 56 * 2**20

NN = (((1,), (0,)), ((), ()))
NT = (((1,), (1,)), ((), ()))
TN = (((0,), (0,)), ((), ()))


def dot(left, right, dims=NN):
    return lax.dot_general(left, right, dims, preferred_element_type=F32)


def vmem(count):
    return [pl.BlockSpec(memory_space=pltpu.VMEM)] * count


def params():
    return pltpu.CompilerParams(vmem_limit_bytes=VMEM_LIMIT)


def roll_half(value):
    return pltpu.roll(value, value.shape[-1] // 2, 1)


def project_kernel(x_ref, g_ref, *refs, heads, normed, width):
    count = len(heads)
    w_refs = refs[:count]
    gain_refs = refs[count : 2 * count]
    cos_ref, sin_ref = refs[2 * count : 2 * count + 2]
    h_ref, out_ref = refs[2 * count + 2 : 2 * count + 4]
    raw_refs = refs[2 * count + 4 :]
    x = x_ref[...].astype(F32)
    h = (x * lax.rsqrt(jnp.mean(x * x, axis=1, keepdims=True) + EPS) * g_ref[...]).astype(BF16)
    h_ref[...] = h
    cos, sin = cos_ref[...], sin_ref[...]
    column = 0
    raw_at = 0
    for i in range(count):
        product = dot(h, w_refs[i][...])
        if normed[i]:
            raw_refs[raw_at][...] = product
            raw_at += 1
        for j in range(heads[i]):
            u = product[:, j * width : (j + 1) * width]
            if normed[i]:
                u = u * lax.rsqrt(jnp.mean(u * u, axis=1, keepdims=True) + EPS) * gain_refs[i][...]
                u = u * cos + roll_half(u) * sin
            out_ref[:, column : column + width] = u.astype(BF16)
            column += width


def project(x, gain, weights, gains, normed, cos, sin, name):
    rows, model = x.shape
    width = cos.shape[1]
    heads = tuple(w.shape[1] // width for w in weights)
    columns = sum(w.shape[1] for w in weights)
    raws = [w for w, n in zip(weights, normed) if n]
    return pl.pallas_call(
        functools.partial(project_kernel, heads=heads, normed=normed, width=width),
        out_shape=[
            jax.ShapeDtypeStruct((rows, model), BF16),
            jax.ShapeDtypeStruct((rows, columns), BF16),
        ]
        + [jax.ShapeDtypeStruct((rows, w.shape[1]), F32) for w in raws],
        in_specs=vmem(4 + 2 * len(weights)),
        out_specs=vmem(2 + len(raws)),
        compiler_params=params(),
        cost_estimate=pl.CostEstimate(
            flops=2 * rows * model * columns,
            bytes_accessed=4 * rows * model + 2 * model * columns,
            transcendentals=0,
        ),
        name=name,
    )(x, gain, *weights, *gains, cos, sin)


def unproject_kernel(d_ref, raw_ref, gain_ref, cos_ref, sin_ref, out_ref, gain_out_ref, *, width, plain):
    columns = d_ref.shape[1]
    cos, sin = cos_ref[...], sin_ref[...]
    gain = gain_ref[...]
    total = jnp.zeros((1, width), F32)
    for at in range(0, columns - plain, width):
        d = d_ref[:, at : at + width].astype(F32)
        c = d * cos - roll_half(d) * sin
        v = raw_ref[:, at : at + width]
        r = lax.rsqrt(jnp.mean(v * v, axis=1, keepdims=True) + EPS)
        n = v * r
        total = total + jnp.sum(c * n, axis=0, keepdims=True)
        gc = gain * c
        out_ref[:, at : at + width] = (r * (gc - n * jnp.mean(n * gc, axis=1, keepdims=True))).astype(BF16)
    if plain:
        out_ref[:, columns - plain :] = d_ref[:, columns - plain :].astype(BF16)
    gain_out_ref[...] = total


def unproject(d, raw, gain, cos, sin, plain, name):
    rows, columns = d.shape
    width = cos.shape[1]
    return pl.pallas_call(
        functools.partial(unproject_kernel, width=width, plain=plain),
        out_shape=[jax.ShapeDtypeStruct((rows, columns), BF16), jax.ShapeDtypeStruct((1, width), F32)],
        in_specs=vmem(5),
        out_specs=vmem(2),
        compiler_params=params(),
        cost_estimate=pl.CostEstimate(
            flops=20 * rows * columns, bytes_accessed=10 * rows * columns, transcendentals=0
        ),
        name=name,
    )(d, raw, gain, cos, sin)


def block_flags(scalar_ref, slot, rows):
    member, prefix = scalar_ref[0], scalar_ref[1]
    other = scalar_ref[2 + slot]
    key0 = other * rows
    needed = (other >= 0) & ((other <= member) | (key0 < prefix))
    full = (other < member) | (key0 + rows <= prefix)
    return key0, needed, full


def visible(shape, key0, row0, prefix):
    key_pos = key0 + lax.broadcasted_iota(jnp.int32, shape, 1)
    row_pos = row0 + lax.broadcasted_iota(jnp.int32, shape, 0)
    return (key_pos <= row_pos) | (key_pos < prefix)


def attn_fwd_kernel(scalar_ref, q_ref, *refs, slots, kv_heads, repeat, width, tile, coef, first, last):
    kv_refs = refs[:slots]
    rest = refs[slots:]
    if not first:
        acc_in, rest = rest[0], rest[1:]
    if last:
        o_ref, lse_ref, acc = rest
    else:
        (acc,) = rest
    rows = q_ref.shape[0]
    kv_width = kv_heads * width
    if first:
        acc[...] = jnp.zeros_like(acc)
    else:
        acc[...] = acc_in[...]
    ones = jnp.ones((rows, width), BF16)
    row0 = scalar_ref[0] * rows
    prefix = scalar_ref[1]
    for slot in range(slots):
        key0, needed, full = block_flags(scalar_ref, slot, rows)

        def work(masked, slot=slot, key0=key0):
            for h in range(kv_heads):
                k = kv_refs[slot][:, h * width : (h + 1) * width]
                v = kv_refs[slot][:, kv_width + h * width : kv_width + (h + 1) * width]
                v = jnp.concatenate([v, ones], axis=1)
                for g in range(repeat):
                    head = h * repeat + g
                    for at in range(0, rows, tile):
                        q = q_ref[at : at + tile, head * width : (head + 1) * width]
                        p = jnp.exp2(dot(q, k, NT) * coef)
                        if masked:
                            p = jnp.where(visible(p.shape, key0, row0 + at, prefix), p, 0.0)
                        acc[at : at + tile, 2 * head * width : 2 * (head + 1) * width] += dot(
                            p.astype(BF16), v
                        )

        pl.when(needed & full)(functools.partial(work, False))
        pl.when(needed & jnp.logical_not(full))(functools.partial(work, True))
    if last:
        for head in range(kv_heads * repeat):
            total = acc[:, (2 * head + 1) * width : (2 * head + 2) * width]
            o_ref[:, head * width : (head + 1) * width] = (
                acc[:, 2 * head * width : (2 * head + 1) * width] / total
            ).astype(BF16)
            lse_ref[:, head * width : (head + 1) * width] = jnp.log2(total) * (1.0 / coef)


def attn_fwd(scalars, q, blocks, acc, last, dims):
    kv_heads, repeat, width = dims
    rows = q.shape[0]
    columns = kv_heads * repeat * width
    first = acc is None
    acc_shape = jax.ShapeDtypeStruct((rows, 2 * columns), F32)
    if last:
        out_shape = [
            jax.ShapeDtypeStruct((rows, columns), BF16),
            jax.ShapeDtypeStruct((rows, columns), F32),
        ]
        scratch = [pltpu.VMEM(acc_shape.shape, F32)]
    else:
        out_shape = [acc_shape]
        scratch = []
    slots = len(blocks)
    args = [scalars, q, *blocks] + ([] if first else [acc])
    return pl.pallas_call(
        functools.partial(
            attn_fwd_kernel,
            slots=slots,
            kv_heads=kv_heads,
            repeat=repeat,
            width=width,
            tile=min(rows, 256),
            coef=math.log2(math.e) / math.sqrt(width),
            first=first,
            last=last,
        ),
        out_shape=out_shape,
        in_specs=[pl.BlockSpec(memory_space=pltpu.SMEM)] + vmem(len(args) - 1),
        out_specs=vmem(len(out_shape)),
        scratch_shapes=scratch,
        compiler_params=params(),
        cost_estimate=pl.CostEstimate(
            flops=slots * 8 * rows * rows * columns,
            bytes_accessed=12 * rows * columns,
            transcendentals=slots * rows * rows * kv_heads * repeat,
        ),
        name="attn_fwd",
    )(*args)


def split_three(value):
    high = value.astype(BF16)
    left = value - high.astype(F32)
    mid = left.astype(BF16)
    return high.astype(F32), mid.astype(F32), (left - mid.astype(F32)).astype(BF16).astype(F32)


def attn_prep_kernel(q_ref, do_ref, o_ref, lse_ref, qx_ref, dox_ref, *, heads, width):
    rows = q_ref.shape[0]
    lane = lax.broadcasted_iota(jnp.int32, (rows, width), 1)

    def extra(value):
        a, b, c = split_three(value)
        return jnp.where(lane == 0, a, jnp.where(lane == 1, b, jnp.where(lane == 2, c, 0.0))).astype(BF16)

    for head in range(heads):
        at = slice(head * width, (head + 1) * width)
        qx_ref[head, :, :width] = q_ref[:, at]
        qx_ref[head, :, width:] = extra(lse_ref[:, at])
        d = do_ref[:, at]
        delta = jnp.sum(d.astype(F32) * o_ref[:, at].astype(F32), axis=1, keepdims=True)
        dox_ref[head, :, :width] = d
        dox_ref[head, :, width:] = extra(jnp.broadcast_to(delta, (rows, width)))


def attn_prep(q, d_out, out, lse, width):
    rows, columns = q.shape
    heads = columns // width
    return pl.pallas_call(
        functools.partial(attn_prep_kernel, heads=heads, width=width),
        out_shape=[jax.ShapeDtypeStruct((heads, rows, 2 * width), BF16)] * 2,
        in_specs=vmem(4),
        out_specs=vmem(2),
        compiler_params=params(),
        cost_estimate=pl.CostEstimate(
            flops=20 * rows * columns, bytes_accessed=14 * rows * columns, transcendentals=0
        ),
        name="attn_prep",
    )(q, d_out, out, lse)


def attn_bwd_kernel(scalar_ref, qx_ref, dox_ref, *refs, slots, kv_heads, repeat, width, coef, scale, first, last):
    kv_refs = refs[:slots]
    rest = refs[slots:]
    if not first:
        dq_in, rest = rest[0], rest[1:]
    dq_ref = rest[0]
    dkv_refs = rest[1:]
    rows = qx_ref.shape[1]
    kv_width = kv_heads * width
    if first:
        dq_ref[...] = jnp.zeros_like(dq_ref)
    else:
        dq_ref[...] = dq_in[...]
    lane = lax.broadcasted_iota(jnp.int32, (rows, width), 1)
    minus = jnp.where(lane < 3, -1.0, 0.0).astype(BF16)
    row0 = scalar_ref[0] * rows
    prefix = scalar_ref[1]
    for slot in range(slots):
        key0, needed, full = block_flags(scalar_ref, slot, rows)

        def work(masked, slot=slot, key0=key0):
            for h in range(kv_heads):
                k_at = slice(h * width, (h + 1) * width)
                v_at = slice(kv_width + h * width, kv_width + (h + 1) * width)
                k = kv_refs[slot][:, k_at]
                v = kv_refs[slot][:, v_at]
                kx = jnp.concatenate([k, minus], axis=1)
                vx = jnp.concatenate([v, minus], axis=1)
                dk = jnp.zeros((rows, width), F32)
                dv = jnp.zeros((rows, width), F32)
                for g in range(repeat):
                    head = h * repeat + g
                    qx = qx_ref[head]
                    dox = dox_ref[head]
                    p = jnp.exp2(dot(qx, kx, NT) * coef)
                    if masked:
                        p = jnp.where(visible(p.shape, key0, row0, prefix), p, 0.0)
                    ds = (p * dot(dox, vx, NT)).astype(BF16)
                    dv += dot(p.astype(BF16), dox[:, :width], TN)
                    dk += dot(ds, qx[:, :width], TN)
                    dq_ref[:, head * width : (head + 1) * width] += dot(ds, k)
                dkv_refs[slot][:, k_at] = (dk * scale).astype(BF16)
                dkv_refs[slot][:, v_at] = dv.astype(BF16)

        pl.when(needed & full)(functools.partial(work, False))
        pl.when(needed & jnp.logical_not(full))(functools.partial(work, True))

        @pl.when(jnp.logical_not(needed))
        def _(slot=slot):
            dkv_refs[slot][...] = jnp.zeros_like(dkv_refs[slot])

    if last:
        dq_ref[...] = dq_ref[...] * scale


def attn_bwd(scalars, qx, dox, blocks, dq, last, dims):
    kv_heads, repeat, width = dims
    rows = qx.shape[1]
    columns = kv_heads * repeat * width
    first = dq is None
    slots = len(blocks)
    args = [scalars, qx, dox, *blocks] + ([] if first else [dq])
    out_shape = [jax.ShapeDtypeStruct((rows, columns), F32)] + [
        jax.ShapeDtypeStruct(b.shape, BF16) for b in blocks
    ]
    return pl.pallas_call(
        functools.partial(
            attn_bwd_kernel,
            slots=slots,
            kv_heads=kv_heads,
            repeat=repeat,
            width=width,
            coef=math.log2(math.e) / math.sqrt(width),
            scale=1.0 / math.sqrt(width),
            first=first,
            last=last,
        ),
        out_shape=out_shape,
        in_specs=[pl.BlockSpec(memory_space=pltpu.SMEM)] + vmem(len(args) - 1),
        out_specs=vmem(len(out_shape)),
        compiler_params=params(),
        cost_estimate=pl.CostEstimate(
            flops=slots * 20 * rows * rows * columns,
            bytes_accessed=16 * rows * columns,
            transcendentals=slots * rows * rows * kv_heads * repeat,
        ),
        name="attn_bwd",
    )(*args)


def rms_parts(value):
    r = lax.rsqrt(jnp.mean(value * value, axis=-1, keepdims=True) + EPS)
    return r, value * r


def rms_back(r, n, gain, c):
    gc = gain * c
    return r * (gc - n * jnp.mean(n * gc, axis=-1, keepdims=True))


def shards(
    dp_size,
    tensor_size,
    tokens,
    norm_attn,
    w_query,
    key_weight,
    value_weight,
    query_gain,
    key_gain,
    w_out,
    norm_mlp,
    w_gate,
    w_up,
    w_down,
    out_grad,
    prefix_len,
):
    rows, model = tokens.shape
    width = query_gain.shape[0]
    kv_heads = key_weight.shape[1] // width
    repeat = w_query.shape[1] // key_weight.shape[1]
    dims = (kv_heads, repeat, width)
    group = dp_size // prefix_len.shape[0]
    planes = dp_size // 2
    group_planes = group // 2
    half = rows // 2
    shard = model // dp_size
    assert tensor_size == 4 and MAX_PREFIX <= 4 * rows

    device = lax.axis_index("dp")
    core = lax.axis_index("tensor") % 2
    x_at = device % 2
    z_at = device // 2
    sequence = device // group
    member = device % group
    plane = member // 2
    prefix = jnp.sum(jnp.where(jnp.arange(prefix_len.shape[0]) == sequence, prefix_len, 0))

    core_pairs = [(t, t ^ 1) for t in range(tensor_size)]
    y_pairs = [(t, t ^ 2) for t in range(tensor_size)]
    x_pairs = [(d, d ^ 1) for d in range(dp_size)]

    def core_swap(value):
        return lax.ppermute(value, "tensor", core_pairs)

    def y_swap(value):
        return lax.ppermute(value, "tensor", y_pairs)

    def x_swap(value):
        return lax.ppermute(value, "dp", x_pairs)

    def plane_of(d):
        return (d % group) // 2

    def own_half(value):
        return lax.dynamic_slice_in_dim(value, core * half, half, 0)

    def other_half(value):
        return lax.dynamic_slice_in_dim(value, (1 - core) * half, half, 0)

    def join(mine, theirs):
        return jnp.where(
            core == 0, jnp.concatenate([mine, theirs], 0), jnp.concatenate([theirs, mine], 0)
        )

    def sum_tensor(left, right):
        away = dot(other_half(left), right).astype(BF16)
        came = core_swap(away)
        both = (dot(own_half(left), right) + came.astype(F32)).astype(BF16)
        return both.astype(F32) + y_swap(both).astype(F32)

    def columns_of(value, side):
        cut = value.reshape(value.shape[0], planes, 2, shard)
        return lax.dynamic_index_in_dim(cut, side, 2, keepdims=False).reshape(
            value.shape[0], planes * shard
        )

    def gather_columns(mine):
        came = x_swap(columns_of(mine, 1 - x_at))
        return join(came, core_swap(came))

    def scatter_z(stack):
        up_carry = stack(jnp.clip(planes - 1 + z_at, 0, planes - 1))
        down_carry = stack(jnp.clip(1 - planes + z_at, 0, planes - 1))
        for step in range(1, planes):
            up_pairs = [
                (2 * z + x, 2 * z + 2 + x) for z in range(planes - 1) for x in range(2) if z <= step - 1
            ]
            down_pairs = [
                (2 * (planes - 1 - z) + x, 2 * (planes - 2 - z) + x)
                for z in range(planes - 1)
                for x in range(2)
                if z <= step - 1
            ]
            up = lax.ppermute(up_carry, "dp", up_pairs)
            down = lax.ppermute(down_carry, "dp", down_pairs)
            if step < planes - 1:
                up_carry = up + stack(jnp.clip(planes - step - 1 + z_at, 0, planes - 1))
                down_carry = down + stack(jnp.clip(step + 1 - planes + z_at, 0, planes - 1))
        return stack(z_at).astype(F32) + up.astype(F32) + down.astype(F32)

    def scatter_rows(left_own, left_came, right_own, right_came):
        part = dot(left_own, right_own, TN) + dot(left_came, right_came, TN)
        part = part.astype(BF16)
        return scatter_z(lambda j: lax.dynamic_slice_in_dim(part, j * shard, shard, 0))

    def scatter_columns(left_own, left_came, right_own, right_came):
        part = dot(left_own, right_own, TN) + dot(left_came, right_came, TN)
        part = part.astype(BF16)
        return scatter_z(lambda j: lax.dynamic_slice_in_dim(part, j * shard, shard, 1))

    def sum_all(value, axes):
        for axis, bit in axes:
            size = dp_size if axis == "dp" else tensor_size
            value = value + lax.ppermute(value, axis, [(d, d ^ bit) for d in range(size)])
        return value

    dp_bits = []
    bit = 1
    while bit < dp_size:
        dp_bits.append(("dp", bit))
        bit *= 2

    positions = (member * rows + jnp.arange(rows)).astype(F32)
    counter = jnp.arange(width // 2, dtype=F32)
    angles = positions[:, None] * (ROPE_BASE ** (-2.0 * counter / width))[None, :]
    cos, sin = jnp.cos(angles), jnp.sin(angles)
    cos = jnp.concatenate([cos, cos], axis=1)
    sin = jnp.concatenate([-sin, sin], axis=1)
    norm_attn_row = norm_attn[None, :]
    norm_mlp_row = norm_mlp[None, :]
    q_gain_row = query_gain[None, :]
    k_gain_row = key_gain[None, :]

    h_one, kv, k_raw = project(
        tokens,
        norm_attn_row,
        (key_weight, value_weight),
        (k_gain_row, k_gain_row),
        (True, False),
        cos,
        sin,
        "project_kv",
    )
    later_pairs = [(d, d + 2) for d in range(dp_size) if plane_of(d) < group_planes - 1]
    to_first_pairs = [(d, d - 2) for d in range(dp_size) if plane_of(d) == 1]
    kv_own = [kv]
    came = kv
    for step in range(1, group_planes):
        came = lax.ppermute(came, "dp", later_pairs)
        kv_own.append(came)
    if group_planes > 1:
        kv_own[1] = kv_own[1] + lax.ppermute(kv, "dp", to_first_pairs)
    kv_far = [x_swap(b) for b in kv_own]
    scalars = []
    for step in range(group_planes):
        if step == 1:
            there = jnp.where(plane == 0, 1, plane - 1)
        else:
            there = plane - step
        mine = jnp.where(there >= 0, 2 * there + x_at, -1)
        far = jnp.where(there >= 0, 2 * there + 1 - x_at, -1)
        scalars.append(jnp.stack([member, prefix, mine, far]).astype(jnp.int32))

    _, q, q_raw = project(
        tokens, norm_attn_row, (w_query,), (q_gain_row,), (True,), cos, sin, "project_q"
    )
    d_hidden = dot(out_grad, w_down, NT)

    acc = None
    for step in range(group_planes):
        last = step == group_planes - 1
        outs = attn_fwd(scalars[step], q, [kv_own[step], kv_far[step]], acc, last, dims)
        acc = outs[0]
    heads_b, lse = outs

    x_half = own_half(tokens).astype(F32)
    middle = x_half + sum_tensor(heads_b, w_out)
    r_two, n_two = rms_parts(middle)
    h_two_half = (n_two * norm_mlp_row).astype(BF16)
    h_two = join(h_two_half, core_swap(h_two_half))
    gate_proj = dot(h_two, w_gate)
    up_proj = dot(h_two, w_up)
    sig = jax.nn.sigmoid(gate_proj)
    silu = gate_proj * sig
    hidden = (silu * up_proj).astype(BF16)
    d_gate = (d_hidden * up_proj * sig * (1.0 + gate_proj * (1.0 - sig))).astype(BF16)
    d_up = (d_hidden * silu).astype(BF16)

    def d_h_two_part(which):
        return dot(which(d_gate), w_gate, NT) + dot(which(d_up), w_up, NT)

    away = d_h_two_part(other_half).astype(BF16)
    both = (d_h_two_part(own_half) + core_swap(away).astype(F32)).astype(BF16)
    d_h_two = both.astype(F32) + y_swap(both).astype(F32)
    out_grad_half = own_half(out_grad)
    d_middle_half = out_grad_half.astype(F32) + rms_back(r_two, n_two, norm_mlp_row, d_h_two)
    norm_mlp_part = jnp.sum(d_h_two * n_two, axis=0)
    d_attn_half = d_middle_half.astype(BF16)
    d_attn = join(d_attn_half, core_swap(d_attn_half))
    d_heads = dot(d_attn, w_out, NT).astype(BF16)

    og_came = gather_columns(out_grad_half)
    hidden_came = x_swap(hidden)
    w_down_grad = scatter_columns(hidden, hidden_came, columns_of(out_grad, x_at), og_came)
    h_two_came = gather_columns(h_two_half)
    h_two_cols = columns_of(h_two, x_at)
    w_gate_grad = scatter_rows(h_two_cols, h_two_came, d_gate, x_swap(d_gate))
    w_up_grad = scatter_rows(h_two_cols, h_two_came, d_up, x_swap(d_up))

    mlp_out = sum_tensor(hidden, w_down)
    block_half = (middle + mlp_out).astype(BF16)
    block_out = join(block_half, core_swap(block_half))

    qx, dox = attn_prep(q, d_heads, heads_b, lse, width)
    dq = None
    sums = [None] * group_planes
    for step in reversed(range(group_planes)):
        dq, d_own, d_far = attn_bwd(
            scalars[step], qx, dox, [kv_own[step], kv_far[step]], dq, step == 0, dims
        )
        sums[step] = (d_own, x_swap(d_far))
    earlier_pairs = [(d, d - 2) for d in range(dp_size) if plane_of(d) > 0]
    from_first_pairs = [(d, d + 2) for d in range(dp_size) if plane_of(d) == 0]
    came = None
    for step in reversed(range(1, group_planes)):
        carry = sums[step][0].astype(F32) + sums[step][1].astype(F32)
        if came is not None:
            carry = carry + came.astype(F32)
        carry = carry.astype(BF16)
        pairs = [(a, b) for a, b in earlier_pairs if plane_of(a) >= step]
        came = lax.ppermute(carry, "dp", pairs)
    kv_grad = sums[0][0].astype(F32) + sums[0][1].astype(F32)
    if group_planes > 1:
        kv_grad = kv_grad + came.astype(F32) + lax.ppermute(carry, "dp", from_first_pairs).astype(F32)

    d_attn_came = gather_columns(d_attn_half)
    w_out_grad = scatter_columns(heads_b, x_swap(heads_b), columns_of(d_attn, x_at), d_attn_came)

    kv_width = kv_heads * width
    dq_b, q_gain_part = unproject(dq, q_raw, q_gain_row, cos, sin, 0, "unproject_q")
    dkv_b, k_gain_part = unproject(kv_grad, k_raw, k_gain_row, cos, sin, kv_width, "unproject_kv")
    h_one_came = gather_columns(own_half(h_one))
    h_one_cols = columns_of(h_one, x_at)
    w_query_grad = scatter_rows(h_one_cols, h_one_came, dq_b, x_swap(dq_b))
    w_kv_grad = scatter_rows(h_one_cols, h_one_came, dkv_b, x_swap(dkv_b))

    def d_h_one_part(which):
        dkv_rows = which(dkv_b)
        return (
            dot(which(dq_b), w_query, NT)
            + dot(dkv_rows[:, :kv_width], key_weight, NT)
            + dot(dkv_rows[:, kv_width:], value_weight, NT)
        )

    away = d_h_one_part(other_half)
    mine = d_h_one_part(own_half)
    x_other = other_half(tokens).astype(F32)
    r_own, n_own = rms_parts(x_half)
    r_other, n_other = rms_parts(x_other)
    norm_attn_part = jnp.sum(away * n_other + mine * n_own, axis=0)
    both = (mine + core_swap(away.astype(BF16)).astype(F32)).astype(BF16)
    d_h_one = (both.astype(F32) + y_swap(both).astype(F32)).astype(BF16)
    d_h_one_other = core_swap(d_h_one)
    d_middle_other = core_swap(d_middle_half)
    grad_own = d_middle_half + rms_back(r_own, n_own, norm_attn_row, d_h_one.astype(F32))
    grad_other = d_middle_other + rms_back(r_other, n_other, norm_attn_row, d_h_one_other.astype(F32))
    tokens_grad = join(grad_own, grad_other)

    norm_mlp_sum = sum_all(norm_mlp_part, [("tensor", 1)] + dp_bits)
    small = jnp.concatenate([norm_attn_part, q_gain_part[0], k_gain_part[0]])
    small = sum_all(small, [("tensor", 1), ("tensor", 2)] + dp_bits)
    norm_mlp_grad = lax.dynamic_slice_in_dim(norm_mlp_sum, device * shard, shard, 0)
    norm_attn_grad = lax.dynamic_slice_in_dim(small, device * shard, shard, 0)
    return (
        block_out,
        tokens_grad,
        norm_attn_grad,
        w_query_grad,
        w_kv_grad[:, :kv_width],
        w_kv_grad[:, kv_width:],
        small[model : model + width],
        small[model + width :],
        w_out_grad,
        norm_mlp_grad,
        w_gate_grad,
        w_up_grad,
        w_down_grad,
    )


def solution(mesh):
    placed = (
        P("dp", None),
        P(),
        P(None, "tensor"),
        P(None, "tensor"),
        P(None, "tensor"),
        P(),
        P(),
        P("tensor", None),
        P(),
        P(None, "tensor"),
        P(None, "tensor"),
        P("tensor", None),
        P("dp", None),
        P(),
    )
    return jax.shard_map(
        functools.partial(shards, mesh.shape["dp"], mesh.shape["tensor"]),
        mesh=mesh,
        in_specs=placed,
        out_specs=(
            P("dp", None),
            P("dp", None),
            P("dp"),
            P("dp", "tensor"),
            P("dp", "tensor"),
            P("dp", "tensor"),
            P(),
            P(),
            P("tensor", "dp"),
            P("dp"),
            P("dp", "tensor"),
            P("dp", "tensor"),
            P("tensor", "dp"),
        ),
        check_vma=False,
    )
```

time: 1270 us -> 697 us (0.55)
  waiting for transfers between devices: 918 us -> 191 us
  starting transfers between devices: 1.5 us -> 194 us
  Pallas kernels: 0 us -> 90 us
  blocking collectives: 62.5 us -> 0 us
  matrix products: 130 us -> 97.4 us
  loops' own time: 21.8 us -> 0 us
  between operations: 16.6 us -> 3.27 us
    reduce_scatter x8 -> x0, waiting for transfers between devices: 621 us -> none  [the longest x1 119 us: shards(): lax.psum_scatter(w_down_grad.astype(jnp.bfloat16), 'dp', scatter_dimensio...]
    psum x3 -> x0, waiting for transfers between devices: 225 us -> none  [the longest x1 87.4 us: shards(): lax.psum(jnp.dot(heads_b, w_out, preferred_element_type=jnp.float32).asty...]
    ppermute x0 -> x88, starting transfers between devices: none -> 194 us  [the longest x18 113 us: scatter_z(): up = lax.ppermute(up_carry, 'dp', up_pairs)]
    ppermute x0 -> x88, waiting for transfers between devices: none -> 191 us  [the longest x18 90.1 us: x_swap(): return lax.ppermute(value, 'dp', x_pairs)]
    pallas_call x0 -> x13, Pallas kernels: none -> 90 us  [the longest x4 37.5 us: attn_bwd(): pl.pallas_call(functools.partial(attn_bwd_kernel, slots=slots, kv_heads=k...]
    all_gather x1 -> x0, waiting for transfers between devices: 72.2 us -> none  [shards(): kv_all = lax.all_gather(kv_local, 'dp', axis=0, tiled=True)]
    psum x1 -> x0, blocking collectives: 40.2 us -> none  [shards(): lax.psum((query_gain_part, key_gain_part), ('dp', 'tensor'))]
    dot_general x42 -> x30, matrix products: 130 us -> 97.4 us  [dot(): return lax.dot_general(left, right, dims, preferred_element_type=F32)]
  transfers between devices with their start and end apart: 12 -> 88, of which waited for: 12 -> 31; matrix products, arithmetic and copies ran while one was open for 7% -> 28% of each run, Pallas kernels for 0% -> 10%
where the time goes in v1:
time: 697 us; the launch traced here: 686 us
  starting transfers between devices  194 us (28%)
  waiting for transfers between devices  191 us (27%)
  matrix products  97.4 us (14%)
  Pallas kernels  90 us (13%)
  local copies, waits for them, and re-layouts  62.2 us (9%)
  other arithmetic  47.9 us (7%)
    ppermute x18, starting transfers between devices, scatter_z(): up = lax.ppermute(up_carry, 'dp', up_pairs)  113 us
    dot_general x30, matrix products, dot(): return lax.dot_general(left, right, dims, preferred_element_type=F32)  97.4 us
    ppermute x18, waiting for transfers between devices, x_swap(): return lax.ppermute(value, 'dp', x_pairs)  90.1 us
    ppermute x18, waiting for transfers between devices, scatter_z(): up = lax.ppermute(up_carry, 'dp', up_pairs)  50.3 us
    pallas_call x4, Pallas kernels, attn_bwd(): pl.pallas_call(functools.partial(attn_bwd_kernel, slots=slots, kv_heads=k...  37.5 us
    pallas_call x4, Pallas kernels, attn_fwd(): pl.pallas_call(functools.partial(attn_fwd_kernel, slots=slots, kv_heads=k...  29.9 us
    concatenate x8, local copies, waits for them, and re-layouts, join(): jnp.concatenate([mine, theirs], 0)  23.3 us
    ppermute x18, starting transfers between devices, x_swap(): return lax.ppermute(value, 'dp', x_pairs)  21 us
  transfers between devices with their start and end apart: 88, of which 31 were waited for; matrix products, arithmetic and copies ran while one was open for 28% of the time, Pallas kernels for 10%

profile of v1, /device:TPU:0, one launch (start us, length us, event | category | flops | bytes accessed | tf_op | source)
XLA Modules:
  0.0 686.0 jit_solution(10864593307240332154)
XLA Ops:
  2.7 5.8 project_kv.1
  13.5 11.4 %collective-permute-done = bf16[512,512]{1,0:T(8,128)(2,1)S(1)} collective-permute-done((bf16[512,512]{1,0:T(8,128)(2,1)}, bf16[512,512]{1,0:T(8,128)(2,1)S(1)}, u32[]{:S(2)}, u32[]{:S(2)}) %collective-permute-start) | collective-permute-done | bytes 524320 | tf_op jit(solution)/shard_map/ppermute | solution.py:523
  31.3 8.2 %collective-permute-done.1.refs_0_ = bf16[512,512]{1,0:T(8,128)(2,1)} collective-permute-done((bf16[512,512]{1,0:T(8,128)(2,1)S(1)}, bf16[512,512]{1,0:T(8,128)(2,1)}, u32[]{:S(2)}, u32[]{:S(2)}) %collective-permute-start.1) | collective-permute-done | bytes 524320 | tf_op jit(solution)/shard_map/ppermute | solution.py:523
  39.5 5.3 collective-permute-start.2
  51.5 6.5 project_q.1
  60.0 5.7 attn_fwd.4.refs_2_
  65.7 5.4 collective-permute-done.6.refs_1_
  71.9 6.3 attn_fwd.5.refs_2_
  91.1 14.3 %attn_fwd.7 = (bf16[512,512]{1,0:T(8,128)(2,1)}, f32[512,512]{1,0:T(8,128)}) custom-call(s32[4]{0:T(128)} %get-tuple-element.130.scalar_ref, bf16[512,512]{1,0:T(8,128)(2,1)} %get-tuple-element.38.q_ref, bf16[512,512]{1,0:T(8,128)(2,1)} %collective-permute-done.2.refs_0_, bf16[512,512]{1,0:T(8,128)(2,1)} %copy-done.41, f32[512,1024]{1,0:T(8,128)} %attn_fwd.6.refs_2_), custom_call_target="tpu_custom_call" | custom-call | flops 2147483648 | bytes 3145728 | tf_op jit(solution)/shard_map/attn_fwd/pallas_call | solution.py:206
  122.5 8.7 %fusion.107 = f32[512,1536]{1,0:T(8,128)} fusion(bf16[512,2048]{1,0:T(8,128)(2,1)} %param.26, bf16[1536,2048]{1,0:T(8,128)(2,1)} %param.25), kind=kOutput, calls=%fused_computation.227 | convolution fusion | flops 3221225472 | bytes 11534336 | tf_op jit(solution)/shard_map/dot_general | solution.py:24
  131.2 10.4 %collective-permute-done.9 = bf16[256,2048]{1,0:T(8,128)(2,1)} collective-permute-done((bf16[256,2048]{1,0:T(8,128)(2,1)}, bf16[256,2048]{1,0:T(8,128)(2,1)}, u32[]{:S(2)}, u32[]{:S(2)}) %collective-permute-start.9) | collective-permute-done | bytes 1048608 | tf_op jit(solution)/shard_map/ppermute | solution.py:420
  168.1 11.0 %collective-permute-done.63 = bf16[256,1024]{0,1:T(8,128)(2,1)} collective-permute-done((bf16[256,1024]{0,1:T(8,128)(2,1)S(1)}, bf16[256,1024]{0,1:T(8,128)(2,1)}, u32[]{:S(2)}, u32[]{:S(2)}) %collective-permute-start.63) | collective-permute-done | bytes 524320 | tf_op jit(solution)/shard_map/ppermute | solution.py:423
  179.1 7.5 %fusion.64 = f32[512,1536]{1,0:T(8,128)S(1)} fusion(bf16[2048,1536]{1,0:T(8,128)(2,1)} %param.24, bf16[256,2048]{1,0:T(8,128)(2,1)} %collective-permute-done.10, bf16[256,2048]{1,0:T(8,128)(2,1)} %multiply_convert_fusion.3, pred[]{:T(512)S(6)} %eq.24), kind=kOutput, calls=%fused_computation.135 | convolution fusion | flops 3230662656 | bytes 11534337 | tf_op jit(solution)/shard_map/dot_general | solution.py:24
  186.7 9.0 %multiply_convert_fusion = (bf16[512,1536]{1,0:T(8,128)(2,1)}, bf16[512,1536]{1,0:T(8,128)(2,1)}, bf16[512,1536]{1,0:T(8,128)(2,1)}) fusion(f32[512,1536]{1,0:T(8,128)S(1)} %copy-done.49, f32[512,1536]{1,0:T(8,128)S(1)} %fusion.64, bf16[2048,1536]{1,0:T(8,128)(2,1)S(1)} %bitcast.87, bf16[256,2048]{1,0:T(8,128)(2,1)} %collective-permute-done.10, ...), kind=kOutput, calls=%fused_computation.4 | convolution fusion | flops 3242459136 | bytes 19398656 | tf_op jit(solution)/shard_map/dot_general | solution.py:24
  231.2 6.1 fusion.110
  258.5 12.2 %collective-permute-done.72 = bf16[512,1536]{1,0:T(8,128)(2,1)S(1)} collective-permute-done((bf16[512,1536]{1,0:T(8,128)(2,1)}, bf16[512,1536]{1,0:T(8,128)(2,1)S(1)}, u32[]{:S(2)}, u32[]{:S(2)}) %collective-permute-start.72) | collective-permute-done | bytes 1572896 | tf_op jit(solution)/shard_map/ppermute | solution.py:423
  283.0 5.4 collective-permute-done.12
  320.1 24.8 %collective-permute-done.51 = bf16[256,1024]{0,1:T(8,128)(2,1)} collective-permute-done((bf16[256,1024]{0,1:T(8,128)(2,1)S(1)}, bf16[256,1024]{0,1:T(8,128)(2,1)}, u32[]{:S(2)}, u32[]{:S(2)}) %collective-permute-start.51) | collective-permute-done | bytes 524320 | tf_op jit(solution)/shard_map/ppermute | solution.py:423
  354.7 13.6 %attn_bwd.5 = (f32[512,512]{1,0:T(8,128)}, bf16[512,512]{1,0:T(8,128)(2,1)}, bf16[512,512]{1,0:T(8,128)(2,1)}) custom-call(s32[4]{0:T(128)} %get-tuple-element.129.scalar_ref, bf16[4,512,256]{2,1,0:T(8,128)(2,1)} %get-tuple-element.42.qx_ref, bf16[4,512,256]{2,1,0:T(8,128)(2,1)} %get-tuple-element.43.dox_ref, ...), custom_call_target="tpu_custom_call" | custom-call | flops 5368709120 | bytes 4194304 | tf_op jit(solution)/shard_map/attn_bwd/pallas_call | solution.py:338
  368.3 10.1 %attn_bwd.6 = (f32[512,512]{1,0:T(8,128)}, bf16[512,512]{1,0:T(8,128)(2,1)}, bf16[512,512]{1,0:T(8,128)(2,1)}) custom-call(s32[4]{0:T(128)} %get-tuple-element.128.scalar_ref, bf16[4,512,256]{2,1,0:T(8,128)(2,1)} %get-tuple-element.42.qx_ref, bf16[4,512,256]{2,1,0:T(8,128)(2,1)} %get-tuple-element.43.dox_ref, bf16[512,512]{1,0:T(8,128)(2,1)} %copy-done.30, ...), custom_call_target="tpu_custom_call" | custom-call | flops 5368709120 | bytes 4194304 | tf_op jit(solution)/shard_map/attn_bwd/pallas_call | solution.py:338
  378.5 10.2 %attn_bwd.7 = (f32[512,512]{1,0:T(8,128)}, bf16[512,512]{1,0:T(8,128)(2,1)}, bf16[512,512]{1,0:T(8,128)(2,1)}) custom-call(s32[4]{0:T(128)} %get-tuple-element.75.scalar_ref, bf16[4,512,256]{2,1,0:T(8,128)(2,1)} %get-tuple-element.42.qx_ref, bf16[4,512,256]{2,1,0:T(8,128)(2,1)} %get-tuple-element.43.dox_ref, bf16[512,512]{1,0:T(8,128)(2,1)} %get-tuple-element.39.refs_0_, ...), custom_call_target="tpu_custom_call" | custom-call | flops 5368709120 | bytes 4194304 | tf_op jit(solution)/shard_map/attn_bwd/pallas_call | solution.py:338
  416.6 12.4 %collective-permute-done.74 = bf16[256,1536]{1,0:T(8,128)(2,1)S(1)} collective-permute-done((bf16[256,1536]{1,0:T(8,128)(2,1)S(1)}, bf16[256,1536]{1,0:T(8,128)(2,1)S(1)}, u32[]{:S(2)}, u32[]{:S(2)}) %collective-permute-start.74) | collective-permute-done | bytes 786464 | tf_op jit(solution)/shard_map/ppermute | solution.py:468
  431.5 9.6 %collective-permute-done.79 = bf16[512,1536]{1,0:T(8,128)(2,1)S(1)} collective-permute-done((bf16[512,1536]{1,0:T(8,128)(2,1)}, bf16[512,1536]{1,0:T(8,128)(2,1)S(1)}, u32[]{:S(2)}, u32[]{:S(2)}) %collective-permute-start.79) | collective-permute-done | bytes 1572896 | tf_op jit(solution)/shard_map/ppermute | solution.py:423
  471.4 9.1 %collective-permute-done.54 = bf16[512,256]{1,0:T(8,128)(2,1)S(1)} collective-permute-done((bf16[512,256]{1,0:T(8,128)(2,1)S(1)}, bf16[512,256]{1,0:T(8,128)(2,1)S(1)}, u32[]{:S(2)}, u32[]{:S(2)}) %collective-permute-start.54) | collective-permute-done | bytes 262176 | tf_op jit(solution)/shard_map/ppermute | solution.py:468
  513.3 21.5 %collective-permute-start.55 = (bf16[512,256]{1,0:T(8,128)(2,1)S(1)}, bf16[512,256]{1,0:T(8,128)(2,1)S(1)}, u32[]{:S(2)}, u32[]{:S(2)}) collective-permute-start(bf16[512,256]{1,0:T(8,128)(2,1)S(1)} %get-tuple-element.103), channel_id=1, source_target_pairs={{0,8},{4,12},{8,16},{12,20},{16,24},{20,28},{1,9},{5,13},{9,17},{1... | collective-permute-start | bytes 786440 | tf_op jit(solution)/shard_map/ppermute | solution.py:468
  535.0 19.2 %collective-permute-start.38 = (bf16[256,512]{1,0:T(8,128)(2,1)S(1)}, bf16[256,512]{1,0:T(8,128)(2,1)S(1)}, u32[]{:S(2)}, u32[]{:S(2)}) collective-permute-start(bf16[256,512]{1,0:T(8,128)(2,1)S(1)} %get-tuple-element.117), channel_id=1, source_target_pairs={{0,8},{4,12},{8,16},{12,20},{1,9},{5,13},{9,17},{13,21},{2,10},{6,... | collective-permute-start | bytes 786440 | tf_op jit(solution)/shard_map/ppermute | solution.py:468
  563.3 5.5 collective-permute-start.83
  572.6 5.3 collective-permute-start.39
  594.1 12.6 %collective-permute-done.43 = bf16[512,512]{1,0:T(8,128)(2,1)S(1)} collective-permute-done((bf16[512,512]{1,0:T(8,128)(2,1)S(1)}, bf16[512,512]{1,0:T(8,128)(2,1)S(1)}, u32[]{:S(2)}, u32[]{:S(2)}) %collective-permute-start.43) | collective-permute-done | bytes 524320 | tf_op jit(solution)/shard_map/ppermute | solution.py:423
  612.0 8.0 %collective-permute-start.44 = (bf16[256,512]{1,0:T(8,128)(2,1)S(1)}, bf16[256,512]{1,0:T(8,128)(2,1)S(1)}, u32[]{:S(2)}, u32[]{:S(2)}) collective-permute-start(bf16[256,512]{1,0:T(8,128)(2,1)S(1)} %get-tuple-element.113), channel_id=1, source_target_pairs={{0,8},{4,12},{1,9},{5,13},{2,10},{6,14},{3,11},{7,15}} | collective-permute-start | bytes 786440 | tf_op jit(solution)/shard_map/ppermute | solution.py:468
  634.7 15.9 %collective-permute-done.45 = bf16[256,512]{1,0:T(8,128)(2,1)S(1)} collective-permute-done((bf16[256,512]{1,0:T(8,128)(2,1)S(1)}, bf16[256,512]{1,0:T(8,128)(2,1)S(1)}, u32[]{:S(2)}, u32[]{:S(2)}) %collective-permute-start.45) | collective-permute-done | bytes 262176 | tf_op jit(solution)/shard_map/ppermute | solution.py:468
  652.0 5.4 collective-permute-start.46
  (392 shorter events, 360.4 us)
Async XLA Ops:
  49.4 33.1 %collective-permute-start.4 = (bf16[512,512]{1,0:T(8,128)(2,1)}, bf16[512,512]{1,0:T(8,128)(2,1)}, u32[]{:S(2)}, u32[]{:S(2)}) collective-permute-start(bf16[512,512]{1,0:T(8,128)(2,1)} %collective-permute-done.1.refs_0_), channel_id=1, source_target_pairs={{0,4},{4,0},{8,12},{12,8},{16,20},{20,16},{24,28},{28,24},{1,5},{5... | collective-permute-start | bytes 1572872 | tf_op jit(solution)/shard_map/ppermute | solution.py:423
  58.0 32.3 %collective-permute-start.3 = (bf16[512,512]{1,0:T(8,128)(2,1)}, bf16[512,512]{1,0:T(8,128)(2,1)S(1)}, u32[]{:S(2)}, u32[]{:S(2)}) collective-permute-start(bf16[512,512]{1,0:T(8,128)(2,1)} %collective-permute-done.2.refs_0_), channel_id=1, source_target_pairs={{0,4},{4,0},{8,12},{12,8},{16,20},{20,16},{24,28},{28,24},{1,5},{5... | collective-permute-start | bytes 1572872 | tf_op jit(solution)/shard_map/ppermute | solution.py:423
  146.7 32.5 %collective-permute-start.10 = (bf16[256,2048]{1,0:T(8,128)(2,1)}, bf16[256,2048]{1,0:T(8,128)(2,1)}, u32[]{:S(2)}, u32[]{:S(2)}) collective-permute-start(bf16[256,2048]{1,0:T(8,128)(2,1)} %multiply_convert_fusion.3), channel_id=1, source_target_pairs={{0,1},{1,0},{2,3},{3,2},{4,5},{5,4},{6,7},{7,6},{8,9},{9,8},{10,11... | collective-permute-start | bytes 3145736 | tf_op jit(solution)/shard_map/ppermute | solution.py:417
  179.1 68.6 %collective-permute-start.64 = (bf16[256,1024]{0,1:T(8,128)(2,1)}, bf16[256,1024]{0,1:T(8,128)(2,1)}, u32[]{:S(2)}, u32[]{:S(2)}) collective-permute-start(bf16[256,1024]{0,1:T(8,128)(2,1)} %collective-permute-done.63), channel_id=1, source_target_pairs={{0,1},{1,0},{2,3},{3,2},{4,5},{5,4},{6,7},{7,6},{8,9},{9,8},{10,11... | collective-permute-start | bytes 1572872 | tf_op jit(solution)/shard_map/ppermute | solution.py:417
  199.9 47.8 %collective-permute-start.65 = (bf16[512,1536]{1,0:T(8,128)(2,1)}, bf16[512,1536]{1,0:T(8,128)(2,1)}, u32[]{:S(2)}, u32[]{:S(2)}) collective-permute-start(bf16[512,1536]{1,0:T(8,128)(2,1)} %get-tuple-element.78), channel_id=1, source_target_pairs={{0,4},{4,0},{8,12},{12,8},{16,20},{20,16},{24,28},{28,24},{1,5},{5... | collective-permute-start | bytes 4718600 | tf_op jit(solution)/shard_map/ppermute | solution.py:423
  216.6 54.1 %collective-permute-start.72 = (bf16[512,1536]{1,0:T(8,128)(2,1)}, bf16[512,1536]{1,0:T(8,128)(2,1)S(1)}, u32[]{:S(2)}, u32[]{:S(2)}) collective-permute-start(bf16[512,1536]{1,0:T(8,128)(2,1)} %get-tuple-element.77), channel_id=1, source_target_pairs={{0,4},{4,0},{8,12},{12,8},{16,20},{20,16},{24,28},{28,24},{1,5},{5... | collective-permute-start | bytes 4718600 | tf_op jit(solution)/shard_map/ppermute | solution.py:423
  240.7 38.7 %collective-permute-start.15 = (bf16[256,2048]{1,0:T(8,128)(2,1)S(1)}, bf16[256,2048]{1,0:T(8,128)(2,1)S(1)}, u32[]{:S(2)}, u32[]{:S(2)}) collective-permute-start(bf16[256,2048]{1,0:T(8,128)(2,1)S(1)} %add_convert_fusion.8), channel_id=1, source_target_pairs={{0,2},{1,3},{2,0},{3,1},{4,6},{5,7},{6,4},{7,5},{8,10},{9,11},{10,... | collective-permute-start | bytes 3145736 | tf_op jit(solution)/shard_map/ppermute | solution.py:420
  247.2 41.2 %collective-permute-start.12 = (bf16[256,2048]{1,0:T(8,128)(2,1)S(1)}, bf16[256,2048]{1,0:T(8,128)(2,1)S(1)}, u32[]{:S(2)}, u32[]{:S(2)}) collective-permute-start(bf16[256,2048]{1,0:T(8,128)(2,1)S(1)} %add_convert_fusion.10), channel_id=1, source_target_pairs={{0,2},{1,3},{2,0},{3,1},{4,6},{5,7},{6,4},{7,5},{8,10},{9,11},{10,... | collective-permute-start | bytes 3145736 | tf_op jit(solution)/shard_map/ppermute | solution.py:420
  253.3 57.7 %collective-permute-start.66 = (bf16[256,1536]{1,0:T(8,128)(2,1)}, bf16[256,1536]{1,0:T(8,128)(2,1)}, u32[]{:S(2)}, u32[]{:S(2)}) collective-permute-start(bf16[256,1536]{1,0:T(8,128)(2,1)} %get-tuple-element.96), channel_id=1, source_target_pairs={{0,8},{4,12},{1,9},{5,13},{2,10},{6,14},{3,11},{7,15}} | collective-permute-start | bytes 2359304 | tf_op jit(solution)/shard_map/ppermute | solution.py:468
  257.0 55.7 %collective-permute-start.69 = (bf16[256,1536]{1,0:T(8,128)(2,1)}, bf16[256,1536]{1,0:T(8,128)(2,1)}, u32[]{:S(2)}, u32[]{:S(2)}) collective-permute-start(bf16[256,1536]{1,0:T(8,128)(2,1)} %get-tuple-element.97), channel_id=1, source_target_pairs={{24,16},{28,20},{25,17},{29,21},{26,18},{30,22},{27,19},{31,23}} | collective-permute-start | bytes 2359304 | tf_op jit(solution)/shard_map/ppermute | solution.py:469
  275.4 40.6 %collective-permute-start.73 = (bf16[256,1536]{1,0:T(8,128)(2,1)}, bf16[256,1536]{1,0:T(8,128)(2,1)}, u32[]{:S(2)}, u32[]{:S(2)}) collective-permute-start(bf16[256,1536]{1,0:T(8,128)(2,1)} %get-tuple-element.90), channel_id=1, source_target_pairs={{0,8},{4,12},{1,9},{5,13},{2,10},{6,14},{3,11},{7,15}} | collective-permute-start | bytes 2359304 | tf_op jit(solution)/shard_map/ppermute | solution.py:468
  281.4 35.2 %collective-permute-start.76 = (bf16[256,1536]{1,0:T(8,128)(2,1)}, bf16[256,1536]{1,0:T(8,128)(2,1)}, u32[]{:S(2)}, u32[]{:S(2)}) collective-permute-start(bf16[256,1536]{1,0:T(8,128)(2,1)} %get-tuple-element.91), channel_id=1, source_target_pairs={{24,16},{28,20},{25,17},{29,21},{26,18},{30,22},{27,19},{31,23}} | collective-permute-start | bytes 2359304 | tf_op jit(solution)/shard_map/ppermute | solution.py:469
  309.9 98.2 %collective-permute-start.34 = (bf16[256,1024]{0,1:T(8,128)(2,1)}, bf16[256,1024]{0,1:T(8,128)(2,1)}, u32[]{:S(2)}, u32[]{:S(2)}) collective-permute-start(bf16[256,1024]{0,1:T(8,128)(2,1)} %bitcast.72), channel_id=1, source_target_pairs={{0,4},{4,0},{8,12},{12,8},{16,20},{20,16},{24,28},{28,24},{1,5},{5... | collective-permute-start | bytes 1572872 | tf_op jit(solution)/shard_map/ppermute | solution.py:423
  311.1 87.2 %collective-permute-start.50 = (bf16[512,512]{1,0:T(8,128)(2,1)}, bf16[512,512]{1,0:T(8,128)(2,1)}, u32[]{:S(2)}, u32[]{:S(2)}) collective-permute-start(bf16[512,512]{1,0:T(8,128)(2,1)} %get-tuple-element.40.o_ref), channel_id=1, source_target_pairs={{0,4},{4,0},{8,12},{12,8},{16,20},{20,16},{24,28},{28,24},{1,5},{5... | collective-permute-start | bytes 1572872 | tf_op jit(solution)/shard_map/ppermute | solution.py:423
  312.6 32.7 %collective-permute-start.16 = (bf16[256,2048]{1,0:T(8,128)(2,1)}, bf16[256,2048]{1,0:T(8,128)(2,1)S(1)}, u32[]{:S(2)}, u32[]{:S(2)}) collective-permute-start(bf16[256,2048]{1,0:T(8,128)(2,1)} %get-tuple-element.70), channel_id=1, source_target_pairs={{0,1},{1,0},{2,3},{3,2},{4,5},{5,4},{6,7},{7,6},{8,9},{9,8},{10,11... | collective-permute-start | bytes 3145736 | tf_op jit(solution)/shard_map/ppermute | solution.py:417
  316.0 72.6 %collective-permute-start.13 = (bf16[256,2048]{1,0:T(8,128)(2,1)S(1)}, bf16[256,2048]{1,0:T(8,128)(2,1)S(1)}, u32[]{:S(2)}, u32[]{:S(2)}) collective-permute-start(bf16[256,2048]{1,0:T(8,128)(2,1)S(1)} %copy-done.21), channel_id=1, source_target_pairs={{0,1},{1,0},{2,3},{3,2},{4,5},{5,4},{6,7},{7,6},{8,9},{9,8},{10,11... | collective-permute-start | bytes 3145736 | tf_op jit(solution)/shard_map/ppermute | solution.py:417
  344.9 67.3 %collective-permute-start.80 = (bf16[256,1024]{0,1:T(8,128)(2,1)}, bf16[256,1024]{0,1:T(8,128)(2,1)}, u32[]{:S(2)}, u32[]{:S(2)}) collective-permute-start(bf16[256,1024]{0,1:T(8,128)(2,1)} %bitcast.25), channel_id=1, source_target_pairs={{0,4},{4,0},{8,12},{12,8},{16,20},{20,16},{24,28},{28,24},{1,5},{5... | collective-permute-start | bytes 1572872 | tf_op jit(solution)/shard_map/ppermute | solution.py:423
  345.4 57.7 %collective-permute-start.52 = (bf16[256,1024]{0,1:T(8,128)(2,1)}, bf16[256,1024]{0,1:T(8,128)(2,1)}, u32[]{:S(2)}, u32[]{:S(2)}) collective-permute-start(bf16[256,1024]{0,1:T(8,128)(2,1)} %collective-permute-done.51), channel_id=1, source_target_pairs={{0,1},{1,0},{2,3},{3,2},{4,5},{5,4},{6,7},{7,6},{8,9},{9,8},{10,11... | collective-permute-start | bytes 1572872 | tf_op jit(solution)/shard_map/ppermute | solution.py:417
  403.1 37.9 %collective-permute-start.79 = (bf16[512,1536]{1,0:T(8,128)(2,1)}, bf16[512,1536]{1,0:T(8,128)(2,1)S(1)}, u32[]{:S(2)}, u32[]{:S(2)}) collective-permute-start(bf16[512,1536]{1,0:T(8,128)(2,1)} %get-tuple-element.79), channel_id=1, source_target_pairs={{0,4},{4,0},{8,12},{12,8},{16,20},{20,16},{24,28},{28,24},{1,5},{5... | collective-permute-start | bytes 4718600 | tf_op jit(solution)/shard_map/ppermute | solution.py:423
  413.8 43.2 %collective-permute-start.35 = (bf16[256,1024]{0,1:T(8,128)(2,1)}, bf16[256,1024]{0,1:T(8,128)(2,1)S(1)}, u32[]{:S(2)}, u32[]{:S(2)}) collective-permute-start(bf16[256,1024]{0,1:T(8,128)(2,1)} %collective-permute-done.34), channel_id=1, source_target_pairs={{0,1},{1,0},{2,3},{3,2},{4,5},{5,4},{6,7},{7,6},{8,9},{9,8},{10,11... | collective-permute-start | bytes 1572872 | tf_op jit(solution)/shard_map/ppermute | solution.py:417
  429.0 37.5 %collective-permute-start.20 = (bf16[512,512]{1,0:T(8,128)(2,1)S(1)}, bf16[512,512]{1,0:T(8,128)(2,1)S(1)}, u32[]{:S(2)}, u32[]{:S(2)}) collective-permute-start(bf16[512,512]{1,0:T(8,128)(2,1)S(1)} %copy-done.47), channel_id=1, source_target_pairs={{0,4},{4,0},{8,12},{12,8},{16,20},{20,16},{24,28},{28,24},{1,5},{5... | collective-permute-start | bytes 1572872 | tf_op jit(solution)/shard_map/ppermute | solution.py:423
  429.4 33.6 %collective-permute-start.36 = (bf16[512,512]{1,0:T(8,128)(2,1)S(1)}, bf16[512,512]{1,0:T(8,128)(2,1)S(1)}, u32[]{:S(2)}, u32[]{:S(2)}) collective-permute-start(bf16[512,512]{1,0:T(8,128)(2,1)S(1)} %copy-done.23), channel_id=1, source_target_pairs={{0,4},{4,0},{8,12},{12,8},{16,20},{20,16},{24,28},{28,24},{1,5},{5... | collective-permute-start | bytes 1572872 | tf_op jit(solution)/shard_map/ppermute | solution.py:423
  451.0 35.7 %collective-permute-start.71 = (bf16[256,1536]{1,0:T(8,128)(2,1)S(1)}, bf16[256,1536]{1,0:T(8,128)(2,1)S(1)}, u32[]{:S(2)}, u32[]{:S(2)}) collective-permute-start(bf16[256,1536]{1,0:T(8,128)(2,1)S(1)} %get-tuple-element.93), channel_id=1, source_target_pairs={{24,16},{28,20},{16,8},{20,12},{8,0},{12,4},{25,17},{29,21},{17,9}... | collective-permute-start | bytes 2359304 | tf_op jit(solution)/shard_map/ppermute | solution.py:469
  452.3 39.6 %collective-permute-start.68 = (bf16[256,1536]{1,0:T(8,128)(2,1)S(1)}, bf16[256,1536]{1,0:T(8,128)(2,1)S(1)}, u32[]{:S(2)}, u32[]{:S(2)}) collective-permute-start(bf16[256,1536]{1,0:T(8,128)(2,1)S(1)} %get-tuple-element.92), channel_id=1, source_target_pairs={{0,8},{4,12},{8,16},{12,20},{16,24},{20,28},{1,9},{5,13},{9,17},{1... | collective-permute-start | bytes 2359304 | tf_op jit(solution)/shard_map/ppermute | solution.py:468
  496.2 73.5 %collective-permute-start.17 = (bf16[512,512]{1,0:T(8,128)(2,1)S(1)}, bf16[512,512]{1,0:T(8,128)(2,1)S(1)}, u32[]{:S(2)}, u32[]{:S(2)}) collective-permute-start(bf16[512,512]{1,0:T(8,128)(2,1)S(1)} %copy-done.42), channel_id=1, source_target_pairs={{0,4},{4,0},{8,12},{12,8},{16,20},{20,16},{24,28},{28,24},{1,5},{5... | collective-permute-start | bytes 1572872 | tf_op jit(solution)/shard_map/ppermute | solution.py:423
  498.2 56.7 %collective-permute-start.82 = (bf16[1536,256]{1,0:T(8,128)(2,1)S(1)}, bf16[1536,256]{1,0:T(8,128)(2,1)S(1)}, u32[]{:S(2)}, u32[]{:S(2)}) collective-permute-start(bf16[1536,256]{1,0:T(8,128)(2,1)S(1)} %get-tuple-element.84), channel_id=1, source_target_pairs={{0,8},{4,12},{1,9},{5,13},{2,10},{6,14},{3,11},{7,15}} | collective-permute-start | bytes 2359304 | tf_op jit(solution)/shard_map/ppermute | solution.py:468
  504.3 55.1 %collective-permute-start.85 = (bf16[1536,256]{1,0:T(8,128)(2,1)S(1)}, bf16[1536,256]{1,0:T(8,128)(2,1)S(1)}, u32[]{:S(2)}, u32[]{:S(2)}) collective-permute-start(bf16[1536,256]{1,0:T(8,128)(2,1)S(1)} %get-tuple-element.85), channel_id=1, source_target_pairs={{24,16},{28,20},{25,17},{29,21},{26,18},{30,22},{27,19},{31,23}} | collective-permute-start | bytes 2359304 | tf_op jit(solution)/shard_map/ppermute | solution.py:469
  513.3 40.9 %collective-permute-start.55 = (bf16[512,256]{1,0:T(8,128)(2,1)S(1)}, bf16[512,256]{1,0:T(8,128)(2,1)S(1)}, u32[]{:S(2)}, u32[]{:S(2)}) collective-permute-start(bf16[512,256]{1,0:T(8,128)(2,1)S(1)} %get-tuple-element.103), channel_id=1, source_target_pairs={{0,8},{4,12},{8,16},{12,20},{16,24},{20,28},{1,9},{5,13},{9,17},{1... | collective-permute-start | bytes 786440 | tf_op jit(solution)/shard_map/ppermute | solution.py:468
  563.3 112.9 %collective-permute-start.27 = (f32[256,2048]{1,0:T(8,128)}, f32[256,2048]{1,0:T(8,128)}, u32[]{:S(2)}, u32[]{:S(2)}) collective-permute-start(f32[256,2048]{1,0:T(8,128)} %get-tuple-element.71), channel_id=1, source_target_pairs={{0,1},{1,0},{2,3},{3,2},{4,5},{5,4},{6,7},{7,6},{8,9},{9,8},{10,11... | collective-permute-start | bytes 6291464 | tf_op jit(solution)/shard_map/ppermute | solution.py:417
  563.3 56.6 %collective-permute-start.83 = (bf16[1536,256]{1,0:T(8,128)(2,1)}, bf16[1536,256]{1,0:T(8,128)(2,1)}, u32[]{:S(2)}, u32[]{:S(2)}) collective-permute-start(bf16[1536,256]{1,0:T(8,128)(2,1)} %get-tuple-element.82), channel_id=1, source_target_pairs={{0,8},{4,12},{8,16},{12,20},{1,9},{5,13},{9,17},{13,21},{2,10},{6,... | collective-permute-start | bytes 2359304 | tf_op jit(solution)/shard_map/ppermute | solution.py:468
  569.7 50.9 %collective-permute-start.86 = (bf16[1536,256]{1,0:T(8,128)(2,1)}, bf16[1536,256]{1,0:T(8,128)(2,1)}, u32[]{:S(2)}, u32[]{:S(2)}) collective-permute-start(bf16[1536,256]{1,0:T(8,128)(2,1)} %get-tuple-element.83), channel_id=1, source_target_pairs={{24,16},{28,20},{16,8},{20,12},{25,17},{29,21},{17,9},{21,13},{26,... | collective-permute-start | bytes 2359304 | tf_op jit(solution)/shard_map/ppermute | solution.py:469
  625.1 32.4 %collective-permute-start.84 = (bf16[1536,256]{1,0:T(8,128)(2,1)S(1)}, bf16[1536,256]{1,0:T(8,128)(2,1)S(1)}, u32[]{:S(2)}, u32[]{:S(2)}) collective-permute-start(bf16[1536,256]{1,0:T(8,128)(2,1)S(1)} %get-tuple-element.80), channel_id=1, source_target_pairs={{0,8},{4,12},{8,16},{12,20},{16,24},{20,28},{1,9},{5,13},{9,17},{1... | collective-permute-start | bytes 2359304 | tf_op jit(solution)/shard_map/ppermute | solution.py:468
  (114 other events, 1566.8 us)

commit v2 on v1

--- a/solution.py
+++ b/solution.py
@@ -138,95 +138,228 @@
     return (key_pos <= row_pos) | (key_pos < prefix)
 
 
-def attn_fwd_kernel(scalar_ref, q_ref, *refs, slots, kv_heads, repeat, width, tile, coef, first, last):
-    kv_refs = refs[:slots]
-    rest = refs[slots:]
-    if not first:
-        acc_in, rest = rest[0], rest[1:]
-    if last:
-        o_ref, lse_ref, acc = rest
-    else:
-        (acc,) = rest
+def attn_fwd_kernel(
+    prefix_ref,
+    q_ref,
+    kv_ref,
+    o_ref,
+    lse_ref,
+    all_ref,
+    acc,
+    send_x,
+    recv_x,
+    send_z,
+    recv_z,
+    send_down,
+    *,
+    group,
+    kv_heads,
+    repeat,
+    width,
+    tile,
+    coef,
+):
     rows = q_ref.shape[0]
     kv_width = kv_heads * width
-    if first:
-        acc[...] = jnp.zeros_like(acc)
-    else:
-        acc[...] = acc_in[...]
+    planes = group // 2
+    device = lax.axis_index("dp")
+    member = device % group
+    plane = member // 2
+    x_at = member % 2
+    x_other = device + 1 - 2 * x_at
+    inner = plane < planes - 1
+    prefix = prefix_ref[0]
+
+    barrier = pltpu.get_barrier_semaphore()
+    pl.semaphore_signal(barrier, 1, device_id={"dp": x_other}, device_id_type=pl.DeviceIdType.MESH)
+
+    @pl.when(inner)
+    def _():
+        pl.semaphore_signal(
+            barrier, 1, device_id={"dp": device + 2}, device_id_type=pl.DeviceIdType.MESH
+        )
+
+    @pl.when(plane > 0)
+    def _():
+        pl.semaphore_signal(
+            barrier, 1, device_id={"dp": device - 2}, device_id_type=pl.DeviceIdType.MESH
+        )
+
+    pl.semaphore_wait(barrier, 1 + inner.astype(jnp.int32) + (plane > 0).astype(jnp.int32))
+
+    def source(slot):
+        return kv_ref if slot == 0 else all_ref.at[2 * slot]
+
+    def to_x(slot):
+        return pltpu.make_async_remote_copy(
+            src_ref=source(slot),
+            dst_ref=all_ref.at[2 * slot + 1],
+            send_sem=send_x.at[slot],
+            recv_sem=recv_x.at[slot],
+            device_id={"dp": x_other},
+            device_id_type=pl.DeviceIdType.MESH,
+        )
+
+    def to_z(slot):
+        return pltpu.make_async_remote_copy(
+            src_ref=source(slot - 1),
+            dst_ref=all_ref.at[2 * slot],
+            send_sem=send_z.at[slot],
+            recv_sem=recv_z.at[slot],
+            device_id={"dp": device + 2},
+            device_id_type=pl.DeviceIdType.MESH,
+        )
+
+    def to_first():
+        return pltpu.make_async_remote_copy(
+            src_ref=kv_ref,
+            dst_ref=all_ref.at[2],
+            send_sem=send_down,
+            recv_sem=recv_z.at[1],
+            device_id={"dp": device - 2},
+            device_id_type=pl.DeviceIdType.MESH,
+        )
+
     ones = jnp.ones((rows, width), BF16)
-    row0 = scalar_ref[0] * rows
-    prefix = scalar_ref[1]
-    for slot in range(slots):
-        key0, needed, full = block_flags(scalar_ref, slot, rows)
-
-        def work(masked, slot=slot, key0=key0):
-            for h in range(kv_heads):
-                k = kv_refs[slot][:, h * width : (h + 1) * width]
-                v = kv_refs[slot][:, kv_width + h * width : kv_width + (h + 1) * width]
-                v = jnp.concatenate([v, ones], axis=1)
-                for g in range(repeat):
-                    head = h * repeat + g
-                    for at in range(0, rows, tile):
-                        q = q_ref[at : at + tile, head * width : (head + 1) * width]
-                        p = jnp.exp2(dot(q, k, NT) * coef)
-                        if masked:
-                            p = jnp.where(visible(p.shape, key0, row0 + at, prefix), p, 0.0)
-                        acc[at : at + tile, 2 * head * width : 2 * (head + 1) * width] += dot(
-                            p.astype(BF16), v
-                        )
-
-        pl.when(needed & full)(functools.partial(work, False))
-        pl.when(needed & jnp.logical_not(full))(functools.partial(work, True))
-    if last:
-        for head in range(kv_heads * repeat):
-            total = acc[:, (2 * head + 1) * width : (2 * head + 2) * width]
-            o_ref[:, head * width : (head + 1) * width] = (
-                acc[:, 2 * head * width : (2 * head + 1) * width] / total
-            ).astype(BF16)
-            lse_ref[:, head * width : (head + 1) * width] = jnp.log2(total) * (1.0 / coef)
-
-
-def attn_fwd(scalars, q, blocks, acc, last, dims):
+    row0 = member * rows
+
+    def work(block, other, masked, start=False):
+        key0 = other * rows
+
+        def head_pair(h, carry):
+            k = block[:, pl.ds(pl.multiple_of(h * width, width), width)]
+            v = block[:, pl.ds(pl.multiple_of(kv_width + h * width, width), width)]
+            v = jnp.concatenate([v, ones], axis=1)
+            for g in range(repeat):
+                head = h * repeat + g
+                for at in range(0, rows, tile):
+                    q = q_ref[at : at + tile, pl.ds(pl.multiple_of(head * width, width), width)]
+                    p = jnp.exp2(dot(q, k, NT) * coef)
+                    if masked:
+                        p = jnp.where(visible(p.shape, key0, row0 + at, prefix), p, 0.0)
+                    term = dot(p.astype(BF16), v)
+                    if start:
+                        acc[head, at : at + tile, :] = term
+                    else:
+                        acc[head, at : at + tile, :] += term
+            return carry
+
+        lax.fori_loop(0, kv_heads, head_pair, 0)
+
+    to_x(0).start()
+    if planes > 1:
+
+        @pl.when(inner)
+        def _():
+            to_z(1).start()
+
+        @pl.when(plane == 1)
+        def _():
+            to_first().start()
+
+    work(kv_ref, member, True, True)
+    to_x(0).wait_recv()
+    work(all_ref.at[1], member + 1 - 2 * x_at, True)
+    for slot in range(1, planes):
+
+        def step(slot=slot):
+            to_z(slot).wait_recv()
+            if slot < planes - 1:
+
+                @pl.when(inner & (plane >= slot))
+                def _():
+                    to_z(slot + 1).start()
+
+            to_x(slot).start()
+            there = 2 * (plane - slot)
+            if slot == 1:
+
+                @pl.when(plane == 0)
+                def _():
+                    work(all_ref.at[2 * slot], 2 + x_at, True)
+
+                @pl.when(plane > 0)
+                def _():
+                    work(all_ref.at[2 * slot], there + x_at, False)
+            else:
+                work(all_ref.at[2 * slot], there + x_at, False)
+            to_x(slot).wait_recv()
+            if slot == 1:
+
+                @pl.when(plane == 0)
+                def _():
+                    work(all_ref.at[2 * slot + 1], 3 - x_at, True)
+
+                @pl.when(plane > 0)
+                def _():
+                    work(all_ref.at[2 * slot + 1], there + 1 - x_at, False)
+            else:
+                work(all_ref.at[2 * slot + 1], there + 1 - x_at, False)
+
+        if slot == 1:
+            step()
+        else:
+            pl.when(plane >= slot)(step)
+
+    for head in range(kv_heads * repeat):
+        total = acc[head, :, width:]
+        o_ref[:, head * width : (head + 1) * width] = (acc[head, :, :width] / total).astype(BF16)
+        lse_ref[:, head * width : (head + 1) * width] = jnp.log2(total) * (1.0 / coef)
+
+    to_x(0).wait_send()
+    for slot in range(1, planes):
+
+        @pl.when(inner & (plane >= slot - 1))
+        def _(slot=slot):
+            to_z(slot).wait_send()
+
+        @pl.when((plane >= slot) | (slot == 1))
+        def _(slot=slot):
+            to_x(slot).wait_send()
+
+    if planes > 1:
+
+        @pl.when(plane == 1)
+        def _():
+            to_first().wait_send()
+
+
+def attn_fwd(prefix, q, kv, group, dims):
     kv_heads, repeat, width = dims
     rows = q.shape[0]
-    columns = kv_heads * repeat * width
-    first = acc is None
-    acc_shape = jax.ShapeDtypeStruct((rows, 2 * columns), F32)
-    if last:
-        out_shape = [
-            jax.ShapeDtypeStruct((rows, columns), BF16),
-            jax.ShapeDtypeStruct((rows, columns), F32),
-        ]
-        scratch = [pltpu.VMEM(acc_shape.shape, F32)]
-    else:
-        out_shape = [acc_shape]
-        scratch = []
-    slots = len(blocks)
-    args = [scalars, q, *blocks] + ([] if first else [acc])
+    heads = kv_heads * repeat
+    columns = heads * width
+    planes = group // 2
     return pl.pallas_call(
         functools.partial(
             attn_fwd_kernel,
-            slots=slots,
+            group=group,
             kv_heads=kv_heads,
             repeat=repeat,
             width=width,
             tile=min(rows, 256),
             coef=math.log2(math.e) / math.sqrt(width),
-            first=first,
-            last=last,
-        ),
-        out_shape=out_shape,
-        in_specs=[pl.BlockSpec(memory_space=pltpu.SMEM)] + vmem(len(args) - 1),
-        out_specs=vmem(len(out_shape)),
-        scratch_shapes=scratch,
-        compiler_params=params(),
+        ),
+        out_shape=[
+            jax.ShapeDtypeStruct((rows, columns), BF16),
+            jax.ShapeDtypeStruct((rows, columns), F32),
+            jax.ShapeDtypeStruct((group,) + kv.shape, BF16),
+        ],
+        in_specs=[pl.BlockSpec(memory_space=pltpu.SMEM)] + vmem(2),
+        out_specs=vmem(3),
+        scratch_shapes=[pltpu.VMEM((heads, rows, 2 * width), F32)]
+        + [pltpu.SemaphoreType.DMA((planes,))] * 4
+        + [pltpu.SemaphoreType.DMA],
+        compiler_params=pltpu.CompilerParams(
+            vmem_limit_bytes=VMEM_LIMIT, collective_id=0, has_side_effects=True
+        ),
         cost_estimate=pl.CostEstimate(
-            flops=slots * 8 * rows * rows * columns,
-            bytes_accessed=12 * rows * columns,
-            transcendentals=slots * rows * rows * kv_heads * repeat,
+            flops=group * 8 * rows * rows * columns,
+            bytes_accessed=40 * rows * columns,
+            transcendentals=group * rows * rows * heads,
         ),
         name="attn_fwd",
-    )(*args)
+    )(prefix, q, kv)
 
 
 def split_three(value):
@@ -236,38 +369,44 @@
     return high.astype(F32), mid.astype(F32), (left - mid.astype(F32)).astype(BF16).astype(F32)
 
 
-def attn_prep_kernel(q_ref, do_ref, o_ref, lse_ref, qx_ref, dox_ref, *, heads, width):
-    rows = q_ref.shape[0]
-    lane = lax.broadcasted_iota(jnp.int32, (rows, width), 1)
+def attn_prep_kernel(core_ref, own_ref, far_ref, w_ref, q_ref, o_ref, lse_ref, qx_ref, dox_ref, *, heads, width):
+    half = own_ref.shape[0]
+    core = core_ref[0]
+    lane = lax.broadcasted_iota(jnp.int32, (half, width), 1)
 
     def extra(value):
         a, b, c = split_three(value)
         return jnp.where(lane == 0, a, jnp.where(lane == 1, b, jnp.where(lane == 2, c, 0.0))).astype(BF16)
 
-    for head in range(heads):
-        at = slice(head * width, (head + 1) * width)
-        qx_ref[head, :, :width] = q_ref[:, at]
-        qx_ref[head, :, width:] = extra(lse_ref[:, at])
-        d = do_ref[:, at]
-        delta = jnp.sum(d.astype(F32) * o_ref[:, at].astype(F32), axis=1, keepdims=True)
-        dox_ref[head, :, :width] = d
-        dox_ref[head, :, width:] = extra(jnp.broadcast_to(delta, (rows, width)))
-
-
-def attn_prep(q, d_out, out, lse, width):
+    for ref, at_core in ((own_ref, core), (far_ref, 1 - core)):
+        at_rows = pl.ds(pl.multiple_of(at_core * half, half), half)
+        d_heads = dot(ref[...], w_ref[...], NT)
+        for head in range(heads):
+            at = slice(head * width, (head + 1) * width)
+            qx_ref[head, at_rows, :width] = q_ref[at_rows, at]
+            qx_ref[head, at_rows, width:] = extra(lse_ref[at_rows, at])
+            d = d_heads[:, at].astype(BF16)
+            delta = jnp.sum(d.astype(F32) * o_ref[at_rows, at].astype(F32), axis=1, keepdims=True)
+            dox_ref[head, at_rows, :width] = d
+            dox_ref[head, at_rows, width:] = extra(jnp.broadcast_to(delta, (half, width)))
+
+
+def attn_prep(core, d_own, d_far, w_out, q, out, lse, width):
     rows, columns = q.shape
     heads = columns // width
     return pl.pallas_call(
         functools.partial(attn_prep_kernel, heads=heads, width=width),
         out_shape=[jax.ShapeDtypeStruct((heads, rows, 2 * width), BF16)] * 2,
-        in_specs=vmem(4),
+        in_specs=[pl.BlockSpec(memory_space=pltpu.SMEM)] + vmem(6),
         out_specs=vmem(2),
         compiler_params=params(),
         cost_estimate=pl.CostEstimate(
-            flops=20 * rows * columns, bytes_accessed=14 * rows * columns, transcendentals=0
+            flops=2 * rows * columns * w_out.shape[1],
+            bytes_accessed=14 * rows * columns,
+            transcendentals=0,
         ),
         name="attn_prep",
-    )(q, d_out, out, lse)
+    )(core, d_own, d_far, w_out, q, out, lse)
 
 
 def attn_bwd_kernel(scalar_ref, qx_ref, dox_ref, *refs, slots, kv_heads, repeat, width, coef, scale, first, last):
@@ -325,16 +464,16 @@
         dq_ref[...] = dq_ref[...] * scale
 
 
-def attn_bwd(scalars, qx, dox, blocks, dq, last, dims):
+def attn_bwd(scalars, qx, dox, stack, at, dq, last, dims):
     kv_heads, repeat, width = dims
     rows = qx.shape[1]
     columns = kv_heads * repeat * width
     first = dq is None
-    slots = len(blocks)
-    args = [scalars, qx, dox, *blocks] + ([] if first else [dq])
-    out_shape = [jax.ShapeDtypeStruct((rows, columns), F32)] + [
-        jax.ShapeDtypeStruct(b.shape, BF16) for b in blocks
-    ]
+    slots = len(at)
+    args = [scalars, qx, dox] + [stack] * slots + ([] if first else [dq])
+    block = stack.shape[1:]
+    out_shape = [jax.ShapeDtypeStruct((rows, columns), F32)] + [jax.ShapeDtypeStruct(block, BF16)] * slots
+    picks = [pl.BlockSpec((None,) + block, lambda i, j=j: (j, 0, 0)) for j in at]
     return pl.pallas_call(
         functools.partial(
             attn_bwd_kernel,
@@ -348,7 +487,8 @@
             last=last,
         ),
         out_shape=out_shape,
-        in_specs=[pl.BlockSpec(memory_space=pltpu.SMEM)] + vmem(len(args) - 1),
+        grid=(1,),
+        in_specs=[pl.BlockSpec(memory_space=pltpu.SMEM)] + vmem(2) + picks + vmem(0 if first else 1),
         out_specs=vmem(len(out_shape)),
         compiler_params=params(),
         cost_estimate=pl.CostEstimate(
@@ -358,6 +498,181 @@
         ),
         name="attn_bwd",
     )(*args)
+
+
+def smem():
+    return pl.BlockSpec(memory_space=pltpu.SMEM)
+
+
+def cut_kernel(at_ref, *refs, halves, planes, shard):
+    x_at, core = at_ref[0], at_ref[1]
+    keep_ref, send_ref = refs[-2:]
+    half = send_ref.shape[0]
+    for z in range(planes):
+        to = slice(z * shard, (z + 1) * shard)
+        keep = pl.ds(pl.multiple_of((2 * z + x_at) * shard, shard), shard)
+        send = pl.ds(pl.multiple_of((2 * z + 1 - x_at) * shard, shard), shard)
+        if halves:
+            own_ref, far_ref = refs[:2]
+            keep_ref[pl.ds(pl.multiple_of(core * half, half), half), to] = own_ref[:, keep]
+            keep_ref[pl.ds(pl.multiple_of((1 - core) * half, half), half), to] = far_ref[:, keep]
+            send_ref[:, to] = own_ref[:, send]
+        else:
+            keep_ref[:, to] = refs[0][:, keep]
+            send_ref[:, to] = refs[0][pl.ds(pl.multiple_of(core * half, half), half), send]
+
+
+def cut(x_at, core, parts, planes, shard, join):
+    halves = len(parts) == 2
+    half = parts[0].shape[0] // (1 if halves else 2)
+    if shard % 128:
+        whole = join(*parts) if halves else parts[0]
+        own = parts[0] if halves else lax.dynamic_slice_in_dim(whole, core * half, half, 0)
+
+        def columns(value, side):
+            view = value.reshape(value.shape[0], planes, 2, shard)
+            return lax.dynamic_index_in_dim(view, side, 2, keepdims=False).reshape(
+                value.shape[0], planes * shard
+            )
+
+        return columns(whole, x_at), columns(own, 1 - x_at)
+    return pl.pallas_call(
+        functools.partial(cut_kernel, halves=halves, planes=planes, shard=shard),
+        out_shape=[
+            jax.ShapeDtypeStruct((2 * half, planes * shard), BF16),
+            jax.ShapeDtypeStruct((half, planes * shard), BF16),
+        ],
+        in_specs=[smem()] + vmem(len(parts)),
+        out_specs=vmem(2),
+        compiler_params=params(),
+        cost_estimate=pl.CostEstimate(
+            flops=0, bytes_accessed=10 * half * planes * shard, transcendentals=0
+        ),
+        name="cut",
+    )(jnp.stack([x_at, core]).astype(jnp.int32), *parts)
+
+
+def norm_kernel(core_ref, both_ref, y_ref, x_ref, gain_ref, middle_ref, h_ref):
+    half = both_ref.shape[0]
+    x = x_ref[pl.ds(pl.multiple_of(core_ref[0] * half, half), half), :].astype(F32)
+    middle = x + both_ref[...].astype(F32) + y_ref[...].astype(F32)
+    middle_ref[...] = middle
+    r = lax.rsqrt(jnp.mean(middle * middle, axis=1, keepdims=True) + EPS)
+    h_ref[...] = (middle * r * gain_ref[...]).astype(BF16)
+
+
+def norm_forward(core, both, came, x, gain):
+    return pl.pallas_call(
+        norm_kernel,
+        out_shape=[jax.ShapeDtypeStruct(both.shape, F32), jax.ShapeDtypeStruct(both.shape, BF16)],
+        in_specs=[smem()] + vmem(4),
+        out_specs=vmem(2),
+        compiler_params=params(),
+        cost_estimate=pl.CostEstimate(
+            flops=10 * both.size, bytes_accessed=14 * both.size, transcendentals=0
+        ),
+        name="norm_forward",
+    )(core, both, came, x, gain)
+
+
+def norm_back_kernel(core_ref, both_ref, y_ref, middle_ref, add_ref, gain_ref, d_ref, d_low_ref, gain_out_ref):
+    half = both_ref.shape[0]
+    c = both_ref[...].astype(F32) + y_ref[...].astype(F32)
+    v = middle_ref[...]
+    r = lax.rsqrt(jnp.mean(v * v, axis=1, keepdims=True) + EPS)
+    n = v * r
+    gain_out_ref[...] = jnp.sum(c * n, axis=0, keepdims=True)
+    gc = c * gain_ref[...]
+    d = r * (gc - n * jnp.mean(n * gc, axis=1, keepdims=True))
+    d = d + add_ref[pl.ds(pl.multiple_of(core_ref[0] * half, half), half), :].astype(F32)
+    d_ref[...] = d
+    d_low_ref[...] = d.astype(BF16)
+
+
+def norm_back(core, both, came, middle, add, gain):
+    return pl.pallas_call(
+        norm_back_kernel,
+        out_shape=[
+            jax.ShapeDtypeStruct(both.shape, F32),
+            jax.ShapeDtypeStruct(both.shape, BF16),
+            jax.ShapeDtypeStruct((1, both.shape[1]), F32),
+        ],
+        in_specs=[smem()] + vmem(5),
+        out_specs=vmem(3),
+        compiler_params=params(),
+        cost_estimate=pl.CostEstimate(
+            flops=20 * both.size, bytes_accessed=18 * both.size, transcendentals=0
+        ),
+        name="norm_back",
+    )(core, both, came, middle, add, gain)
+
+
+def mlp_kernel(core_ref, own_ref, far_ref, gate_ref, up_ref, d_ref, hidden_ref, d_gate_ref, d_up_ref):
+    half = own_ref.shape[0]
+    core = core_ref[0]
+    for ref, at_core in ((own_ref, core), (far_ref, 1 - core)):
+        at = pl.ds(pl.multiple_of(at_core * half, half), half)
+        gate = dot(ref[...], gate_ref[...])
+        up = dot(ref[...], up_ref[...])
+        sig = 1.0 / (1.0 + jnp.exp(-gate))
+        silu = gate * sig
+        d = d_ref[at, :]
+        hidden_ref[at, :] = (silu * up).astype(BF16)
+        d_up_ref[at, :] = (d * silu).astype(BF16)
+        d_gate_ref[at, :] = (d * up * (sig * (1.0 + gate * (1.0 - sig)))).astype(BF16)
+
+
+def mlp(core, own, far, w_gate, w_up, d_hidden):
+    half, model = own.shape
+    units = w_gate.shape[1]
+    tile = math.gcd(units, 256)
+    rows_spec = pl.BlockSpec((half, model), lambda i: (0, 0))
+    weight_spec = pl.BlockSpec((model, tile), lambda i: (0, i))
+    unit_spec = pl.BlockSpec((2 * half, tile), lambda i: (0, i))
+    return pl.pallas_call(
+        mlp_kernel,
+        out_shape=[jax.ShapeDtypeStruct((2 * half, units), BF16)] * 3,
+        grid=(units // tile,),
+        in_specs=[smem(), rows_spec, rows_spec, weight_spec, weight_spec, unit_spec],
+        out_specs=[unit_spec] * 3,
+        compiler_params=params(),
+        cost_estimate=pl.CostEstimate(
+            flops=8 * half * model * units,
+            bytes_accessed=4 * model * units + 20 * half * units,
+            transcendentals=2 * half * units,
+        ),
+        name="mlp",
+    )(core, own, far, w_gate, w_up, d_hidden)
+
+
+def pair_kernel(core_ref, gate_ref, up_ref, w_gate_ref, w_up_ref, *refs):
+    half = gate_ref.shape[0] // 2
+    at = pl.ds(pl.multiple_of(core_ref[0] * half, half), half)
+    total = dot(gate_ref[at, :], w_gate_ref[...], NT) + dot(up_ref[at, :], w_up_ref[...], NT)
+    if len(refs) == 2:
+        total = total + refs[0][...].astype(F32)
+    refs[-1][...] = total.astype(BF16)
+
+
+def pair(core, d_gate, d_up, w_gate, w_up, add):
+    rows, units = d_gate.shape
+    model = w_gate.shape[0]
+    tile = math.gcd(model, 256)
+    all_spec = pl.BlockSpec((rows, units), lambda i: (0, 0))
+    weight_spec = pl.BlockSpec((tile, units), lambda i: (i, 0))
+    out_spec = pl.BlockSpec((rows // 2, tile), lambda i: (0, i))
+    return pl.pallas_call(
+        pair_kernel,
+        out_shape=jax.ShapeDtypeStruct((rows // 2, model), BF16),
+        grid=(model // tile,),
+        in_specs=[smem(), all_spec, all_spec, weight_spec, weight_spec] + [out_spec] * len(add),
+        out_specs=out_spec,
+        compiler_params=params(),
+        cost_estimate=pl.CostEstimate(
+            flops=2 * rows * units * model, bytes_accessed=4 * model * units, transcendentals=0
+        ),
+        name="pair",
+    )(core, d_gate, d_up, w_gate, w_up, *add)
 
 
 def rms_parts(value):
@@ -440,17 +755,12 @@
         away = dot(other_half(left), right).astype(BF16)
         came = core_swap(away)
         both = (dot(own_half(left), right) + came.astype(F32)).astype(BF16)
-        return both.astype(F32) + y_swap(both).astype(F32)
-
-    def columns_of(value, side):
-        cut = value.reshape(value.shape[0], planes, 2, shard)
-        return lax.dynamic_index_in_dim(cut, side, 2, keepdims=False).reshape(
-            value.shape[0], planes * shard
-        )
-
-    def gather_columns(mine):
-        came = x_swap(columns_of(mine, 1 - x_at))
-        return join(came, core_swap(came))
+        return both, y_swap(both)
+
+    def cut_columns(*parts):
+        keep, send = cut(x_at, core, parts, planes, shard, join)
+        came = x_swap(send)
+        return keep, join(came, core_swap(came))
 
     def scatter_z(stack):
         up_carry = stack(jnp.clip(planes - 1 + z_at, 0, planes - 1))
@@ -505,26 +815,22 @@
     q_gain_row = query_gain[None, :]
     k_gain_row = key_gain[None, :]
 
-    h_one, kv, k_raw = project(
+    core_at = core[None].astype(jnp.int32)
+    core_not = 1 - core_at
+    h_one, qkv, q_raw, k_raw = project(
         tokens,
         norm_attn_row,
-        (key_weight, value_weight),
-        (k_gain_row, k_gain_row),
-        (True, False),
+        (w_query, key_weight, value_weight),
+        (q_gain_row, k_gain_row, k_gain_row),
+        (True, True, False),
         cos,
         sin,
-        "project_kv",
+        "project",
     )
-    later_pairs = [(d, d + 2) for d in range(dp_size) if plane_of(d) < group_planes - 1]
-    to_first_pairs = [(d, d - 2) for d in range(dp_size) if plane_of(d) == 1]
-    kv_own = [kv]
-    came = kv
-    for step in range(1, group_planes):
-        came = lax.ppermute(came, "dp", later_pairs)
-        kv_own.append(came)
-    if group_planes > 1:
-        kv_own[1] = kv_own[1] + lax.ppermute(kv, "dp", to_first_pairs)
-    kv_far = [x_swap(b) for b in kv_own]
+    q = qkv[:, : w_query.shape[1]]
+    kv = qkv[:, w_query.shape[1] :]
+    heads_b, lse, kv_all = attn_fwd(prefix[None].astype(jnp.int32), q, kv, group, dims)
+    kv_all = lax.dynamic_update_slice(kv_all, kv[None], (0, 0, 0))
     scalars = []
     for step in range(group_planes):
         if step == 1:
@@ -535,62 +841,38 @@
         far = jnp.where(there >= 0, 2 * there + 1 - x_at, -1)
         scalars.append(jnp.stack([member, prefix, mine, far]).astype(jnp.int32))
 
-    _, q, q_raw = project(
-        tokens, norm_attn_row, (w_query,), (q_gain_row,), (True,), cos, sin, "project_q"
+    both, came = sum_tensor(heads_b, w_out)
+    d_hidden = dot(out_grad, w_down, NT)
+    og_cols, og_came = cut_columns(out_grad)
+    h_one_cols, h_one_came = cut_columns(h_one)
+    middle, h_two_half = norm_forward(core_at, both, came, tokens, norm_mlp_row)
+    h_two_far = core_swap(h_two_half)
+    hidden, d_gate, d_up = mlp(core_at, h_two_half, h_two_far, w_gate, w_up, d_hidden)
+
+    away = pair(core_not, d_gate, d_up, w_gate, w_up, [])
+    both = pair(core_at, d_gate, d_up, w_gate, w_up, [core_swap(away)])
+    came = y_swap(both)
+    d_middle_half, d_attn_half, norm_mlp_part = norm_back(
+        core_at, both, came, middle, out_grad, norm_mlp_row
     )
-    d_hidden = dot(out_grad, w_down, NT)
-
-    acc = None
-    for step in range(group_planes):
-        last = step == group_planes - 1
-        outs = attn_fwd(scalars[step], q, [kv_own[step], kv_far[step]], acc, last, dims)
-        acc = outs[0]
-    heads_b, lse = outs
-
-    x_half = own_half(tokens).astype(F32)
-    middle = x_half + sum_tensor(heads_b, w_out)
-    r_two, n_two = rms_parts(middle)
-    h_two_half = (n_two * norm_mlp_row).astype(BF16)
-    h_two = join(h_two_half, core_swap(h_two_half))
-    gate_proj = dot(h_two, w_gate)
-    up_proj = dot(h_two, w_up)
-    sig = jax.nn.sigmoid(gate_proj)
-    silu = gate_proj * sig
-    hidden = (silu * up_proj).astype(BF16)
-    d_gate = (d_hidden * up_proj * sig * (1.0 + gate_proj * (1.0 - sig))).astype(BF16)
-    d_up = (d_hidden * silu).astype(BF16)
-
-    def d_h_two_part(which):
-        return dot(which(d_gate), w_gate, NT) + dot(which(d_up), w_up, NT)
-
-    away = d_h_two_part(other_half).astype(BF16)
-    both = (d_h_two_part(own_half) + core_swap(away).astype(F32)).astype(BF16)
-    d_h_two = both.astype(F32) + y_swap(both).astype(F32)
-    out_grad_half = own_half(out_grad)
-    d_middle_half = out_grad_half.astype(F32) + rms_back(r_two, n_two, norm_mlp_row, d_h_two)
-    norm_mlp_part = jnp.sum(d_h_two * n_two, axis=0)
-    d_attn_half = d_middle_half.astype(BF16)
-    d_attn = join(d_attn_half, core_swap(d_attn_half))
-    d_heads = dot(d_attn, w_out, NT).astype(BF16)
-
-    og_came = gather_columns(out_grad_half)
+    d_attn_far = core_swap(d_attn_half)
+
     hidden_came = x_swap(hidden)
-    w_down_grad = scatter_columns(hidden, hidden_came, columns_of(out_grad, x_at), og_came)
-    h_two_came = gather_columns(h_two_half)
-    h_two_cols = columns_of(h_two, x_at)
+    w_down_grad = scatter_columns(hidden, hidden_came, og_cols, og_came)
+    h_two_cols, h_two_came = cut_columns(h_two_half, h_two_far)
     w_gate_grad = scatter_rows(h_two_cols, h_two_came, d_gate, x_swap(d_gate))
     w_up_grad = scatter_rows(h_two_cols, h_two_came, d_up, x_swap(d_up))
 
-    mlp_out = sum_tensor(hidden, w_down)
-    block_half = (middle + mlp_out).astype(BF16)
+    both, came = sum_tensor(hidden, w_down)
+    block_half = (middle + (both.astype(F32) + came.astype(F32))).astype(BF16)
     block_out = join(block_half, core_swap(block_half))
 
-    qx, dox = attn_prep(q, d_heads, heads_b, lse, width)
+    qx, dox = attn_prep(core_at, d_attn_half, d_attn_far, w_out, q, heads_b, lse, width)
     dq = None
     sums = [None] * group_planes
     for step in reversed(range(group_planes)):
         dq, d_own, d_far = attn_bwd(
-            scalars[step], qx, dox, [kv_own[step], kv_far[step]], dq, step == 0, dims
+            scalars[step], qx, dox, kv_all, (2 * step, 2 * step + 1), dq, step == 0, dims
         )
         sums[step] = (d_own, x_swap(d_far))
     earlier_pairs = [(d, d - 2) for d in range(dp_size) if plane_of(d) > 0]
@@ -607,14 +889,12 @@
     if group_planes > 1:
         kv_grad = kv_grad + came.astype(F32) + lax.ppermute(carry, "dp", from_first_pairs).astype(F32)
 
-    d_attn_came = gather_columns(d_attn_half)
-    w_out_grad = scatter_columns(heads_b, x_swap(heads_b), columns_of(d_attn, x_at), d_attn_came)
+    d_attn_cols, d_attn_came = cut_columns(d_attn_half, d_attn_far)
+    w_out_grad = scatter_columns(heads_b, x_swap(heads_b), d_attn_cols, d_attn_came)
 
     kv_width = kv_heads * width
     dq_b, q_gain_part = unproject(dq, q_raw, q_gain_row, cos, sin, 0, "unproject_q")
     dkv_b, k_gain_part = unproject(kv_grad, k_raw, k_gain_row, cos, sin, kv_width, "unproject_kv")
-    h_one_came = gather_columns(own_half(h_one))
-    h_one_cols = columns_of(h_one, x_at)
     w_query_grad = scatter_rows(h_one_cols, h_one_came, dq_b, x_swap(dq_b))
     w_kv_grad = scatter_rows(h_one_cols, h_one_came, dkv_b, x_swap(dkv_b))
 
@@ -628,6 +908,7 @@
 
     away = d_h_one_part(other_half)
     mine = d_h_one_part(own_half)
+    x_half = own_half(tokens).astype(F32)
     x_other = other_half(tokens).astype(F32)
     r_own, n_own = rms_parts(x_half)
     r_other, n_other = rms_parts(x_other)
@@ -640,7 +921,7 @@
     grad_other = d_middle_other + rms_back(r_other, n_other, norm_attn_row, d_h_one_other.astype(F32))
     tokens_grad = join(grad_own, grad_other)
 
-    norm_mlp_sum = sum_all(norm_mlp_part, [("tensor", 1)] + dp_bits)
+    norm_mlp_sum = sum_all(norm_mlp_part[0], [("tensor", 1)] + dp_bits)
     small = jnp.concatenate([norm_attn_part, q_gain_part[0], k_gain_part[0]])
     small = sum_all(small, [("tensor", 1), ("tensor", 2)] + dp_bits)
     norm_mlp_grad = lax.dynamic_slice_in_dim(norm_mlp_sum, device * shard, shard, 0)

time: 697 us -> 671 us (0.963)
  Pallas kernels: 90 us -> 152 us
  local copies, waits for them, and re-layouts: 62.2 us -> 14.9 us
  waiting for transfers between devices: 191 us -> 229 us
  matrix products: 97.4 us -> 63.4 us
  starting transfers between devices: 194 us -> 160 us
  other arithmetic: 47.9 us -> 39.1 us
    pallas_call x4 -> x10, Pallas kernels: 29.9 us -> 93.8 us  [the longest x1 35.7 us: attn_fwd(): pl.pallas_call(functools.partial(attn_fwd_kernel, group=group, kv_heads=k...]
    dot_general x30 -> x23, matrix products: 97.4 us -> 63.4 us  [dot(): return lax.dot_general(left, right, dims, preferred_element_type=F32)]
    ppermute x18 -> x14, waiting for transfers between devices: 90.1 us -> 121 us  [x_swap(): return lax.ppermute(value, 'dp', x_pairs)]
    ppermute x18, starting transfers between devices: 113 us -> 83 us  [scatter_z(): up = lax.ppermute(up_carry, 'dp', up_pairs)]
    concatenate x8 -> x0, local copies, waits for them, and re-layouts: 23.3 us -> none  [join(): jnp.concatenate([mine, theirs], 0)]
    ppermute x9, starting transfers between devices: 11.2 us -> 33.7 us  [sum_all(): lax.ppermute(value, axis, [(d, d ^ bit) for d in range(size)])]
    ppermute x4 -> x0, waiting for transfers between devices: 19.6 us -> none  [the longest x3 19.6 us: shards(): came = lax.ppermute(came, 'dp', later_pairs)]
    ppermute x4 -> x0, starting transfers between devices: 16.6 us -> none  [the longest x3 15.3 us: shards(): came = lax.ppermute(came, 'dp', later_pairs)]
  transfers between devices with their start and end apart: 88 -> 80, of which waited for: 31 -> 29; matrix products, arithmetic and copies ran while one was open for 28% -> 15% of each run, Pallas kernels for 10% -> 16%
where the time goes in v2:
time: 671 us; the launch traced here: 661 us
  waiting for transfers between devices  229 us (34%)
  starting transfers between devices  160 us (24%)
  Pallas kernels  152 us (23%)
  matrix products  63.4 us (9%)
  other arithmetic  39.1 us (6%)
  local copies, waits for them, and re-layouts  14.9 us (2%)
    ppermute x14, waiting for transfers between devices, x_swap(): return lax.ppermute(value, 'dp', x_pairs)  121 us
    ppermute x18, starting transfers between devices, scatter_z(): up = lax.ppermute(up_carry, 'dp', up_pairs)  83 us
    dot_general x23, matrix products, dot(): return lax.dot_general(left, right, dims, preferred_element_type=F32)  63.4 us
    ppermute x18, waiting for transfers between devices, scatter_z(): up = lax.ppermute(up_carry, 'dp', up_pairs)  57.8 us
    pallas_call x4, Pallas kernels, attn_bwd(): pl.pallas_call(functools.partial(attn_bwd_kernel, slots=slots, kv_heads=k...  37.4 us
    pallas_call x1, Pallas kernels, attn_fwd(): pl.pallas_call(functools.partial(attn_fwd_kernel, group=group, kv_heads=k...  35.7 us
    ppermute x9, starting transfers between devices, sum_all(): lax.ppermute(value, axis, [(d, d ^ bit) for d in range(size)])  33.7 us
    ppermute x4, waiting for transfers between devices, y_swap(): return lax.ppermute(value, 'tensor', y_pairs)  29 us
  transfers between devices with their start and end apart: 80, of which 29 were waited for; matrix products, arithmetic and copies ran while one was open for 15% of the time, Pallas kernels for 16%

profile of v2, /device:TPU:0, one launch (start us, length us, event | category | flops | bytes accessed | tf_op | source)
XLA Modules:
  0.0 660.9 jit_solution(4407537484050134218)
XLA Ops:
  3.4 8.2 %project.1 = (bf16[512,2048]{1,0:T(8,128)(2,1)}, bf16[512,1024]{1,0:T(8,128)(2,1)}, f32[512,512]{1,0:T(8,128)}, f32[512,256]{1,0:T(8,128)}) custom-call(bf16[512,2048]{1,0:T(8,128)(2,1)} %x_ref.3, f32[1,2048]{1,0:T(1,128)} %bitcast.53, bf16[2048,512]{1,0:T(8,128)(2,1)} %refs_0_.2, bf16[2048,256]{1,0:T(8,128)(2,1)} %refs_1_.1, bf16[2048,256]{1,0:T(8,128)(2,1)} %refs_2_.1, ...), custom_call_target="tpu_custom_call" | custom-call | flops 2147483648 | bytes 8388608 | tf_op jit(solution)/shard_map/project/pallas_call | solution.py:72
  13.8 35.7 %attn_fwd.1 = (bf16[512,512]{1,0:T(8,128)(2,1)}, f32[512,512]{1,0:T(8,128)}, bf16[8,512,512]{2,1,0:T(8,128)(2,1)}) custom-call(s32[1]{0:T(128)S(6)} %select_n.171.prefix_ref, bf16[512,512]{1,0:T(8,128)(2,1)} %get-tuple-element.141.q_ref, bf16[512,512]{1,0:T(8,128)(2,1)} %get-tuple-element.140.kv_ref), custom_call_target="tpu_custom_call" | custom-call | flops 8589934592 | bytes 10485760 | tf_op jit(solution)/shard_map/attn_fwd/pallas_call | solution.py:333
  59.6 23.9 %collective-permute-done.1.y_ref = bf16[256,2048]{1,0:T(8,128)(2,1)S(1)} collective-permute-done((bf16[256,2048]{1,0:T(8,128)(2,1)}, bf16[256,2048]{1,0:T(8,128)(2,1)S(1)}, u32[]{:S(2)}, u32[]{:S(2)}) %collective-permute-start.1) | collective-permute-done | bytes 1048608 | tf_op jit(solution)/shard_map/ppermute | solution.py:735
  97.7 7.9 %fusion.75.d_ref = f32[512,1536]{1,0:T(8,128)} fusion(bf16[512,2048]{1,0:T(8,128)(2,1)S(1)} %copy-done.5, bf16[1536,2048]{1,0:T(8,128)(2,1)} %param.25), kind=kOutput, calls=%fused_computation.165 | convolution fusion | flops 3221225472 | bytes 11534336 | tf_op jit(solution)/shard_map/dot_general | solution.py:24
  106.5 13.5 %mlp.1 = (bf16[512,1536]{1,0:T(8,128)(2,1)}, bf16[512,1536]{1,0:T(8,128)(2,1)}, bf16[512,1536]{1,0:T(8,128)(2,1)}) custom-call(s32[1]{0:T(128)} %bitcast.core_ref, bf16[256,2048]{1,0:T(8,128)(2,1)} %get-tuple-element.57.own_ref.refs_0_, bf16[256,2048]{1,0:T(8,128)(2,1)} %copy-done.31, bf16[2048,1536]{1,0:T(8,128)(2,1)} %w_gate_ref.3, ...), custom_call_target="tpu_custom_call" | custom-call | flops 6442450944 | bytes 20447232 | tf_op jit(solution)/shard_map/mlp/pallas_call | solution.py:632
  120.1 5.9 convolution_convert_fusion.1
  132.4 10.8 %pair.2 = bf16[256,2048]{1,0:T(8,128)(2,1)} custom-call(s32[1]{0:T(128)S(6)} %sub.49.core_ref, bf16[512,1536]{1,0:T(8,128)(2,1)} %get-tuple-element.59.gate_ref, bf16[512,1536]{1,0:T(8,128)(2,1)} %get-tuple-element.60.up_ref, bf16[2048,1536]{1,0:T(8,128)(2,1)} %w_gate_ref.3, bf16[2048,1536]{1,0:T(8,128)(2,1)} %w_up_ref.3), custom_call_target="tpu_custom_call" | custom-call | flops 3221225472 | bytes 12582912 | tf_op jit(solution)/shard_map/pair/pallas_call | solution.py:664
  145.2 30.8 %collective-permute-done.55 = bf16[256,1024]{1,0:T(8,128)(2,1)} collective-permute-done((bf16[256,1024]{1,0:T(8,128)(2,1)}, bf16[256,1024]{1,0:T(8,128)(2,1)}, u32[]{:S(2)}, u32[]{:S(2)}) %collective-permute-start.55) | collective-permute-done | bytes 524320 | tf_op jit(solution)/shard_map/ppermute | solution.py:738
  183.5 11.3 %pair.3.both_ref = bf16[256,2048]{1,0:T(8,128)(2,1)} custom-call(s32[1]{0:T(128)} %bitcast.core_ref, bf16[512,1536]{1,0:T(8,128)(2,1)} %get-tuple-element.59.gate_ref, bf16[512,1536]{1,0:T(8,128)(2,1)} %get-tuple-element.60.up_ref, bf16[2048,1536]{1,0:T(8,128)(2,1)} %w_gate_ref.3, bf16[2048,1536]{1,0:T(8,128)(2,1)} %w_up_ref.3, bf16[256,2048]{1,0:T(8,128)(2,1)} %copy-done.28), custom_call_target="tpu_custom_call" | custom-call | flops 3221225472 | bytes 12582912 | tf_op jit(solution)/shard_map/pair/pallas_call | solution.py:664
  204.6 16.3 %collective-permute-done.64 = bf16[512,1536]{1,0:T(8,128)(2,1)} collective-permute-done((bf16[512,1536]{1,0:T(8,128)(2,1)S(1)}, bf16[512,1536]{1,0:T(8,128)(2,1)}, u32[]{:S(2)}, u32[]{:S(2)}) %collective-permute-start.64) | collective-permute-done | bytes 1572896 | tf_op jit(solution)/shard_map/ppermute | solution.py:738
  230.7 23.1 %collective-permute-done.71 = bf16[512,1536]{1,0:T(8,128)(2,1)S(1)} collective-permute-done((bf16[512,1536]{1,0:T(8,128)(2,1)}, bf16[512,1536]{1,0:T(8,128)(2,1)S(1)}, u32[]{:S(2)}, u32[]{:S(2)}) %collective-permute-start.71) | collective-permute-done | bytes 1572896 | tf_op jit(solution)/shard_map/ppermute | solution.py:738
  255.6 6.1 fusion.27
  266.3 6.1 norm_back.1
  289.3 25.2 %collective-permute-start.54 = (f32[2048]{0:T(1024)S(1)}, f32[2048]{0:T(1024)S(1)}, u32[]{:S(2)}, u32[]{:S(2)}) collective-permute-start(f32[2048]{0:T(1024)S(1)} %add.486), channel_id=1, source_target_pairs={{0,16},{4,20},{8,24},{12,28},{16,0},{20,4},{24,8},{28,12},{1,17},{... | collective-permute-start | bytes 24584 | tf_op jit(solution)/shard_map/ppermute | solution.py:798
  317.0 18.7 %collective-permute-start.74 = (bf16[1536,256]{1,0:T(8,128)(2,1)S(1)}, bf16[1536,256]{1,0:T(8,128)(2,1)S(1)}, u32[]{:S(2)}, u32[]{:S(2)}) collective-permute-start(bf16[1536,256]{1,0:T(8,128)(2,1)S(1)} %get-tuple-element.106), channel_id=1, source_target_pairs={{0,8},{4,12},{1,9},{5,13},{2,10},{6,14},{3,11},{7,15}} | collective-permute-start | bytes 2359304 | tf_op jit(solution)/shard_map/ppermute | solution.py:778
  340.7 12.8 %collective-permute-done.74 = bf16[1536,256]{1,0:T(8,128)(2,1)S(1)} collective-permute-done((bf16[1536,256]{1,0:T(8,128)(2,1)S(1)}, bf16[1536,256]{1,0:T(8,128)(2,1)S(1)}, u32[]{:S(2)}, u32[]{:S(2)}) %collective-permute-start.74) | collective-permute-done | bytes 786464 | tf_op jit(solution)/shard_map/ppermute | solution.py:778
  359.2 11.1 %collective-permute-done.59 = bf16[256,1536]{1,0:T(8,128)(2,1)S(1)} collective-permute-done((bf16[256,1536]{1,0:T(8,128)(2,1)S(1)}, bf16[256,1536]{1,0:T(8,128)(2,1)S(1)}, u32[]{:S(2)}, u32[]{:S(2)}) %collective-permute-start.59) | collective-permute-done | bytes 786464 | tf_op jit(solution)/shard_map/ppermute | solution.py:778
  377.4 9.8 %collective-permute-done.66 = bf16[256,1536]{1,0:T(8,128)(2,1)S(1)} collective-permute-done((bf16[256,1536]{1,0:T(8,128)(2,1)S(1)}, bf16[256,1536]{1,0:T(8,128)(2,1)S(1)}, u32[]{:S(2)}, u32[]{:S(2)}) %collective-permute-start.66) | collective-permute-done | bytes 786464 | tf_op jit(solution)/shard_map/ppermute | solution.py:778
  389.2 14.4 %collective-permute-done.75 = bf16[1536,256]{1,0:T(8,128)(2,1)S(1)} collective-permute-done((bf16[1536,256]{1,0:T(8,128)(2,1)S(1)}, bf16[1536,256]{1,0:T(8,128)(2,1)S(1)}, u32[]{:S(2)}, u32[]{:S(2)}) %collective-permute-start.75) | collective-permute-done | bytes 786464 | tf_op jit(solution)/shard_map/ppermute | solution.py:778
  404.9 5.9 collective-permute-start.60
  413.3 5.8 attn_prep.1
  422.8 6.9 %attn_bwd.5 = (f32[512,512]{1,0:T(8,128)}, bf16[512,512]{1,0:T(8,128)(2,1)}, bf16[512,512]{1,0:T(8,128)(2,1)}) custom-call(s32[4]{0:T(128)} %get-tuple-element.150.scalar_ref, bf16[4,512,256]{2,1,0:T(8,128)(2,1)} %get-tuple-element.64.qx_ref, bf16[4,512,256]{2,1,0:T(8,128)(2,1)} %get-tuple-element.65.dox_ref, ...), custom_call_target="tpu_custom_call" | custom-call | flops 5368709120 | bytes 4194304 | tf_op jit(solution)/shard_map/attn_bwd/pallas_call | solution.py:477
  429.7 16.8 %attn_bwd.6 = (f32[512,512]{1,0:T(8,128)}, bf16[512,512]{1,0:T(8,128)(2,1)}, bf16[512,512]{1,0:T(8,128)(2,1)}) custom-call(s32[4]{0:T(128)} %get-tuple-element.149.scalar_ref, bf16[4,512,256]{2,1,0:T(8,128)(2,1)} %get-tuple-element.64.qx_ref, bf16[4,512,256]{2,1,0:T(8,128)(2,1)} %get-tuple-element.65.dox_ref, ...), custom_call_target="tpu_custom_call" | custom-call | flops 5368709120 | bytes 4194304 | tf_op jit(solution)/shard_map/attn_bwd/pallas_call | solution.py:477
  446.6 10.0 %attn_bwd.7 = (f32[512,512]{1,0:T(8,128)}, bf16[512,512]{1,0:T(8,128)(2,1)}, bf16[512,512]{1,0:T(8,128)(2,1)}) custom-call(s32[4]{0:T(128)} %get-tuple-element.100.scalar_ref, bf16[4,512,256]{2,1,0:T(8,128)(2,1)} %get-tuple-element.64.qx_ref, bf16[4,512,256]{2,1,0:T(8,128)(2,1)} %get-tuple-element.65.dox_ref, ...), custom_call_target="tpu_custom_call" | custom-call | flops 5368709120 | bytes 4194304 | tf_op jit(solution)/shard_map/attn_bwd/pallas_call | solution.py:477
  492.1 7.8 %collective-permute-done.11 = bf16[512,512]{1,0:T(8,128)(2,1)S(1)} collective-permute-done((bf16[512,512]{1,0:T(8,128)(2,1)S(1)}, bf16[512,512]{1,0:T(8,128)(2,1)S(1)}, u32[]{:S(2)}, u32[]{:S(2)}) %collective-permute-start.11) | collective-permute-done | bytes 524320 | tf_op jit(solution)/shard_map/ppermute | solution.py:738
  506.8 13.2 %collective-permute-done.43 = bf16[256,1024]{1,0:T(8,128)(2,1)S(1)} collective-permute-done((bf16[256,1024]{1,0:T(8,128)(2,1)S(1)}, bf16[256,1024]{1,0:T(8,128)(2,1)S(1)}, u32[]{:S(2)}, u32[]{:S(2)}) %collective-permute-start.43) | collective-permute-done | bytes 524320 | tf_op jit(solution)/shard_map/ppermute | solution.py:738
  526.5 8.3 %collective-permute-done.42 = bf16[512,512]{1,0:T(8,128)(2,1)S(1)} collective-permute-done((bf16[512,512]{1,0:T(8,128)(2,1)S(1)}, bf16[512,512]{1,0:T(8,128)(2,1)S(1)}, u32[]{:S(2)}, u32[]{:S(2)}) %collective-permute-start.42) | collective-permute-done | bytes 524320 | tf_op jit(solution)/shard_map/ppermute | solution.py:738
  560.7 13.0 %collective-permute-done.35 = bf16[512,512]{1,0:T(8,128)(2,1)S(1)} collective-permute-done((bf16[512,512]{1,0:T(8,128)(2,1)S(1)}, bf16[512,512]{1,0:T(8,128)(2,1)S(1)}, u32[]{:S(2)}, u32[]{:S(2)}) %collective-permute-start.35) | collective-permute-done | bytes 524320 | tf_op jit(solution)/shard_map/ppermute | solution.py:738
  596.8 5.1 collective-permute-done.18
  609.3 8.3 %collective-permute-done.37 = bf16[256,512]{1,0:T(8,128)(2,1)S(1)} collective-permute-done((bf16[256,512]{1,0:T(8,128)(2,1)S(1)}, bf16[256,512]{1,0:T(8,128)(2,1)S(1)}, u32[]{:S(2)}, u32[]{:S(2)}) %collective-permute-start.37) | collective-permute-done | bytes 262176 | tf_op jit(solution)/shard_map/ppermute | solution.py:778
  619.1 5.3 collective-permute-start.47
  626.0 7.5 %collective-permute-start.38 = (bf16[256,512]{1,0:T(8,128)(2,1)S(1)}, bf16[256,512]{1,0:T(8,128)(2,1)S(1)}, u32[]{:S(2)}, u32[]{:S(2)}) collective-permute-start(bf16[256,512]{1,0:T(8,128)(2,1)S(1)} %get-tuple-element.128), channel_id=1, source_target_pairs={{0,8},{4,12},{8,16},{12,20},{16,24},{20,28},{1,9},{5,13},{9,17},{1... | collective-permute-start | bytes 786440 | tf_op jit(solution)/shard_map/ppermute | solution.py:778
  (327 shorter events, 252.5 us)
Async XLA Ops:
  92.6 52.1 %collective-permute-start.72 = (bf16[256,1024]{1,0:T(8,128)(2,1)}, bf16[256,1024]{1,0:T(8,128)(2,1)}, u32[]{:S(2)}, u32[]{:S(2)}) collective-permute-start(bf16[256,1024]{1,0:T(8,128)(2,1)} %get-tuple-element.94), channel_id=1, source_target_pairs={{0,4},{4,0},{8,12},{12,8},{16,20},{20,16},{24,28},{28,24},{1,5},{5... | collective-permute-start | bytes 1572872 | tf_op jit(solution)/shard_map/ppermute | solution.py:738
  126.0 50.0 %collective-permute-start.3 = (bf16[256,2048]{1,0:T(8,128)(2,1)}, bf16[256,2048]{1,0:T(8,128)(2,1)S(1)}, u32[]{:S(2)}, u32[]{:S(2)}) collective-permute-start(bf16[256,2048]{1,0:T(8,128)(2,1)} %convolution_convert_fusion.1), channel_id=1, source_target_pairs={{0,1},{1,0},{2,3},{3,2},{4,5},{5,4},{6,7},{7,6},{8,9},{9,8},{10,11... | collective-permute-start | bytes 3145736 | tf_op jit(solution)/shard_map/ppermute | solution.py:732
  127.4 68.6 %collective-permute-start.57 = (bf16[512,1536]{1,0:T(8,128)(2,1)S(1)}, bf16[512,1536]{1,0:T(8,128)(2,1)}, u32[]{:S(2)}, u32[]{:S(2)}) collective-permute-start(bf16[512,1536]{1,0:T(8,128)(2,1)S(1)} %copy-done.10), channel_id=1, source_target_pairs={{0,4},{4,0},{8,12},{12,8},{16,20},{20,16},{24,28},{28,24},{1,5},{5... | collective-permute-start | bytes 4718600 | tf_op jit(solution)/shard_map/ppermute | solution.py:738
  130.9 45.1 %collective-permute-start.55 = (bf16[256,1024]{1,0:T(8,128)(2,1)}, bf16[256,1024]{1,0:T(8,128)(2,1)}, u32[]{:S(2)}, u32[]{:S(2)}) collective-permute-start(bf16[256,1024]{1,0:T(8,128)(2,1)} %get-tuple-element.92), channel_id=1, source_target_pairs={{0,4},{4,0},{8,12},{12,8},{16,20},{20,16},{24,28},{28,24},{1,5},{5... | collective-permute-start | bytes 1572872 | tf_op jit(solution)/shard_map/ppermute | solution.py:738
  143.2 39.3 %collective-permute-start.6 = (bf16[256,2048]{1,0:T(8,128)(2,1)}, bf16[256,2048]{1,0:T(8,128)(2,1)S(1)}, u32[]{:S(2)}, u32[]{:S(2)}) collective-permute-start(bf16[256,2048]{1,0:T(8,128)(2,1)} %pair.2), channel_id=1, source_target_pairs={{0,1},{1,0},{2,3},{3,2},{4,5},{5,4},{6,7},{7,6},{8,9},{9,8},{10,11... | collective-permute-start | bytes 3145736 | tf_op jit(solution)/shard_map/ppermute | solution.py:732
  144.7 143.7 %collective-permute-start.26 = (bf16[256,1024]{1,0:T(8,128)(2,1)}, bf16[256,1024]{1,0:T(8,128)(2,1)}, u32[]{:S(2)}, u32[]{:S(2)}) collective-permute-start(bf16[256,1024]{1,0:T(8,128)(2,1)} %get-tuple-element.87), channel_id=1, source_target_pairs={{0,4},{4,0},{8,12},{12,8},{16,20},{20,16},{24,28},{28,24},{1,5},{5... | collective-permute-start | bytes 1572872 | tf_op jit(solution)/shard_map/ppermute | solution.py:738
  176.0 50.4 %collective-permute-start.73 = (bf16[256,1024]{1,0:T(8,128)(2,1)}, bf16[256,1024]{1,0:T(8,128)(2,1)}, u32[]{:S(2)}, u32[]{:S(2)}) collective-permute-start(bf16[256,1024]{1,0:T(8,128)(2,1)} %collective-permute-done.72), channel_id=1, source_target_pairs={{0,1},{1,0},{2,3},{3,2},{4,5},{5,4},{6,7},{7,6},{8,9},{9,8},{10,11... | collective-permute-start | bytes 1572872 | tf_op jit(solution)/shard_map/ppermute | solution.py:732
  182.6 38.4 %collective-permute-start.64 = (bf16[512,1536]{1,0:T(8,128)(2,1)S(1)}, bf16[512,1536]{1,0:T(8,128)(2,1)}, u32[]{:S(2)}, u32[]{:S(2)}) collective-permute-start(bf16[512,1536]{1,0:T(8,128)(2,1)S(1)} %copy-done.8), channel_id=1, source_target_pairs={{0,4},{4,0},{8,12},{12,8},{16,20},{20,16},{24,28},{28,24},{1,5},{5... | collective-permute-start | bytes 4718600 | tf_op jit(solution)/shard_map/ppermute | solution.py:738
  194.8 59.0 %collective-permute-start.71 = (bf16[512,1536]{1,0:T(8,128)(2,1)}, bf16[512,1536]{1,0:T(8,128)(2,1)S(1)}, u32[]{:S(2)}, u32[]{:S(2)}) collective-permute-start(bf16[512,1536]{1,0:T(8,128)(2,1)} %get-tuple-element.58), channel_id=1, source_target_pairs={{0,4},{4,0},{8,12},{12,8},{16,20},{20,16},{24,28},{28,24},{1,5},{5... | collective-permute-start | bytes 4718600 | tf_op jit(solution)/shard_map/ppermute | solution.py:738
  196.0 93.2 %collective-permute-start.4 = (bf16[256,2048]{1,0:T(8,128)(2,1)S(1)}, bf16[256,2048]{1,0:T(8,128)(2,1)}, u32[]{:S(2)}, u32[]{:S(2)}) collective-permute-start(bf16[256,2048]{1,0:T(8,128)(2,1)S(1)} %fusion.8), channel_id=1, source_target_pairs={{0,2},{1,3},{2,0},{3,1},{4,6},{5,7},{6,4},{7,5},{8,10},{9,11},{10,... | collective-permute-start | bytes 3145736 | tf_op jit(solution)/shard_map/ppermute | solution.py:735
  220.9 44.4 %collective-permute-start.7 = (bf16[256,2048]{1,0:T(8,128)(2,1)S(1)}, bf16[256,2048]{1,0:T(8,128)(2,1)S(1)}, u32[]{:S(2)}, u32[]{:S(2)}) collective-permute-start(bf16[256,2048]{1,0:T(8,128)(2,1)S(1)} %copy-done.14), channel_id=1, source_target_pairs={{0,2},{1,3},{2,0},{3,1},{4,6},{5,7},{6,4},{7,5},{8,10},{9,11},{10,... | collective-permute-start | bytes 3145736 | tf_op jit(solution)/shard_map/ppermute | solution.py:735
  226.4 90.6 %collective-permute-start.58 = (bf16[256,1536]{1,0:T(8,128)(2,1)}, bf16[256,1536]{1,0:T(8,128)(2,1)}, u32[]{:S(2)}, u32[]{:S(2)}) collective-permute-start(bf16[256,1536]{1,0:T(8,128)(2,1)} %get-tuple-element.118), channel_id=1, source_target_pairs={{0,8},{4,12},{1,9},{5,13},{2,10},{6,14},{3,11},{7,15}} | collective-permute-start | bytes 2359304 | tf_op jit(solution)/shard_map/ppermute | solution.py:778
  253.8 81.8 %collective-permute-start.61 = (bf16[256,1536]{1,0:T(8,128)(2,1)}, bf16[256,1536]{1,0:T(8,128)(2,1)}, u32[]{:S(2)}, u32[]{:S(2)}) collective-permute-start(bf16[256,1536]{1,0:T(8,128)(2,1)} %get-tuple-element.119), channel_id=1, source_target_pairs={{24,16},{28,20},{25,17},{29,21},{26,18},{30,22},{27,19},{31,23}} | collective-permute-start | bytes 2359304 | tf_op jit(solution)/shard_map/ppermute | solution.py:779
  284.9 53.3 %collective-permute-start.65 = (bf16[256,1536]{1,0:T(8,128)(2,1)S(1)}, bf16[256,1536]{1,0:T(8,128)(2,1)S(1)}, u32[]{:S(2)}, u32[]{:S(2)}) collective-permute-start(bf16[256,1536]{1,0:T(8,128)(2,1)S(1)} %get-tuple-element.112), channel_id=1, source_target_pairs={{0,8},{4,12},{1,9},{5,13},{2,10},{6,14},{3,11},{7,15}} | collective-permute-start | bytes 2359304 | tf_op jit(solution)/shard_map/ppermute | solution.py:778
  288.4 51.1 %collective-permute-start.68 = (bf16[256,1536]{1,0:T(8,128)(2,1)S(1)}, bf16[256,1536]{1,0:T(8,128)(2,1)S(1)}, u32[]{:S(2)}, u32[]{:S(2)}) collective-permute-start(bf16[256,1536]{1,0:T(8,128)(2,1)S(1)} %get-tuple-element.113), channel_id=1, source_target_pairs={{24,16},{28,20},{25,17},{29,21},{26,18},{30,22},{27,19},{31,23}} | collective-permute-start | bytes 2359304 | tf_op jit(solution)/shard_map/ppermute | solution.py:779
  316.2 156.2 %collective-permute-start.27 = (bf16[256,1024]{1,0:T(8,128)(2,1)}, bf16[256,1024]{1,0:T(8,128)(2,1)}, u32[]{:S(2)}, u32[]{:S(2)}) collective-permute-start(bf16[256,1024]{1,0:T(8,128)(2,1)} %collective-permute-done.26), channel_id=1, source_target_pairs={{0,1},{1,0},{2,3},{3,2},{4,5},{5,4},{6,7},{7,6},{8,9},{9,8},{10,11... | collective-permute-start | bytes 1572872 | tf_op jit(solution)/shard_map/ppermute | solution.py:732
  317.0 36.5 %collective-permute-start.74 = (bf16[1536,256]{1,0:T(8,128)(2,1)S(1)}, bf16[1536,256]{1,0:T(8,128)(2,1)S(1)}, u32[]{:S(2)}, u32[]{:S(2)}) collective-permute-start(bf16[1536,256]{1,0:T(8,128)(2,1)S(1)} %get-tuple-element.106), channel_id=1, source_target_pairs={{0,8},{4,12},{1,9},{5,13},{2,10},{6,14},{3,11},{7,15}} | collective-permute-start | bytes 2359304 | tf_op jit(solution)/shard_map/ppermute | solution.py:778
  338.2 32.1 %collective-permute-start.59 = (bf16[256,1536]{1,0:T(8,128)(2,1)S(1)}, bf16[256,1536]{1,0:T(8,128)(2,1)S(1)}, u32[]{:S(2)}, u32[]{:S(2)}) collective-permute-start(bf16[256,1536]{1,0:T(8,128)(2,1)S(1)} %get-tuple-element.116), channel_id=1, source_target_pairs={{0,8},{4,12},{8,16},{12,20},{1,9},{5,13},{9,17},{13,21},{2,10},{6,... | collective-permute-start | bytes 2359304 | tf_op jit(solution)/shard_map/ppermute | solution.py:778
  339.5 35.2 %collective-permute-start.62 = (bf16[256,1536]{1,0:T(8,128)(2,1)S(1)}, bf16[256,1536]{1,0:T(8,128)(2,1)S(1)}, u32[]{:S(2)}, u32[]{:S(2)}) collective-permute-start(bf16[256,1536]{1,0:T(8,128)(2,1)S(1)} %get-tuple-element.117), channel_id=1, source_target_pairs={{24,16},{28,20},{16,8},{20,12},{25,17},{29,21},{17,9},{21,13},{26,... | collective-permute-start | bytes 2359304 | tf_op jit(solution)/shard_map/ppermute | solution.py:779
  353.5 33.7 %collective-permute-start.66 = (bf16[256,1536]{1,0:T(8,128)(2,1)S(1)}, bf16[256,1536]{1,0:T(8,128)(2,1)S(1)}, u32[]{:S(2)}, u32[]{:S(2)}) collective-permute-start(bf16[256,1536]{1,0:T(8,128)(2,1)S(1)} %get-tuple-element.110), channel_id=1, source_target_pairs={{0,8},{4,12},{8,16},{12,20},{1,9},{5,13},{9,17},{13,21},{2,10},{6,... | collective-permute-start | bytes 2359304 | tf_op jit(solution)/shard_map/ppermute | solution.py:778
  357.9 29.3 %collective-permute-start.69 = (bf16[256,1536]{1,0:T(8,128)(2,1)S(1)}, bf16[256,1536]{1,0:T(8,128)(2,1)S(1)}, u32[]{:S(2)}, u32[]{:S(2)}) collective-permute-start(bf16[256,1536]{1,0:T(8,128)(2,1)S(1)} %get-tuple-element.111), channel_id=1, source_target_pairs={{24,16},{28,20},{16,8},{20,12},{25,17},{29,21},{17,9},{21,13},{26,... | collective-permute-start | bytes 2359304 | tf_op jit(solution)/shard_map/ppermute | solution.py:779
  370.3 33.3 %collective-permute-start.75 = (bf16[1536,256]{1,0:T(8,128)(2,1)S(1)}, bf16[1536,256]{1,0:T(8,128)(2,1)S(1)}, u32[]{:S(2)}, u32[]{:S(2)}) collective-permute-start(bf16[1536,256]{1,0:T(8,128)(2,1)S(1)} %get-tuple-element.104), channel_id=1, source_target_pairs={{0,8},{4,12},{8,16},{12,20},{1,9},{5,13},{9,17},{13,21},{2,10},{6,... | collective-permute-start | bytes 2359304 | tf_op jit(solution)/shard_map/ppermute | solution.py:778
  374.8 30.2 %collective-permute-start.78 = (bf16[1536,256]{1,0:T(8,128)(2,1)S(1)}, bf16[1536,256]{1,0:T(8,128)(2,1)S(1)}, u32[]{:S(2)}, u32[]{:S(2)}) collective-permute-start(bf16[1536,256]{1,0:T(8,128)(2,1)S(1)} %get-tuple-element.105), channel_id=1, source_target_pairs={{24,16},{28,20},{16,8},{20,12},{25,17},{29,21},{17,9},{21,13},{26,... | collective-permute-start | bytes 2359304 | tf_op jit(solution)/shard_map/ppermute | solution.py:779
  387.2 76.3 %collective-permute-start.5 = (bf16[256,2048]{1,0:T(8,128)(2,1)S(1)}, bf16[256,2048]{1,0:T(8,128)(2,1)}, u32[]{:S(2)}, u32[]{:S(2)}) collective-permute-start(bf16[256,2048]{1,0:T(8,128)(2,1)S(1)} %add_convert_fusion.8), channel_id=1, source_target_pairs={{0,1},{1,0},{2,3},{3,2},{4,5},{5,4},{6,7},{7,6},{8,9},{9,8},{10,11... | collective-permute-start | bytes 3145736 | tf_op jit(solution)/shard_map/ppermute | solution.py:732
  403.6 83.0 %collective-permute-start.63 = (bf16[256,1536]{1,0:T(8,128)(2,1)}, bf16[256,1536]{1,0:T(8,128)(2,1)}, u32[]{:S(2)}, u32[]{:S(2)}) collective-permute-start(bf16[256,1536]{1,0:T(8,128)(2,1)} %get-tuple-element.115), channel_id=1, source_target_pairs={{24,16},{28,20},{16,8},{20,12},{8,0},{12,4},{25,17},{29,21},{17,9}... | collective-permute-start | bytes 2359304 | tf_op jit(solution)/shard_map/ppermute | solution.py:779
  404.9 83.5 %collective-permute-start.60 = (bf16[256,1536]{1,0:T(8,128)(2,1)}, bf16[256,1536]{1,0:T(8,128)(2,1)}, u32[]{:S(2)}, u32[]{:S(2)}) collective-permute-start(bf16[256,1536]{1,0:T(8,128)(2,1)} %get-tuple-element.114), channel_id=1, source_target_pairs={{0,8},{4,12},{8,16},{12,20},{16,24},{20,28},{1,9},{5,13},{9,17},{1... | collective-permute-start | bytes 2359304 | tf_op jit(solution)/shard_map/ppermute | solution.py:778
  472.4 30.0 %collective-permute-start.70 = (bf16[256,1536]{1,0:T(8,128)(2,1)}, bf16[256,1536]{1,0:T(8,128)(2,1)S(1)}, u32[]{:S(2)}, u32[]{:S(2)}) collective-permute-start(bf16[256,1536]{1,0:T(8,128)(2,1)} %get-tuple-element.109), channel_id=1, source_target_pairs={{24,16},{28,20},{16,8},{20,12},{8,0},{12,4},{25,17},{29,21},{17,9}... | collective-permute-start | bytes 2359304 | tf_op jit(solution)/shard_map/ppermute | solution.py:779
  486.6 36.3 %collective-permute-start.10 = (bf16[512,512]{1,0:T(8,128)(2,1)S(1)}, bf16[512,512]{1,0:T(8,128)(2,1)S(1)}, u32[]{:S(2)}, u32[]{:S(2)}) collective-permute-start(bf16[512,512]{1,0:T(8,128)(2,1)S(1)} %copy-done.46), channel_id=1, source_target_pairs={{0,4},{4,0},{8,12},{12,8},{16,20},{20,16},{24,28},{28,24},{1,5},{5... | collective-permute-start | bytes 1572872 | tf_op jit(solution)/shard_map/ppermute | solution.py:738
  522.9 56.9 %collective-permute-start.30 = (bf16[256,512]{1,0:T(8,128)(2,1)}, bf16[256,512]{1,0:T(8,128)(2,1)}, u32[]{:S(2)}, u32[]{:S(2)}) collective-permute-start(bf16[256,512]{1,0:T(8,128)(2,1)} %get-tuple-element.136), channel_id=1, source_target_pairs={{0,8},{4,12},{8,16},{12,20},{1,9},{5,13},{9,17},{13,21},{2,10},{6,... | collective-permute-start | bytes 786440 | tf_op jit(solution)/shard_map/ppermute | solution.py:778
  524.9 57.9 %collective-permute-start.33 = (bf16[256,512]{1,0:T(8,128)(2,1)}, bf16[256,512]{1,0:T(8,128)(2,1)}, u32[]{:S(2)}, u32[]{:S(2)}) collective-permute-start(bf16[256,512]{1,0:T(8,128)(2,1)} %get-tuple-element.137), channel_id=1, source_target_pairs={{24,16},{28,20},{16,8},{20,12},{25,17},{29,21},{17,9},{21,13},{26,... | collective-permute-start | bytes 786440 | tf_op jit(solution)/shard_map/ppermute | solution.py:779
  590.8 33.7 %collective-permute-start.34 = (bf16[256,512]{1,0:T(8,128)(2,1)S(1)}, bf16[256,512]{1,0:T(8,128)(2,1)S(1)}, u32[]{:S(2)}, u32[]{:S(2)}) collective-permute-start(bf16[256,512]{1,0:T(8,128)(2,1)S(1)} %get-tuple-element.135), channel_id=1, source_target_pairs={{24,16},{28,20},{16,8},{20,12},{8,0},{12,4},{25,17},{29,21},{17,9}... | collective-permute-start | bytes 786440 | tf_op jit(solution)/shard_map/ppermute | solution.py:779
  592.1 32.5 %collective-permute-start.31 = (bf16[256,512]{1,0:T(8,128)(2,1)S(1)}, bf16[256,512]{1,0:T(8,128)(2,1)S(1)}, u32[]{:S(2)}, u32[]{:S(2)}) collective-permute-start(bf16[256,512]{1,0:T(8,128)(2,1)S(1)} %get-tuple-element.134), channel_id=1, source_target_pairs={{0,8},{4,12},{8,16},{12,20},{16,24},{20,28},{1,9},{5,13},{9,17},{1... | collective-permute-start | bytes 786440 | tf_op jit(solution)/shard_map/ppermute | solution.py:778
  (97 other events, 1272.4 us)

commit v3 on v2

--- a/solution.py
+++ b/solution.py
@@ -14,6 +14,9 @@
 ROPE_BASE = 1000000.0
 MAX_PREFIX = 2048
 VMEM_LIMIT = 56 * 2**20
+BACK_VMEM_LIMIT = 60 * 2**20
+
+COST = pl.CostEstimate(flops=1000, bytes_accessed=1000, transcendentals=0)
 
 NN = (((1,), (0,)), ((), ()))
 NT = (((1,), (1,)), ((), ()))
@@ -30,6 +33,145 @@
 
 def params():
     return pltpu.CompilerParams(vmem_limit_bytes=VMEM_LIMIT)
+
+
+def greet(peers):
+    barrier = pltpu.get_barrier_semaphore()
+    count = 0
+    for peer, there in peers:
+
+        def signal(peer=peer):
+            pl.semaphore_signal(barrier, 1, device_id=peer, device_id_type=pl.DeviceIdType.MESH)
+
+        if there is True:
+            signal()
+            count = count + 1
+        else:
+            pl.when(there)(signal)
+            count = count + there.astype(jnp.int32)
+    pl.semaphore_wait(barrier, count)
+
+
+def remote(src, dst, send, recv, peer):
+    return pltpu.make_async_remote_copy(
+        src_ref=src,
+        dst_ref=dst,
+        send_sem=send,
+        recv_sem=recv,
+        device_id=peer,
+        device_id_type=pl.DeviceIdType.MESH,
+    )
+
+
+def tensor_peers():
+    t = lax.axis_index("tensor")
+    core = t % 2
+    y = t // 2
+    return core, {"tensor": t + 1 - 2 * core}, {"tensor": t + 2 - 4 * y}
+
+
+def rows_of(core, half):
+    return pl.ds(pl.multiple_of(core * half, half), half)
+
+
+def cut_into(out, out_rows, ref, ref_rows, side, planes, shard):
+    for z in range(planes):
+        to = slice(z * shard, (z + 1) * shard)
+        if shard % 128 == 0:
+            at = pl.ds(pl.multiple_of((2 * z + side) * shard, shard), shard)
+            out[out_rows, to] = ref[ref_rows, at]
+        else:
+            low = ref[ref_rows, 2 * z * shard : (2 * z + 1) * shard]
+            high = ref[ref_rows, (2 * z + 1) * shard : (2 * z + 2) * shard]
+            out[out_rows, to] = jnp.where(side == 0, low, high)
+
+
+class Columns:
+    def __init__(self, own, far, keep, came, scratch, x_at, core, x_peer, core_peer, planes, shard):
+        self.own, self.far, self.keep, self.came = own, far, keep, came
+        self.send_ref, self.recv_ref, self.sems = scratch[0], scratch[1], scratch[2:]
+        self.x_at, self.core, self.cut = x_at, core, (planes, shard)
+        self.x_peer, self.core_peer = x_peer, core_peer
+        self.half = own.shape[0]
+
+    @staticmethod
+    def scratch(half, columns):
+        return [pltpu.VMEM((half, columns), BF16)] * 2 + [pltpu.SemaphoreType.DMA] * 4
+
+    def over_x(self):
+        return remote(self.send_ref, self.recv_ref, self.sems[0], self.sems[1], self.x_peer)
+
+    def over_core(self):
+        there = self.came.at[rows_of(self.core, self.half), :]
+        return remote(self.recv_ref, there, self.sems[2], self.sems[3], self.core_peer)
+
+    def start(self):
+        every = slice(None)
+        cut_into(self.send_ref, every, self.own, every, 1 - self.x_at, *self.cut)
+        self.over_x().start()
+
+    def store(self):
+        every = slice(None)
+        for ref, core in ((self.own, self.core), (self.far, 1 - self.core)):
+            cut_into(self.keep, rows_of(core, self.half), ref, every, self.x_at, *self.cut)
+
+    def forward(self):
+        self.over_x().wait_recv()
+        self.over_core().start()
+        self.came[rows_of(self.core, self.half), :] = self.recv_ref[...]
+
+    def finish(self):
+        self.over_core().wait_recv()
+        self.over_x().wait_send()
+        self.over_core().wait_send()
+
+
+class TensorSum:
+    def __init__(self, scratch, core, core_peer, y_peer):
+        (self.away, self.core_came, self.both, self.y_came, self.mine) = scratch[:5]
+        self.sems = scratch[5:]
+        self.core, self.core_peer, self.y_peer = core, core_peer, y_peer
+        self.chunks, self.half, self.width = self.away.shape
+
+    @staticmethod
+    def scratch(chunks, half, width):
+        return (
+            [pltpu.VMEM((chunks, half, width), BF16)] * 4
+            + [pltpu.VMEM((2, 2 * half, width), F32)]
+            + [pltpu.SemaphoreType.DMA((chunks,))] * 4
+        )
+
+    def over_core(self, i):
+        s = self.sems
+        return remote(self.away.at[i], self.core_came.at[i], s[0].at[i], s[1].at[i], self.core_peer)
+
+    def over_y(self, i):
+        s = self.sems
+        return remote(self.both.at[i], self.y_came.at[i], s[2].at[i], s[3].at[i], self.y_peer)
+
+    def add(self, i, value):
+        self.mine[i % 2] = value
+        self.away[i] = self.mine[i % 2, rows_of(1 - self.core, self.half), :].astype(BF16)
+        self.over_core(i).start()
+        if i > 0:
+            self.pass_on(i - 1)
+        if i == self.chunks - 1:
+            self.pass_on(i)
+
+    def pass_on(self, i):
+        self.over_core(i).wait_recv()
+        mine = self.mine[i % 2, rows_of(self.core, self.half), :]
+        self.both[i] = (mine + self.core_came[i].astype(F32)).astype(BF16)
+        self.over_y(i).start()
+
+    def total(self, i):
+        self.over_y(i).wait_recv()
+        return self.both[i].astype(F32) + self.y_came[i].astype(F32)
+
+    def finish(self):
+        for i in range(self.chunks):
+            self.over_core(i).wait_send()
+            self.over_y(i).wait_send()
 
 
 def roll_half(value):
@@ -79,11 +221,7 @@
         in_specs=vmem(4 + 2 * len(weights)),
         out_specs=vmem(2 + len(raws)),
         compiler_params=params(),
-        cost_estimate=pl.CostEstimate(
-            flops=2 * rows * model * columns,
-            bytes_accessed=4 * rows * model + 2 * model * columns,
-            transcendentals=0,
-        ),
+        cost_estimate=COST,
         name=name,
     )(x, gain, *weights, *gains, cos, sin)
 
@@ -116,20 +254,9 @@
         in_specs=vmem(5),
         out_specs=vmem(2),
         compiler_params=params(),
-        cost_estimate=pl.CostEstimate(
-            flops=20 * rows * columns, bytes_accessed=10 * rows * columns, transcendentals=0
-        ),
+        cost_estimate=COST,
         name=name,
     )(d, raw, gain, cos, sin)
-
-
-def block_flags(scalar_ref, slot, rows):
-    member, prefix = scalar_ref[0], scalar_ref[1]
-    other = scalar_ref[2 + slot]
-    key0 = other * rows
-    needed = (other >= 0) & ((other <= member) | (key0 < prefix))
-    full = (other < member) | (key0 + rows <= prefix)
-    return key0, needed, full
 
 
 def visible(shape, key0, row0, prefix):
@@ -220,6 +347,7 @@
             device_id_type=pl.DeviceIdType.MESH,
         )
 
+    all_ref[0] = kv_ref[...]
     ones = jnp.ones((rows, width), BF16)
     row0 = member * rows
 
@@ -353,11 +481,7 @@
         compiler_params=pltpu.CompilerParams(
             vmem_limit_bytes=VMEM_LIMIT, collective_id=0, has_side_effects=True
         ),
-        cost_estimate=pl.CostEstimate(
-            flops=group * 8 * rows * rows * columns,
-            bytes_accessed=40 * rows * columns,
-            transcendentals=group * rows * rows * heads,
-        ),
+        cost_estimate=COST,
         name="attn_fwd",
     )(prefix, q, kv)
 
@@ -400,103 +524,361 @@
         in_specs=[pl.BlockSpec(memory_space=pltpu.SMEM)] + vmem(6),
         out_specs=vmem(2),
         compiler_params=params(),
-        cost_estimate=pl.CostEstimate(
-            flops=2 * rows * columns * w_out.shape[1],
-            bytes_accessed=14 * rows * columns,
-            transcendentals=0,
-        ),
+        cost_estimate=COST,
         name="attn_prep",
     )(core, d_own, d_far, w_out, q, out, lse)
 
 
-def attn_bwd_kernel(scalar_ref, qx_ref, dox_ref, *refs, slots, kv_heads, repeat, width, coef, scale, first, last):
-    kv_refs = refs[:slots]
-    rest = refs[slots:]
-    if not first:
-        dq_in, rest = rest[0], rest[1:]
-    dq_ref = rest[0]
-    dkv_refs = rest[1:]
+def back_kernel(
+    *refs, group, planes, all_planes, shard, kv_heads, repeat, width, coef, scale, sums
+):
+    refs = list(refs)
+
+    def take(count):
+        out = refs[:count]
+        del refs[:count]
+        return out
+
+    prefix_ref, qx_ref, dox_ref, kv_ref = take(4)
+    h_own_ref, h_far_ref, a_own_ref, a_far_ref, heads_ref, up_ref = take(6)
+    if sums:
+        hid_ref, hid_came_ref, og_ref, og_came_ref, gate_ref = take(5)
+    dq_ref, grad_ref, h_ref, h_came_ref, a_ref, a_came_ref, heads_came_ref, up_came_ref = take(8)
+    if sums:
+        w_down_ref, w_gate_ref, w_out_ref = take(3)
+    own_ref, far_ref, xr_ref, zr_ref, first_ref = take(5)
+    send_x, recv_x, send_z, recv_z, send_first, recv_first = take(6)
+    swap_sems = take(4)
+    h_scratch, a_scratch = take(6), take(6)
+    if sums:
+        gate_came_ref, send_gate, recv_gate = take(3)
+        down_sum, gate_sum, out_sum = take(6), take(6), take(6)
+
     rows = qx_ref.shape[1]
     kv_width = kv_heads * width
-    if first:
-        dq_ref[...] = jnp.zeros_like(dq_ref)
-    else:
-        dq_ref[...] = dq_in[...]
+    device = lax.axis_index("dp")
+    member = device % group
+    plane = member // 2
+    last = planes - 1
+    x_at = member % 2
+    x_other = device + 1 - 2 * x_at
+    inner = plane < last
+    prefix = prefix_ref[0]
+
+    core, core_peer, _ = tensor_peers()
+    x_peer = {"dp": x_other}
+    greet(
+        [(x_peer, True), (core_peer, True), ({"dp": device + 2}, inner), ({"dp": device - 2}, plane > 0)]
+    )
+
+    def copy(src, dst, send, recv, there):
+        return remote(src, dst, send, recv, {"dp": there})
+
+    def columns(own, far, keep, came, scratch):
+        return Columns(
+            own, far, keep, came, scratch, x_at, core, x_peer, core_peer, all_planes, shard
+        )
+
+    h_two = columns(h_own_ref, h_far_ref, h_ref, h_came_ref, h_scratch)
+    d_attn = columns(a_own_ref, a_far_ref, a_ref, a_came_ref, a_scratch)
+    heads_swap = copy(heads_ref, heads_came_ref, swap_sems[0], swap_sems[1], x_other)
+    up_swap = copy(up_ref, up_came_ref, swap_sems[2], swap_sems[3], x_other)
+
+    def up(parts, j):
+        stack, came, send_up, recv_up = parts[:4]
+        return copy(stack.at[j], came.at[j], send_up.at[j], recv_up.at[j], device + 2)
+
+    def down(parts, j):
+        stack, came, _, _, send_down, recv_down = parts
+        slot = jnp.where(plane - 1 == j, planes, j)
+        return copy(stack.at[j], came.at[slot], send_down.at[j], recv_down.at[j], device - 2)
+
+    def sum_start(parts):
+        @pl.when(plane == 0)
+        def _():
+            for j in range(last, 0, -1):
+                up(parts, j).start()
+
+        @pl.when(plane == last)
+        def _():
+            for j in range(last):
+                down(parts, j).start()
+
+    def sum_wave(parts, wave):
+        stack, came = parts[:2]
+        j = last - wave
+        i = wave
+
+        @pl.when((plane > 0) & (plane < j))
+        def _():
+            up(parts, j).wait_recv()
+            stack[j] += came[j]
+            up(parts, j).start()
+
+        @pl.when((plane < last) & (plane > i))
+        def _():
+            down(parts, i).wait_recv()
+            stack[i] += came[i]
+            down(parts, i).start()
+
+    def sum_finish(parts, out):
+        stack, came = parts[:2]
+        out[...] = stack[plane].astype(F32)
+
+        @pl.when(plane > 0)
+        def _():
+            up(parts, plane).wait_recv()
+            out[...] += came[plane].astype(F32)
+
+        @pl.when(plane < last)
+        def _():
+            down(parts, plane).wait_recv()
+            out[...] += came[planes].astype(F32)
+
+        for j in range(planes):
+            pl.when(plane < j)(lambda j=j: up(parts, j).wait_send())
+            pl.when(plane > j)(lambda j=j: down(parts, j).wait_send())
+
+    def gate_swap():
+        return copy(gate_ref, gate_came_ref, send_gate, recv_gate, x_other)
+
+    def column_terms(stack, left, left_came, right, right_came):
+        tile = 256
+
+        def body(t, carry):
+            at = pl.ds(pl.multiple_of(t * tile, tile), tile)
+            term = dot(left[:, at], right[...], TN) + dot(left_came[:, at], right_came[...], TN)
+            for j in range(planes):
+                stack[j, at, :] = term[:, j * shard : (j + 1) * shard].astype(BF16)
+            return carry
+
+        lax.fori_loop(0, left.shape[1] // tile, body, 0)
+
+    def down_terms():
+        column_terms(down_sum[0], hid_ref, hid_came_ref, og_ref, og_came_ref)
+
+    def out_terms():
+        column_terms(out_sum[0], heads_ref, heads_came_ref, a_ref, a_came_ref)
+
+    def gate_terms():
+        stack = gate_sum[0]
+
+        def body(j, carry):
+            at = pl.ds(pl.multiple_of(j * shard, shard), shard)
+            stack[j] = (
+                dot(h_ref[:, at], gate_ref[...], TN) + dot(h_came_ref[:, at], gate_came_ref[...], TN)
+            ).astype(BF16)
+            return carry
+
+        lax.fori_loop(0, planes, body, 0)
+
     lane = lax.broadcasted_iota(jnp.int32, (rows, width), 1)
     minus = jnp.where(lane < 3, -1.0, 0.0).astype(BF16)
-    row0 = scalar_ref[0] * rows
-    prefix = scalar_ref[1]
-    for slot in range(slots):
-        key0, needed, full = block_flags(scalar_ref, slot, rows)
-
-        def work(masked, slot=slot, key0=key0):
-            for h in range(kv_heads):
-                k_at = slice(h * width, (h + 1) * width)
-                v_at = slice(kv_width + h * width, kv_width + (h + 1) * width)
-                k = kv_refs[slot][:, k_at]
-                v = kv_refs[slot][:, v_at]
-                kx = jnp.concatenate([k, minus], axis=1)
-                vx = jnp.concatenate([v, minus], axis=1)
-                dk = jnp.zeros((rows, width), F32)
-                dv = jnp.zeros((rows, width), F32)
-                for g in range(repeat):
-                    head = h * repeat + g
-                    qx = qx_ref[head]
-                    dox = dox_ref[head]
-                    p = jnp.exp2(dot(qx, kx, NT) * coef)
-                    if masked:
-                        p = jnp.where(visible(p.shape, key0, row0, prefix), p, 0.0)
-                    ds = (p * dot(dox, vx, NT)).astype(BF16)
-                    dv += dot(p.astype(BF16), dox[:, :width], TN)
-                    dk += dot(ds, qx[:, :width], TN)
-                    dq_ref[:, head * width : (head + 1) * width] += dot(ds, k)
-                dkv_refs[slot][:, k_at] = (dk * scale).astype(BF16)
-                dkv_refs[slot][:, v_at] = dv.astype(BF16)
-
-        pl.when(needed & full)(functools.partial(work, False))
-        pl.when(needed & jnp.logical_not(full))(functools.partial(work, True))
-
-        @pl.when(jnp.logical_not(needed))
-        def _(slot=slot):
-            dkv_refs[slot][...] = jnp.zeros_like(dkv_refs[slot])
-
-    if last:
-        dq_ref[...] = dq_ref[...] * scale
-
-
-def attn_bwd(scalars, qx, dox, stack, at, dq, last, dims):
+    row0 = member * rows
+
+    def work(block, other, masked, out):
+        key0 = other * rows
+
+        def head_group(h, carry):
+            k_at = pl.ds(pl.multiple_of(h * width, width), width)
+            v_at = pl.ds(pl.multiple_of(kv_width + h * width, width), width)
+            k = kv_ref[block, :, k_at]
+            v = kv_ref[block, :, v_at]
+            kx = jnp.concatenate([k, minus], axis=1)
+            vx = jnp.concatenate([v, minus], axis=1)
+            dk = jnp.zeros((rows, width), F32)
+            dv = jnp.zeros((rows, width), F32)
+            for g in range(repeat):
+                head = h * repeat + g
+                qx = qx_ref[head]
+                dox = dox_ref[head]
+                p = jnp.exp2(dot(qx, kx, NT) * coef)
+                if masked:
+                    p = jnp.where(visible(p.shape, key0, row0, prefix), p, 0.0)
+                ds = (p * dot(dox, vx, NT)).astype(BF16)
+                dv += dot(p.astype(BF16), dox[:, :width], TN)
+                dk += dot(ds, qx[:, :width], TN)
+                dq_ref[:, pl.ds(pl.multiple_of(head * width, width), width)] += dot(ds, k)
+            out[:, k_at] = (dk * scale).astype(BF16)
+            out[:, v_at] = dv.astype(BF16)
+            return carry
+
+        lax.fori_loop(0, kv_heads, head_group, 0)
+
+    def far_swap(slot):
+        return copy(far_ref.at[slot], xr_ref.at[slot], send_x.at[slot], recv_x.at[slot], x_other)
+
+    def to_plane(slot):
+        return copy(own_ref.at[slot], zr_ref.at[slot], send_z.at[slot], recv_z.at[slot], device - 2)
+
+    def from_first():
+        return copy(own_ref.at[1], first_ref, send_first, recv_first, device + 2)
+
+    def attend(slot):
+        there = 2 * (plane - slot)
+        far, own = there + 1 - x_at, there + x_at
+
+        def both(far, own, masked):
+            work(2 * slot + 1, far, masked, far_ref.at[slot])
+            far_swap(slot).start()
+            work(2 * slot, own, masked, own_ref.at[slot])
+
+        if slot == 0:
+            both(far, own, True)
+        elif slot == 1:
+            pl.when(plane == 0)(lambda: both(3 - x_at, 2 + x_at, True))
+            pl.when(plane > 0)(lambda: both(far, own, False))
+        else:
+            pl.when(plane >= slot)(lambda: both(far, own, False))
+
+    def pass_back(slot):
+        def go():
+            far_swap(slot).wait_recv()
+            own_ref[slot] += xr_ref[slot]
+            if slot < last:
+
+                @pl.when(inner & (plane >= slot))
+                def _():
+                    to_plane(slot + 1).wait_recv()
+                    own_ref[slot] += zr_ref[slot + 1]
+
+            if slot == 1:
+                pl.when(plane == 0)(lambda: from_first().start())
+                pl.when(plane > 0)(lambda: to_plane(slot).start())
+            else:
+                to_plane(slot).start()
+
+        if slot == 1:
+            go()
+        else:
+            pl.when(plane >= slot)(go)
+
+    dq_ref[...] = jnp.zeros_like(dq_ref)
+    if sums:
+        gate_swap().start()
+        down_terms()
+        sum_start(down_sum)
+    h_two.start()
+    h_two.store()
+    d_attn.store()
+    pending = list(range(last, 0, -1))
+    waves = list(range(max(last - 1, 0)))
+    for count, slot in enumerate(range(last, -1, -1)):
+        attend(slot)
+        if sums and count >= 1 and count - 1 < len(waves):
+            sum_wave(down_sum, waves[count - 1])
+        if count >= 1 and slot >= 1:
+            pass_back(pending.pop(0))
+        if slot == min(1, last):
+            h_two.forward()
+            d_attn.start()
+            heads_swap.start()
+            if sums:
+                gate_swap().wait_recv()
+                h_two.over_core().wait_recv()
+                gate_terms()
+                sum_start(gate_sum)
+    up_swap.start()
+    while pending:
+        pass_back(pending.pop(0))
+    dq_ref[...] = dq_ref[...] * scale
+    d_attn.forward()
+    heads_swap.wait_recv()
+    d_attn.over_core().wait_recv()
+    if sums:
+        out_terms()
+        sum_start(out_sum)
+        for wave in waves:
+            sum_wave(gate_sum, wave)
+        for wave in waves:
+            sum_wave(out_sum, wave)
+
+    far_swap(0).wait_recv()
+    grad_ref[...] = own_ref[0].astype(F32) + xr_ref[0].astype(F32)
+    if last > 0:
+
+        @pl.when(inner)
+        def _():
+            to_plane(1).wait_recv()
+            grad_ref[...] += zr_ref[1].astype(F32)
+
+        @pl.when(plane == 1)
+        def _():
+            from_first().wait_recv()
+            grad_ref[...] += first_ref[...].astype(F32)
+
+    if sums:
+        sum_finish(down_sum, w_down_ref)
+        sum_finish(gate_sum, w_gate_ref)
+        sum_finish(out_sum, w_out_ref)
+        gate_swap().wait_send()
+    up_swap.wait_recv()
+    up_swap.wait_send()
+    heads_swap.wait_send()
+    for part in (h_two, d_attn):
+        part.over_x().wait_send()
+        part.over_core().wait_send()
+    if not sums:
+        h_two.over_core().wait_recv()
+    for slot in range(planes):
+        if slot <= 1:
+            far_swap(slot).wait_send()
+        else:
+            pl.when(plane >= slot)(lambda slot=slot: far_swap(slot).wait_send())
+        if slot >= 1:
+            pl.when(plane >= slot)(lambda slot=slot: to_plane(slot).wait_send())
+    if last > 0:
+        pl.when(plane == 0)(lambda: from_first().wait_send())
+
+
+def back(prefix, qx, dox, kv_all, shared, grads, group, all_planes, shard, dims):
     kv_heads, repeat, width = dims
     rows = qx.shape[1]
     columns = kv_heads * repeat * width
-    first = dq is None
-    slots = len(at)
-    args = [scalars, qx, dox] + [stack] * slots + ([] if first else [dq])
-    block = stack.shape[1:]
-    out_shape = [jax.ShapeDtypeStruct((rows, columns), F32)] + [jax.ShapeDtypeStruct(block, BF16)] * slots
-    picks = [pl.BlockSpec((None,) + block, lambda i, j=j: (j, 0, 0)) for j in at]
+    planes = group // 2
+    block = kv_all.shape[1:]
+    dma = pltpu.SemaphoreType.DMA
+    heads, d_up = shared[4:]
+    units = d_up.shape[1]
+    cut_shape = jax.ShapeDtypeStruct((rows, all_planes * shard), BF16)
+    out_shape = [jax.ShapeDtypeStruct((rows, columns), F32), jax.ShapeDtypeStruct(block, F32)]
+    out_shape += [cut_shape] * 4
+    out_shape += [jax.ShapeDtypeStruct(heads.shape, BF16), jax.ShapeDtypeStruct(d_up.shape, BF16)]
+    scratch = [pltpu.VMEM((planes,) + block, BF16)] * 4 + [pltpu.VMEM(block, BF16)]
+    scratch += [dma((planes,))] * 4 + [dma, dma] + [dma] * 4
+    scratch += Columns.scratch(rows // 2, all_planes * shard) * 2
+    args = [prefix, qx, dox, kv_all, *shared]
+    if grads is not None:
+        args += grads
+        shapes = (units, shard), (shard, units), (heads.shape[1], shard)
+        out_shape += [jax.ShapeDtypeStruct(s, F32) for s in shapes]
+        scratch += [pltpu.VMEM((rows, units), BF16), dma, dma]
+        for shape in shapes:
+            scratch += [pltpu.VMEM((n,) + shape, BF16) for n in (planes, planes + 1)]
+            scratch += [dma((planes,))] * 4
     return pl.pallas_call(
         functools.partial(
-            attn_bwd_kernel,
-            slots=slots,
+            back_kernel,
+            group=group,
+            planes=planes,
+            all_planes=all_planes,
+            shard=shard,
             kv_heads=kv_heads,
             repeat=repeat,
             width=width,
             coef=math.log2(math.e) / math.sqrt(width),
             scale=1.0 / math.sqrt(width),
-            first=first,
-            last=last,
+            sums=grads is not None,
         ),
         out_shape=out_shape,
-        grid=(1,),
-        in_specs=[pl.BlockSpec(memory_space=pltpu.SMEM)] + vmem(2) + picks + vmem(0 if first else 1),
-        out_specs=vmem(len(out_shape)),
-        compiler_params=params(),
-        cost_estimate=pl.CostEstimate(
-            flops=slots * 20 * rows * rows * columns,
-            bytes_accessed=16 * rows * columns,
-            transcendentals=slots * rows * rows * kv_heads * repeat,
+        in_specs=[smem()] + vmem(8) + [pl.BlockSpec(memory_space=pl.ANY)] + vmem(len(args) - 10),
+        out_specs=vmem(7) + [pl.BlockSpec(memory_space=pl.ANY)] + vmem(len(out_shape) - 8),
+        scratch_shapes=scratch,
+        compiler_params=pltpu.CompilerParams(
+            vmem_limit_bytes=BACK_VMEM_LIMIT, collective_id=1, has_side_effects=True
         ),
-        name="attn_bwd",
+        cost_estimate=COST,
+        name="back",
     )(*args)
 
 
@@ -545,9 +927,7 @@
         in_specs=[smem()] + vmem(len(parts)),
         out_specs=vmem(2),
         compiler_params=params(),
-        cost_estimate=pl.CostEstimate(
-            flops=0, bytes_accessed=10 * half * planes * shard, transcendentals=0
-        ),
+        cost_estimate=COST,
         name="cut",
     )(jnp.stack([x_at, core]).astype(jnp.int32), *parts)
 
@@ -568,43 +948,9 @@
         in_specs=[smem()] + vmem(4),
         out_specs=vmem(2),
         compiler_params=params(),
-        cost_estimate=pl.CostEstimate(
-            flops=10 * both.size, bytes_accessed=14 * both.size, transcendentals=0
-        ),
+        cost_estimate=COST,
         name="norm_forward",
     )(core, both, came, x, gain)
-
-
-def norm_back_kernel(core_ref, both_ref, y_ref, middle_ref, add_ref, gain_ref, d_ref, d_low_ref, gain_out_ref):
-    half = both_ref.shape[0]
-    c = both_ref[...].astype(F32) + y_ref[...].astype(F32)
-    v = middle_ref[...]
-    r = lax.rsqrt(jnp.mean(v * v, axis=1, keepdims=True) + EPS)
-    n = v * r
-    gain_out_ref[...] = jnp.sum(c * n, axis=0, keepdims=True)
-    gc = c * gain_ref[...]
-    d = r * (gc - n * jnp.mean(n * gc, axis=1, keepdims=True))
-    d = d + add_ref[pl.ds(pl.multiple_of(core_ref[0] * half, half), half), :].astype(F32)
-    d_ref[...] = d
-    d_low_ref[...] = d.astype(BF16)
-
-
-def norm_back(core, both, came, middle, add, gain):
-    return pl.pallas_call(
-        norm_back_kernel,
-        out_shape=[
-            jax.ShapeDtypeStruct(both.shape, F32),
-            jax.ShapeDtypeStruct(both.shape, BF16),
-            jax.ShapeDtypeStruct((1, both.shape[1]), F32),
-        ],
-        in_specs=[smem()] + vmem(5),
-        out_specs=vmem(3),
-        compiler_params=params(),
-        cost_estimate=pl.CostEstimate(
-            flops=20 * both.size, bytes_accessed=18 * both.size, transcendentals=0
-        ),
-        name="norm_back",
-    )(core, both, came, middle, add, gain)
 
 
 def mlp_kernel(core_ref, own_ref, far_ref, gate_ref, up_ref, d_ref, hidden_ref, d_gate_ref, d_up_ref):
@@ -636,43 +982,118 @@
         in_specs=[smem(), rows_spec, rows_spec, weight_spec, weight_spec, unit_spec],
         out_specs=[unit_spec] * 3,
         compiler_params=params(),
-        cost_estimate=pl.CostEstimate(
-            flops=8 * half * model * units,
-            bytes_accessed=4 * model * units + 20 * half * units,
-            transcendentals=2 * half * units,
-        ),
+        cost_estimate=COST,
         name="mlp",
     )(core, own, far, w_gate, w_up, d_hidden)
 
 
-def pair_kernel(core_ref, gate_ref, up_ref, w_gate_ref, w_up_ref, *refs):
-    half = gate_ref.shape[0] // 2
-    at = pl.ds(pl.multiple_of(core_ref[0] * half, half), half)
-    total = dot(gate_ref[at, :], w_gate_ref[...], NT) + dot(up_ref[at, :], w_up_ref[...], NT)
-    if len(refs) == 2:
-        total = total + refs[0][...].astype(F32)
-    refs[-1][...] = total.astype(BF16)
-
-
-def pair(core, d_gate, d_up, w_gate, w_up, add):
-    rows, units = d_gate.shape
-    model = w_gate.shape[0]
-    tile = math.gcd(model, 256)
-    all_spec = pl.BlockSpec((rows, units), lambda i: (0, 0))
-    weight_spec = pl.BlockSpec((tile, units), lambda i: (i, 0))
-    out_spec = pl.BlockSpec((rows // 2, tile), lambda i: (0, i))
+def d_middle_kernel(
+    hid_ref,
+    d_gate_ref,
+    d_up_ref,
+    w_gate_ref,
+    w_up_ref,
+    middle_ref,
+    add_ref,
+    gain_ref,
+    hid_came_ref,
+    d_ref,
+    own_ref,
+    far_ref,
+    gain_out_ref,
+    gate_buf,
+    up_buf,
+    load_sems,
+    c_ref,
+    hid_send,
+    hid_recv,
+    far_send,
+    far_recv,
+    *scratch,
+    blocks,
+):
+    device = lax.axis_index("dp")
+    core, core_peer, y_peer = tensor_peers()
+    x_peer = {"dp": device + 1 - 2 * (device % 2)}
+    half = middle_ref.shape[0]
+    total = TensorSum(scratch, core, core_peer, y_peer)
+    chunks, width = total.chunks, total.width
+
+    def loads(i):
+        at = pl.ds(i * width, width)
+        return (
+            pltpu.make_async_copy(w_gate_ref.at[at, :], gate_buf.at[i], load_sems.at[2 * i]),
+            pltpu.make_async_copy(w_up_ref.at[at, :], up_buf.at[i], load_sems.at[2 * i + 1]),
+        )
+
+    for i in range(chunks):
+        for load in loads(i):
+            load.start()
+    greet([(x_peer, True), (core_peer, True), (y_peer, True)])
+    swap = remote(hid_ref, hid_came_ref, hid_send, hid_recv, x_peer)
+    swap.start()
+    for i in range(chunks):
+        for load in loads(i):
+            load.wait()
+        total.add(i, dot(d_gate_ref[...], gate_buf[i], NT) + dot(d_up_ref[...], up_buf[i], NT))
+    for i in range(chunks):
+        c_ref[:, i * width : (i + 1) * width] = total.total(i)
+
+    step = half // blocks
+
+    def to_core(b):
+        at = slice(b * step, (b + 1) * step)
+        return remote(own_ref.at[at, :], far_ref.at[at, :], far_send.at[b], far_recv.at[b], core_peer)
+
+    gain_out_ref[...] = jnp.zeros_like(gain_out_ref)
+    for b in range(blocks):
+        at = slice(b * step, (b + 1) * step)
+        add_at = pl.ds(pl.multiple_of(core * half + b * step, step), step)
+        c = c_ref[at, :]
+        v = middle_ref[at, :]
+        r = lax.rsqrt(jnp.mean(v * v, axis=1, keepdims=True) + EPS)
+        n = v * r
+        gain_out_ref[...] += jnp.sum(c * n, axis=0, keepdims=True)
+        gc = c * gain_ref[...]
+        d = r * (gc - n * jnp.mean(n * gc, axis=1, keepdims=True)) + add_ref[add_at, :].astype(F32)
+        d_ref[at, :] = d
+        own_ref[at, :] = d.astype(BF16)
+        to_core(b).start()
+    for b in range(blocks):
+        to_core(b).wait_recv()
+        to_core(b).wait_send()
+    total.finish()
+    swap.wait_recv()
+    swap.wait_send()
+
+
+def d_middle_of(hidden, d_gate, d_up, w_gate, w_up, middle, out_grad, gain):
+    half, model = middle.shape
+    units = hidden.shape[1]
+    chunks, blocks = 4, 4
+    width = model // chunks
+    dma = pltpu.SemaphoreType.DMA
+    anywhere = pl.BlockSpec(memory_space=pl.ANY)
     return pl.pallas_call(
-        pair_kernel,
-        out_shape=jax.ShapeDtypeStruct((rows // 2, model), BF16),
-        grid=(model // tile,),
-        in_specs=[smem(), all_spec, all_spec, weight_spec, weight_spec] + [out_spec] * len(add),
-        out_specs=out_spec,
-        compiler_params=params(),
-        cost_estimate=pl.CostEstimate(
-            flops=2 * rows * units * model, bytes_accessed=4 * model * units, transcendentals=0
+        functools.partial(d_middle_kernel, blocks=blocks),
+        out_shape=[
+            jax.ShapeDtypeStruct(hidden.shape, BF16),
+            jax.ShapeDtypeStruct((half, model), F32),
+            jax.ShapeDtypeStruct((half, model), BF16),
+            jax.ShapeDtypeStruct((half, model), BF16),
+            jax.ShapeDtypeStruct((1, model), F32),
+        ],
+        in_specs=vmem(3) + [anywhere] * 2 + vmem(3),
+        out_specs=vmem(5),
+        scratch_shapes=[pltpu.VMEM((chunks, width, units), BF16)] * 2
+        + [dma((2 * chunks,)), pltpu.VMEM((half, model), F32), dma, dma, dma((blocks,)), dma((blocks,))]
+        + TensorSum.scratch(chunks, half, width),
+        compiler_params=pltpu.CompilerParams(
+            vmem_limit_bytes=VMEM_LIMIT, collective_id=2, has_side_effects=True
         ),
-        name="pair",
-    )(core, d_gate, d_up, w_gate, w_up, *add)
+        cost_estimate=COST,
+        name="d_middle",
+    )(hidden, d_gate, d_up, w_gate, w_up, middle, out_grad, gain)
 
 
 def rms_parts(value):
@@ -683,6 +1104,68 @@
 def rms_back(r, n, gain, c):
     gc = gain * c
     return r * (gc - n * jnp.mean(n * gc, axis=-1, keepdims=True))
+
+
+class Chain:
+    def __init__(self):
+        self.last = None
+
+    def mark(self, value):
+        self.last = value
+
+    def __call__(self, *values):
+        if self.last is None:
+            return values
+        return lax.optimization_barrier((*values, self.last))[:-1]
+
+
+class ZSum:
+    def __init__(self, part, dim, shard, planes, z_at):
+        self.part, self.dim, self.shard, self.planes, self.z_at = part, dim, shard, planes, z_at
+        self.at = 0
+        self.came = None
+
+    def term(self, j):
+        j = jnp.clip(j, 0, self.planes - 1)
+        return lax.dynamic_slice_in_dim(self.part, j * self.shard, self.shard, self.dim)
+
+    def send(self, up, down):
+        last = self.planes - 1
+        self.at += 1
+        up_pairs = [(2 * z + x, 2 * z + 2 + x) for z in range(last) for x in range(2) if z < self.at]
+        down_pairs = [
+            (2 * (last - z) + x, 2 * (last - 1 - z) + x)
+            for z in range(last)
+            for x in range(2)
+            if z < self.at
+        ]
+        self.came = lax.ppermute(up, "dp", up_pairs), lax.ppermute(down, "dp", down_pairs)
+
+    def terms(self):
+        planes, z_at, at = self.planes, self.z_at, self.at
+        return self.term(planes - 1 - at + z_at), self.term(at + 1 - planes + z_at)
+
+    def start(self):
+        self.send(*self.terms())
+
+    def step(self, chain):
+        if self.at >= self.planes - 1:
+            return
+        up, down = chain(*self.came)
+        up_term, down_term = self.terms()
+        up, down = up + up_term, down + down_term
+        chain.mark(up)
+        self.send(up, down)
+
+    def finish(self, chain):
+        if self.at == 0:
+            self.start()
+        while self.at < self.planes - 1:
+            self.step(chain)
+        up, down = chain(*self.came)
+        total = self.term(self.z_at).astype(F32) + up.astype(F32) + down.astype(F32)
+        chain.mark(total)
+        return total
 
 
 def shards(
@@ -751,47 +1234,6 @@
             core == 0, jnp.concatenate([mine, theirs], 0), jnp.concatenate([theirs, mine], 0)
         )
 
-    def sum_tensor(left, right):
-        away = dot(other_half(left), right).astype(BF16)
-        came = core_swap(away)
-        both = (dot(own_half(left), right) + came.astype(F32)).astype(BF16)
-        return both, y_swap(both)
-
-    def cut_columns(*parts):
-        keep, send = cut(x_at, core, parts, planes, shard, join)
-        came = x_swap(send)
-        return keep, join(came, core_swap(came))
-
-    def scatter_z(stack):
-        up_carry = stack(jnp.clip(planes - 1 + z_at, 0, planes - 1))
-        down_carry = stack(jnp.clip(1 - planes + z_at, 0, planes - 1))
-        for step in range(1, planes):
-            up_pairs = [
-                (2 * z + x, 2 * z + 2 + x) for z in range(planes - 1) for x in range(2) if z <= step - 1
-            ]
-            down_pairs = [
-                (2 * (planes - 1 - z) + x, 2 * (planes - 2 - z) + x)
-                for z in range(planes - 1)
-                for x in range(2)
-                if z <= step - 1
-            ]
-            up = lax.ppermute(up_carry, "dp", up_pairs)
-            down = lax.ppermute(down_carry, "dp", down_pairs)
-            if step < planes - 1:
-                up_carry = up + stack(jnp.clip(planes - step - 1 + z_at, 0, planes - 1))
-                down_carry = down + stack(jnp.clip(step + 1 - planes + z_at, 0, planes - 1))
-        return stack(z_at).astype(F32) + up.astype(F32) + down.astype(F32)
-
-    def scatter_rows(left_own, left_came, right_own, right_came):
-        part = dot(left_own, right_own, TN) + dot(left_came, right_came, TN)
-        part = part.astype(BF16)
-        return scatter_z(lambda j: lax.dynamic_slice_in_dim(part, j * shard, shard, 0))
-
-    def scatter_columns(left_own, left_came, right_own, right_came):
-        part = dot(left_own, right_own, TN) + dot(left_came, right_came, TN)
-        part = part.astype(BF16)
-        return scatter_z(lambda j: lax.dynamic_slice_in_dim(part, j * shard, shard, 1))
-
     def sum_all(value, axes):
         for axis, bit in axes:
             size = dp_size if axis == "dp" else tensor_size
@@ -829,74 +1271,70 @@
     )
     q = qkv[:, : w_query.shape[1]]
     kv = qkv[:, w_query.shape[1] :]
-    heads_b, lse, kv_all = attn_fwd(prefix[None].astype(jnp.int32), q, kv, group, dims)
-    kv_all = lax.dynamic_update_slice(kv_all, kv[None], (0, 0, 0))
-    scalars = []
-    for step in range(group_planes):
-        if step == 1:
-            there = jnp.where(plane == 0, 1, plane - 1)
-        else:
-            there = plane - step
-        mine = jnp.where(there >= 0, 2 * there + x_at, -1)
-        far = jnp.where(there >= 0, 2 * there + 1 - x_at, -1)
-        scalars.append(jnp.stack([member, prefix, mine, far]).astype(jnp.int32))
-
-    both, came = sum_tensor(heads_b, w_out)
-    d_hidden = dot(out_grad, w_down, NT)
-    og_cols, og_came = cut_columns(out_grad)
-    h_one_cols, h_one_came = cut_columns(h_one)
-    middle, h_two_half = norm_forward(core_at, both, came, tokens, norm_mlp_row)
+    prefix_at = prefix[None].astype(jnp.int32)
+    heads_b, lse, kv_all = attn_fwd(prefix_at, q, kv, group, dims)
+    chain = Chain()
+
+    away = dot(other_half(heads_b), w_out).astype(BF16)
+    came = core_swap(away)
+    both = (dot(own_half(heads_b), w_out) + came.astype(F32)).astype(BF16)
+    chain.mark(both)
+    y_came = y_swap(both)
+    (og,) = chain(out_grad)
+    og_keep, og_send = cut(x_at, core, [og], planes, shard, join)
+    og_came = x_swap(og_send)
+    chain.mark(og_keep)
+    d_hidden = dot(chain(out_grad)[0], w_down, NT)
+    chain.mark(d_hidden)
+    h_one_keep, h_one_send = cut(x_at, core, chain(h_one), planes, shard, join)
+    h_one_came = x_swap(h_one_send)
+    chain.mark(h_one_keep)
+    middle, h_two_half = norm_forward(core_at, both, *chain(y_came), tokens, norm_mlp_row)
+    chain.mark(h_two_half)
     h_two_far = core_swap(h_two_half)
-    hidden, d_gate, d_up = mlp(core_at, h_two_half, h_two_far, w_gate, w_up, d_hidden)
-
-    away = pair(core_not, d_gate, d_up, w_gate, w_up, [])
-    both = pair(core_at, d_gate, d_up, w_gate, w_up, [core_swap(away)])
-    came = y_swap(both)
-    d_middle_half, d_attn_half, norm_mlp_part = norm_back(
-        core_at, both, came, middle, out_grad, norm_mlp_row
+    og_came = join(og_came, core_swap(og_came))
+    h_one_came = join(h_one_came, core_swap(h_one_came))
+    hidden, d_gate, d_up = mlp(core_at, h_two_half, *chain(h_two_far), w_gate, w_up, d_hidden)
+    chain.mark(hidden)
+
+    hidden_came, d_middle_half, d_attn_half, d_attn_far, norm_mlp_part = d_middle_of(
+        hidden, d_gate, d_up, w_gate, w_up, middle, out_grad, norm_mlp_row
     )
-    d_attn_far = core_swap(d_attn_half)
-
-    hidden_came = x_swap(hidden)
-    w_down_grad = scatter_columns(hidden, hidden_came, og_cols, og_came)
-    h_two_cols, h_two_came = cut_columns(h_two_half, h_two_far)
-    w_gate_grad = scatter_rows(h_two_cols, h_two_came, d_gate, x_swap(d_gate))
-    w_up_grad = scatter_rows(h_two_cols, h_two_came, d_up, x_swap(d_up))
-
-    both, came = sum_tensor(hidden, w_down)
-    block_half = (middle + (both.astype(F32) + came.astype(F32))).astype(BF16)
-    block_out = join(block_half, core_swap(block_half))
-
+    chain.mark(d_attn_far)
     qx, dox = attn_prep(core_at, d_attn_half, d_attn_far, w_out, q, heads_b, lse, width)
-    dq = None
-    sums = [None] * group_planes
-    for step in reversed(range(group_planes)):
-        dq, d_own, d_far = attn_bwd(
-            scalars[step], qx, dox, kv_all, (2 * step, 2 * step + 1), dq, step == 0, dims
-        )
-        sums[step] = (d_own, x_swap(d_far))
-    earlier_pairs = [(d, d - 2) for d in range(dp_size) if plane_of(d) > 0]
-    from_first_pairs = [(d, d + 2) for d in range(dp_size) if plane_of(d) == 0]
-    came = None
-    for step in reversed(range(1, group_planes)):
-        carry = sums[step][0].astype(F32) + sums[step][1].astype(F32)
-        if came is not None:
-            carry = carry + came.astype(F32)
-        carry = carry.astype(BF16)
-        pairs = [(a, b) for a, b in earlier_pairs if plane_of(a) >= step]
-        came = lax.ppermute(carry, "dp", pairs)
-    kv_grad = sums[0][0].astype(F32) + sums[0][1].astype(F32)
-    if group_planes > 1:
-        kv_grad = kv_grad + came.astype(F32) + lax.ppermute(carry, "dp", from_first_pairs).astype(F32)
-
-    d_attn_cols, d_attn_came = cut_columns(d_attn_half, d_attn_far)
-    w_out_grad = scatter_columns(heads_b, x_swap(heads_b), d_attn_cols, d_attn_came)
-
+    chain.mark(dox)
+
+    fused = planes == group_planes and shard % 128 == 0
+    shared = [h_two_half, h_two_far, d_attn_half, d_attn_far, heads_b, d_up]
+    grads = [hidden, hidden_came, og_keep, og_came, d_gate] if fused else None
+    outs = back(prefix_at, qx, *chain(dox), kv_all, shared, grads, group, planes, shard, dims)
+    dq, kv_grad, h_two_keep, h_two_came, d_attn_keep, d_attn_came, heads_came, up_came = outs[:8]
+    chain.mark(dq)
+    if fused:
+        w_down_grad, w_gate_grad, w_out_grad = outs[8:]
+    else:
+        down_part = (dot(hidden, og_keep, TN) + dot(hidden_came, og_came, TN)).astype(BF16)
+        w_down_grad = ZSum(down_part, 1, shard, planes, z_at).finish(chain)
+        gate_part = dot(h_two_keep, d_gate, TN) + dot(h_two_came, x_swap(d_gate), TN)
+        w_gate_grad = ZSum(gate_part.astype(BF16), 0, shard, planes, z_at).finish(chain)
+        out_part = dot(heads_b, d_attn_keep, TN) + dot(heads_came, d_attn_came, TN)
+        w_out_grad = ZSum(out_part.astype(BF16), 1, shard, planes, z_at).finish(chain)
+
+    d_middle_far = core_swap(chain(d_middle_half)[0])
+    dq_b, q_gain_part = unproject(chain(dq)[0], q_raw, q_gain_row, cos, sin, 0, "unproject_q")
+    chain.mark(dq_b)
+    dq_came = x_swap(chain(dq_b)[0])
+    up_part = (dot(h_two_keep, d_up, TN) + dot(h_two_came, *chain(up_came), TN)).astype(BF16)
+    chain.mark(up_part)
+    up = ZSum(up_part, 0, shard, planes, z_at)
+    up.start()
+
+    dkv_b, k_gain_part = unproject(
+        chain(kv_grad)[0], k_raw, k_gain_row, cos, sin, kv_heads * width, "unproject_kv"
+    )
     kv_width = kv_heads * width
-    dq_b, q_gain_part = unproject(dq, q_raw, q_gain_row, cos, sin, 0, "unproject_q")
-    dkv_b, k_gain_part = unproject(kv_grad, k_raw, k_gain_row, cos, sin, kv_width, "unproject_kv")
-    w_query_grad = scatter_rows(h_one_cols, h_one_came, dq_b, x_swap(dq_b))
-    w_kv_grad = scatter_rows(h_one_cols, h_one_came, dkv_b, x_swap(dkv_b))
+    chain.mark(dkv_b)
+    dkv_came = x_swap(dkv_b)
 
     def d_h_one_part(which):
         dkv_rows = which(dkv_b)
@@ -907,22 +1345,54 @@
         )
 
     away = d_h_one_part(other_half)
+    came = core_swap(away.astype(BF16))
     mine = d_h_one_part(own_half)
+    both = (mine + came.astype(F32)).astype(BF16)
+    chain.mark(both)
+    one_y = y_swap(both)
     x_half = own_half(tokens).astype(F32)
     x_other = other_half(tokens).astype(F32)
     r_own, n_own = rms_parts(x_half)
     r_other, n_other = rms_parts(x_other)
     norm_attn_part = jnp.sum(away * n_other + mine * n_own, axis=0)
-    both = (mine + core_swap(away.astype(BF16)).astype(F32)).astype(BF16)
-    d_h_one = (both.astype(F32) + y_swap(both).astype(F32)).astype(BF16)
+
+    up.step(chain)
+    mlp_away = dot(other_half(chain(hidden)[0]), w_down).astype(BF16)
+    mlp_came = core_swap(mlp_away)
+    chain.mark(mlp_away)
+    mlp_both = (dot(own_half(chain(hidden)[0]), w_down) + mlp_came.astype(F32)).astype(BF16)
+    chain.mark(mlp_both)
+    mlp_y = y_swap(mlp_both)
+    (dq_came,) = chain(dq_came)
+    q_part = (dot(h_one_keep, dq_b, TN) + dot(h_one_came, dq_came, TN)).astype(BF16)
+    chain.mark(q_part)
+    query = ZSum(q_part, 0, shard, planes, z_at)
+    query.start()
+    (dkv_came,) = chain(dkv_came)
+    kv_part = (dot(h_one_keep, dkv_b, TN) + dot(h_one_came, dkv_came, TN)).astype(BF16)
+    chain.mark(kv_part)
+    key_value = ZSum(kv_part, 0, shard, planes, z_at)
+    key_value.start()
+    up.step(chain)
+    query.step(chain)
+    key_value.step(chain)
+    w_up_grad = up.finish(chain)
+    query.step(chain)
+    key_value.step(chain)
+
+    d_h_one = (both.astype(F32) + one_y.astype(F32)).astype(BF16)
     d_h_one_other = core_swap(d_h_one)
-    d_middle_other = core_swap(d_middle_half)
     grad_own = d_middle_half + rms_back(r_own, n_own, norm_attn_row, d_h_one.astype(F32))
-    grad_other = d_middle_other + rms_back(r_other, n_other, norm_attn_row, d_h_one_other.astype(F32))
+    grad_other = d_middle_far + rms_back(r_other, n_other, norm_attn_row, d_h_one_other.astype(F32))
     tokens_grad = join(grad_own, grad_other)
-
-    norm_mlp_sum = sum_all(norm_mlp_part[0], [("tensor", 1)] + dp_bits)
+    block_half = (middle + (mlp_both.astype(F32) + mlp_y.astype(F32))).astype(BF16)
+    block_out = join(block_half, core_swap(block_half))
+    w_query_grad = query.finish(chain)
+    w_kv_grad = key_value.finish(chain)
+
     small = jnp.concatenate([norm_attn_part, q_gain_part[0], k_gain_part[0]])
+    norm_mlp_part, small = chain(norm_mlp_part[0], small)
+    norm_mlp_sum = sum_all(norm_mlp_part, [("tensor", 1)] + dp_bits)
     small = sum_all(small, [("tensor", 1), ("tensor", 2)] + dp_bits)
     norm_mlp_grad = lax.dynamic_slice_in_dim(norm_mlp_sum, device * shard, shard, 0)
     norm_attn_grad = lax.dynamic_slice_in_dim(small, device * shard, shard, 0)

time: 671 us -> 567 us (0.85)
  Pallas kernels: 152 us -> 327 us
  waiting for transfers between devices: 229 us -> 74.9 us
  starting transfers between devices: 160 us -> 70.5 us
  matrix products: 63.4 us -> 44.2 us
  other arithmetic: 39.1 us -> 27.3 us
    pallas_call x7 -> x2, Pallas kernels: 65.7 us -> 246 us  [the longest x1 202 us: back(): pl.pallas_call(functools.partial(back_kernel, group=group, planes=planes,...]
    ppermute x14 -> x4, waiting for transfers between devices: 121 us -> 10.5 us  [x_swap(): return lax.ppermute(value, 'dp', x_pairs)]
    ppermute x40 -> x18, starting transfers between devices: 106 us -> 48.4 us  [the longest x9 39.9 us: send(): lax.ppermute(up, 'dp', up_pairs)]
    ppermute x40 -> x18, waiting for transfers between devices: 63.1 us -> 22.9 us  [the longest x9 20.4 us: send(): lax.ppermute(up, 'dp', up_pairs)]
    ppermute x9, starting transfers between devices: 33.7 us -> 11 us  [sum_all(): lax.ppermute(value, axis, [(d, d ^ bit) for d in range(size)])]
    dot_general x23 -> x17, matrix products: 63.4 us -> 44.2 us  [dot(): return lax.dot_general(left, right, dims, preferred_element_type=F32)]
    add x19 -> x9, other arithmetic: 21.3 us -> 8.72 us  [the longest x3 4.55 us: finish(): total = self.term(self.z_at).astype(F32) + up.astype(F32) + down.astype(F32)]
    ppermute x14 -> x4, starting transfers between devices: 12.5 us -> 3.52 us  [x_swap(): return lax.ppermute(value, 'dp', x_pairs)]
  transfers between devices with their start and end apart: 80 -> 43, of which waited for: 29 -> 12; matrix products, arithmetic and copies ran while one was open for 15% -> 10% of each run, Pallas kernels for 16% -> 2%
where the time goes in v3:
time: 567 us; the launch traced here: 558 us
  Pallas kernels  327 us (58%)
  waiting for transfers between devices  74.9 us (13%)
  starting transfers between devices  70.5 us (12%)
  matrix products  44.2 us (8%)
  other arithmetic  27.3 us (5%)
  local copies, waits for them, and re-layouts  12.3 us (2%)
    pallas_call x1, Pallas kernels, back(): pl.pallas_call(functools.partial(back_kernel, group=group, planes=planes,...  202 us
    dot_general x17, matrix products, dot(): return lax.dot_general(left, right, dims, preferred_element_type=F32)  44.2 us
    pallas_call x1, Pallas kernels, d_middle_of(): pl.pallas_call(functools.partial(d_middle_kernel, blocks=blocks), out_sha...  43.8 us
    ppermute x9, starting transfers between devices, send(): lax.ppermute(up, 'dp', up_pairs)  39.9 us
    pallas_call x1, Pallas kernels, attn_fwd(): pl.pallas_call(functools.partial(attn_fwd_kernel, group=group, kv_heads=k...  35.5 us
    ppermute x3, waiting for transfers between devices, y_swap(): return lax.ppermute(value, 'tensor', y_pairs)  31.8 us
    ppermute x9, waiting for transfers between devices, send(): lax.ppermute(up, 'dp', up_pairs)  20.4 us
    pallas_call x1, Pallas kernels, mlp(): pl.pallas_call(mlp_kernel, out_shape=[jax.ShapeDtypeStruct((2 * half, uni...  13.9 us
  transfers between devices with their start and end apart: 43, of which 12 were waited for; matrix products, arithmetic and copies ran while one was open for 10% of the time, Pallas kernels for 2%

profile of v3, /device:TPU:0, one launch (start us, length us, event | category | flops | bytes accessed | tf_op | source)
XLA Modules:
  0.0 558.1 jit_solution(10078914943272564949)
XLA Ops:
  2.7 8.2 %project.1 = (bf16[512,2048]{1,0:T(8,128)(2,1)}, bf16[512,1024]{1,0:T(8,128)(2,1)}, f32[512,512]{1,0:T(8,128)}, f32[512,256]{1,0:T(8,128)}) custom-call(bf16[512,2048]{1,0:T(8,128)(2,1)} %x_ref.3, f32[1,2048]{1,0:T(1,128)} %bitcast.32, bf16[2048,512]{1,0:T(8,128)(2,1)} %refs_0_.1, bf16[2048,256]{1,0:T(8,128)(2,1)} %refs_1_.1, bf16[2048,256]{1,0:T(8,128)(2,1)} %refs_2_.1, ...), custom_call_target="tpu_custom_call" | custom-call | flops 1000 | bytes 1000 | tf_op jit(solution)/shard_map/project/pallas_call | solution.py:214
  13.9 35.5 %attn_fwd.1 = (bf16[512,512]{1,0:T(8,128)(2,1)}, f32[512,512]{1,0:T(8,128)}, bf16[8,512,512]{2,1,0:T(8,128)(2,1)}) custom-call(s32[1]{0:T(128)S(6)} %select_n.110.prefix_ref.refs_0_, bf16[512,512]{1,0:T(8,128)(2,1)} %get-tuple-element.177.q_ref, bf16[512,512]{1,0:T(8,128)(2,1)} %get-tuple-element.176.kv_ref), custom_call_target="tpu_custom_call" | custom-call | flops 1000 | bytes 1000 | tf_op jit(solution)/shard_map/attn_fwd/pallas_call | solution.py:461
  52.1 3.0 collective-permute-done
  55.1 2.9 add_convert_fusion.7.both_ref
  60.1 3.0 cut.2
  64.6 7.9 %fusion.55.d_ref = f32[512,1536]{1,0:T(8,128)} fusion(bf16[512,2048]{1,0:T(8,128)(2,1)S(1)} %copy-done.8, bf16[1536,2048]{1,0:T(8,128)(2,1)} %param.25), kind=kOutput, calls=%fused_computation.107 | convolution fusion | flops 3221225472 | bytes 11534336 | tf_op jit(solution)/shard_map/dot_general | solution.py:27
  72.5 3.0 cut.3
  75.5 8.0 %collective-permute-done.1.y_ref = bf16[256,2048]{1,0:T(8,128)(2,1)S(1)} collective-permute-done((bf16[256,2048]{1,0:T(8,128)(2,1)}, bf16[256,2048]{1,0:T(8,128)(2,1)S(1)}, u32[]{:S(2)}, u32[]{:S(2)}) %collective-permute-start.1) | collective-permute-done | bytes 1048608 | tf_op jit(solution)/shard_map/ppermute | solution.py:1218
  84.4 4.4 norm_forward.1
  89.3 3.1 collective-permute-done.4
  96.1 13.9 %mlp.1 = (bf16[512,1536]{1,0:T(8,128)(2,1)}, bf16[512,1536]{1,0:T(8,128)(2,1)}, bf16[512,1536]{1,0:T(8,128)(2,1)}) custom-call(s32[1]{0:T(128)} %bitcast.core_ref, bf16[256,2048]{1,0:T(8,128)(2,1)} %get-tuple-element.92.own_ref.refs_4_, bf16[256,2048]{1,0:T(8,128)(2,1)} %copy-done.15, bf16[2048,1536]{1,0:T(8,128)(2,1)} %w_gate_ref.1, ...), custom_call_target="tpu_custom_call" | custom-call | flops 1000 | bytes 1000 | tf_op jit(solution)/shard_map/mlp/pallas_call | solution.py:978
  110.0 43.8 %d_middle.1 = (bf16[512,1536]{1,0:T(8,128)(2,1)}, f32[256,2048]{1,0:T(8,128)}, bf16[256,2048]{1,0:T(8,128)(2,1)}, bf16[256,2048]{1,0:T(8,128)(2,1)}, f32[1,2048]{1,0:T(1,128)}) custom-call(bf16[512,1536]{1,0:T(8,128)(2,1)} %get-tuple-element.119.hid_ref.refs_10_, bf16[512,1536]{1,0:T(8,128)(2,1)} %get-tuple-element.95.d_gate_ref.refs_14_, ...), custom_call_target="tpu_custom_call" | custom-call | flops 1000 | bytes 1000 | tf_op jit(solution)/shard_map/d_middle/pallas_call | solution.py:1077
  153.9 5.8 %attn_prep.1 = (bf16[4,512,256]{2,1,0:T(8,128)(2,1)}, bf16[4,512,256]{2,1,0:T(8,128)(2,1)}) custom-call(s32[1]{0:T(128)} %bitcast.core_ref, bf16[256,2048]{1,0:T(8,128)(2,1)} %get-tuple-element.97.own_ref.refs_6_, bf16[256,2048]{1,0:T(8,128)(2,1)} %get-tuple-element.98.far_ref.refs_7_, bf16[512,2048]{1,0:T(8,128)(2,1)} %w_ref.1, ...), custom_call_target="tpu_custom_call" | custom-call | flops 1000 | bytes 1000 | tf_op jit(solution)/shard_map/attn_prep/pallas_call | solution.py:521
  159.6 202.3 %back.1 = (f32[512,512]{1,0:T(8,128)}, f32[512,512]{1,0:T(8,128)}, bf16[512,1024]{1,0:T(8,128)(2,1)}, bf16[512,1024]{1,0:T(8,128)(2,1)}, bf16[512,1024]{1,0:T(8,...) custom-call(s32[1]{0:T(128)S(6)} %select_n.110.prefix_ref.refs_0_, ...), custom_call_target="tpu_custom_call" | custom-call | flops 1000 | bytes 1000 | tf_op jit(solution)/shard_map/back/pallas_call | solution.py:859
  362.0 3.7 unproject_q.1
  367.6 3.5 add_convert_fusion
  371.1 3.0 unproject_kv.1
  385.3 4.3 add_convert_fusion.6
  389.6 10.9 %collective-permute-done.5 = bf16[256,1536]{1,0:T(8,128)(2,1)S(1)} collective-permute-done((bf16[256,1536]{1,0:T(8,128)(2,1)S(1)}, bf16[256,1536]{1,0:T(8,128)(2,1)S(1)}, u32[]{:S(2)}, u32[]{:S(2)}) %collective-permute-start.5) | collective-permute-done | bytes 786464 | tf_op jit(solution)/shard_map/ppermute | solution.py:1142
  410.1 4.4 collective-permute-start.22
  415.5 5.8 %add_convert_fusion.5 = bf16[256,2048]{1,0:T(8,128)(2,1)} fusion(bf16[256,2048]{1,0:T(8,128)(2,1)} %collective-permute-done.8, bf16[1536,2048]{1,0:T(8,128)(2,1)} %param.25, bf16[512,1536]{1,0:T(8,128)(2,1)S(1)} %copy-done.11, s32[]{:T(128)S(6)} %select_n.112), kind=kOutput, calls=%fused_computation.37 | convolution fusion | flops 1612185600 | bytes 9175044 | tf_op jit(solution)/shard_map/dot_general | solution.py:27
  421.3 10.4 %collective-permute-done.17 = bf16[512,512]{1,0:T(8,128)(2,1)S(1)} collective-permute-done((bf16[512,512]{1,0:T(8,128)(2,1)S(1)}, bf16[512,512]{1,0:T(8,128)(2,1)S(1)}, u32[]{:S(2)}, u32[]{:S(2)}) %collective-permute-start.17) | collective-permute-done | bytes 524320 | tf_op jit(solution)/shard_map/ppermute | solution.py:1221
  438.6 4.4 collective-permute-start.20
  446.2 10.8 %collective-permute-done.11 = bf16[256,2048]{1,0:T(8,128)(2,1)S(1)} collective-permute-done((bf16[256,2048]{1,0:T(8,128)(2,1)S(1)}, bf16[256,2048]{1,0:T(8,128)(2,1)S(1)}, u32[]{:S(2)}, u32[]{:S(2)}) %collective-permute-start.11) | collective-permute-done | bytes 1048608 | tf_op jit(solution)/shard_map/ppermute | solution.py:1218
  457.0 4.4 collective-permute-start.28
  463.4 5.6 %collective-permute-start.26 = (bf16[256,512]{1,0:T(8,128)(2,1)S(1)}, bf16[256,512]{1,0:T(8,128)(2,1)S(1)}, u32[]{:S(2)}, u32[]{:S(2)}) collective-permute-start(bf16[256,512]{1,0:T(8,128)(2,1)S(1)} %get-tuple-element.169), channel_id=1, source_target_pairs={{0,8},{4,12},{8,16},{12,20},{1,9},{5,13},{9,17},{13,21},{2,10},{6,... | collective-permute-start | bytes 786440 | tf_op jit(solution)/shard_map/ppermute | solution.py:1142
  469.9 9.5 %collective-permute-done.28 = bf16[256,1536]{1,0:T(8,128)(2,1)S(1)} collective-permute-done((bf16[256,1536]{1,0:T(8,128)(2,1)S(1)}, bf16[256,1536]{1,0:T(8,128)(2,1)S(1)}, u32[]{:S(2)}, u32[]{:S(2)}) %collective-permute-start.28) | collective-permute-done | bytes 786464 | tf_op jit(solution)/shard_map/ppermute | solution.py:1142
  479.4 5.1 collective-permute-start.24
  487.5 8.6 %collective-permute-start.32 = (bf16[256,512]{1,0:T(8,128)(2,1)}, bf16[256,512]{1,0:T(8,128)(2,1)}, u32[]{:S(2)}, u32[]{:S(2)}) collective-permute-start(bf16[256,512]{1,0:T(8,128)(2,1)} %get-tuple-element.165), channel_id=1, source_target_pairs={{0,8},{4,12},{8,16},{12,20},{16,24},{20,28},{1,9},{5,13},{9,17},{1... | collective-permute-start | bytes 786440 | tf_op jit(solution)/shard_map/ppermute | solution.py:1142
  498.3 4.6 collective-permute-start.30
  511.5 4.0 fusion.8
  517.3 13.0 %collective-permute-done.9 = bf16[256,2048]{1,0:T(8,128)(2,1)S(1)} collective-permute-done((bf16[256,2048]{1,0:T(8,128)(2,1)}, bf16[256,2048]{1,0:T(8,128)(2,1)S(1)}, u32[]{:S(2)}, u32[]{:S(2)}) %collective-permute-start.9) | collective-permute-done | bytes 1048608 | tf_op jit(solution)/shard_map/ppermute | solution.py:1218
  (210 shorter events, 94.9 us)
Async XLA Ops:
  58.0 25.4 %collective-permute-start.1 = (bf16[256,2048]{1,0:T(8,128)(2,1)}, bf16[256,2048]{1,0:T(8,128)(2,1)S(1)}, u32[]{:S(2)}, u32[]{:S(2)}) collective-permute-start(bf16[256,2048]{1,0:T(8,128)(2,1)} %add_convert_fusion.7.both_ref), channel_id=1, source_target_pairs={{0,2},{1,3},{2,0},{3,1},{4,6},{5,7},{6,4},{7,5},{8,10},{9,11},{10,... | collective-permute-start | bytes 3145736 | tf_op jit(solution)/shard_map/ppermute | solution.py:1218
  63.1 25.7 %collective-permute-start.3 = (bf16[256,1024]{1,0:T(8,128)(2,1)}, bf16[256,1024]{1,0:T(8,128)(2,1)}, u32[]{:S(2)}, u32[]{:S(2)}) collective-permute-start(bf16[256,1024]{1,0:T(8,128)(2,1)} %get-tuple-element.104), channel_id=1, source_target_pairs={{0,4},{4,0},{8,12},{12,8},{16,20},{20,16},{24,28},{28,24},{1,5},{5... | collective-permute-start | bytes 1572872 | tf_op jit(solution)/shard_map/ppermute | solution.py:1221
  379.8 25.8 %collective-permute-start.14 = (bf16[256,1024]{1,0:T(8,128)(2,1)}, bf16[256,1024]{1,0:T(8,128)(2,1)}, u32[]{:S(2)}, u32[]{:S(2)}) collective-permute-start(bf16[256,1024]{1,0:T(8,128)(2,1)} %get-tuple-element.125), channel_id=1, source_target_pairs={{0,4},{4,0},{8,12},{12,8},{16,20},{20,16},{24,28},{28,24},{1,5},{5... | collective-permute-start | bytes 1572872 | tf_op jit(solution)/shard_map/ppermute | solution.py:1221
  381.4 19.2 %collective-permute-start.5 = (bf16[256,1536]{1,0:T(8,128)(2,1)S(1)}, bf16[256,1536]{1,0:T(8,128)(2,1)S(1)}, u32[]{:S(2)}, u32[]{:S(2)}) collective-permute-start(bf16[256,1536]{1,0:T(8,128)(2,1)S(1)} %get-tuple-element.161), channel_id=1, source_target_pairs={{0,8},{4,12},{1,9},{5,13},{2,10},{6,14},{3,11},{7,15}} | collective-permute-start | bytes 2359304 | tf_op jit(solution)/shard_map/ppermute | solution.py:1142
  382.9 17.6 %collective-permute-start.6 = (bf16[256,1536]{1,0:T(8,128)(2,1)S(1)}, bf16[256,1536]{1,0:T(8,128)(2,1)S(1)}, u32[]{:S(2)}, u32[]{:S(2)}) collective-permute-start(bf16[256,1536]{1,0:T(8,128)(2,1)S(1)} %get-tuple-element.160), channel_id=1, source_target_pairs={{24,16},{28,20},{25,17},{29,21},{26,18},{30,22},{27,19},{31,23}} | collective-permute-start | bytes 2359304 | tf_op jit(solution)/shard_map/ppermute | solution.py:1142
  405.1 9.5 %collective-permute-start.8 = (bf16[256,2048]{1,0:T(8,128)(2,1)}, bf16[256,2048]{1,0:T(8,128)(2,1)}, u32[]{:S(2)}, u32[]{:S(2)}) collective-permute-start(bf16[256,2048]{1,0:T(8,128)(2,1)} %convolution_convert_fusion.1), channel_id=1, source_target_pairs={{0,1},{1,0},{2,3},{3,2},{4,5},{5,4},{6,7},{7,6},{8,9},{9,8},{10,11... | collective-permute-start | bytes 3145736 | tf_op jit(solution)/shard_map/ppermute | solution.py:1215
  405.6 28.4 %collective-permute-start.15 = (bf16[256,1024]{1,0:T(8,128)(2,1)}, bf16[256,1024]{1,0:T(8,128)(2,1)S(1)}, u32[]{:S(2)}, u32[]{:S(2)}) collective-permute-start(bf16[256,1024]{1,0:T(8,128)(2,1)} %collective-permute-done.14), channel_id=1, source_target_pairs={{0,1},{1,0},{2,3},{3,2},{4,5},{5,4},{6,7},{7,6},{8,9},{9,8},{10,11... | collective-permute-start | bytes 1572872 | tf_op jit(solution)/shard_map/ppermute | solution.py:1215
  406.2 29.9 %collective-permute-start.16 = (bf16[512,512]{1,0:T(8,128)(2,1)S(1)}, bf16[512,512]{1,0:T(8,128)(2,1)S(1)}, u32[]{:S(2)}, u32[]{:S(2)}) collective-permute-start(bf16[512,512]{1,0:T(8,128)(2,1)S(1)} %copy-done.20), channel_id=1, source_target_pairs={{0,4},{4,0},{8,12},{12,8},{16,20},{20,16},{24,28},{28,24},{1,5},{5... | collective-permute-start | bytes 1572872 | tf_op jit(solution)/shard_map/ppermute | solution.py:1221
  407.9 23.8 %collective-permute-start.17 = (bf16[512,512]{1,0:T(8,128)(2,1)S(1)}, bf16[512,512]{1,0:T(8,128)(2,1)S(1)}, u32[]{:S(2)}, u32[]{:S(2)}) collective-permute-start(bf16[512,512]{1,0:T(8,128)(2,1)S(1)} %copy-done.23), channel_id=1, source_target_pairs={{0,4},{4,0},{8,12},{12,8},{16,20},{20,16},{24,28},{28,24},{1,5},{5... | collective-permute-start | bytes 1572872 | tf_op jit(solution)/shard_map/ppermute | solution.py:1221
  410.1 28.4 %collective-permute-start.22 = (bf16[256,1536]{1,0:T(8,128)(2,1)S(1)}, bf16[256,1536]{1,0:T(8,128)(2,1)S(1)}, u32[]{:S(2)}, u32[]{:S(2)}) collective-permute-start(bf16[256,1536]{1,0:T(8,128)(2,1)S(1)} %copy-done.30), channel_id=1, source_target_pairs={{0,8},{4,12},{8,16},{12,20},{1,9},{5,13},{9,17},{13,21},{2,10},{6,... | collective-permute-start | bytes 2359304 | tf_op jit(solution)/shard_map/ppermute | solution.py:1142
  414.6 24.0 %collective-permute-start.23 = (bf16[256,1536]{1,0:T(8,128)(2,1)S(1)}, bf16[256,1536]{1,0:T(8,128)(2,1)S(1)}, u32[]{:S(2)}, u32[]{:S(2)}) collective-permute-start(bf16[256,1536]{1,0:T(8,128)(2,1)S(1)} %copy-done.29), channel_id=1, source_target_pairs={{24,16},{28,20},{16,8},{20,12},{25,17},{29,21},{17,9},{21,13},{26,... | collective-permute-start | bytes 2359304 | tf_op jit(solution)/shard_map/ppermute | solution.py:1142
  431.7 25.3 %collective-permute-start.11 = (bf16[256,2048]{1,0:T(8,128)(2,1)S(1)}, bf16[256,2048]{1,0:T(8,128)(2,1)S(1)}, u32[]{:S(2)}, u32[]{:S(2)}) collective-permute-start(bf16[256,2048]{1,0:T(8,128)(2,1)S(1)} %copy-done.16), channel_id=1, source_target_pairs={{0,2},{1,3},{2,0},{3,1},{4,6},{5,7},{6,4},{7,5},{8,10},{9,11},{10,... | collective-permute-start | bytes 3145736 | tf_op jit(solution)/shard_map/ppermute | solution.py:1218
  438.6 22.8 %collective-permute-start.20 = (bf16[256,512]{1,0:T(8,128)(2,1)S(1)}, bf16[256,512]{1,0:T(8,128)(2,1)S(1)}, u32[]{:S(2)}, u32[]{:S(2)}) collective-permute-start(bf16[256,512]{1,0:T(8,128)(2,1)S(1)} %get-tuple-element.173), channel_id=1, source_target_pairs={{0,8},{4,12},{1,9},{5,13},{2,10},{6,14},{3,11},{7,15}} | collective-permute-start | bytes 786440 | tf_op jit(solution)/shard_map/ppermute | solution.py:1142
  443.0 20.1 %collective-permute-start.21 = (bf16[256,512]{1,0:T(8,128)(2,1)S(1)}, bf16[256,512]{1,0:T(8,128)(2,1)S(1)}, u32[]{:S(2)}, u32[]{:S(2)}) collective-permute-start(bf16[256,512]{1,0:T(8,128)(2,1)S(1)} %get-tuple-element.172), channel_id=1, source_target_pairs={{24,16},{28,20},{25,17},{29,21},{26,18},{30,22},{27,19},{31,23}} | collective-permute-start | bytes 786440 | tf_op jit(solution)/shard_map/ppermute | solution.py:1142
  443.8 19.6 %collective-permute-start.18 = (bf16[256,512]{1,0:T(8,128)(2,1)S(1)}, bf16[256,512]{1,0:T(8,128)(2,1)S(1)}, u32[]{:S(2)}, u32[]{:S(2)}) collective-permute-start(bf16[256,512]{1,0:T(8,128)(2,1)S(1)} %get-tuple-element.175), channel_id=1, source_target_pairs={{0,8},{4,12},{1,9},{5,13},{2,10},{6,14},{3,11},{7,15}} | collective-permute-start | bytes 786440 | tf_op jit(solution)/shard_map/ppermute | solution.py:1142
  445.1 24.0 %collective-permute-start.19 = (bf16[256,512]{1,0:T(8,128)(2,1)S(1)}, bf16[256,512]{1,0:T(8,128)(2,1)S(1)}, u32[]{:S(2)}, u32[]{:S(2)}) collective-permute-start(bf16[256,512]{1,0:T(8,128)(2,1)S(1)} %get-tuple-element.174), channel_id=1, source_target_pairs={{24,16},{28,20},{25,17},{29,21},{26,18},{30,22},{27,19},{31,23}} | collective-permute-start | bytes 786440 | tf_op jit(solution)/shard_map/ppermute | solution.py:1142
  457.0 22.4 %collective-permute-start.28 = (bf16[256,1536]{1,0:T(8,128)(2,1)S(1)}, bf16[256,1536]{1,0:T(8,128)(2,1)S(1)}, u32[]{:S(2)}, u32[]{:S(2)}) collective-permute-start(bf16[256,1536]{1,0:T(8,128)(2,1)S(1)} %get-tuple-element.157), channel_id=1, source_target_pairs={{0,8},{4,12},{8,16},{12,20},{16,24},{20,28},{1,9},{5,13},{9,17},{1... | collective-permute-start | bytes 2359304 | tf_op jit(solution)/shard_map/ppermute | solution.py:1142
  461.4 23.0 %collective-permute-start.29 = (bf16[256,1536]{1,0:T(8,128)(2,1)S(1)}, bf16[256,1536]{1,0:T(8,128)(2,1)S(1)}, u32[]{:S(2)}, u32[]{:S(2)}) collective-permute-start(bf16[256,1536]{1,0:T(8,128)(2,1)S(1)} %get-tuple-element.156), channel_id=1, source_target_pairs={{24,16},{28,20},{16,8},{20,12},{8,0},{12,4},{25,17},{29,21},{17,9}... | collective-permute-start | bytes 2359304 | tf_op jit(solution)/shard_map/ppermute | solution.py:1142
  463.2 48.3 %collective-permute-start.13 = (bf16[256,2048]{1,0:T(8,128)(2,1)S(1)}, bf16[256,2048]{1,0:T(8,128)(2,1)}, u32[]{:S(2)}, u32[]{:S(2)}) collective-permute-start(bf16[256,2048]{1,0:T(8,128)(2,1)S(1)} %add_convert_fusion.3), channel_id=1, source_target_pairs={{0,1},{1,0},{2,3},{3,2},{4,5},{5,4},{6,7},{7,6},{8,9},{9,8},{10,11... | collective-permute-start | bytes 3145736 | tf_op jit(solution)/shard_map/ppermute | solution.py:1215
  463.4 23.2 %collective-permute-start.26 = (bf16[256,512]{1,0:T(8,128)(2,1)S(1)}, bf16[256,512]{1,0:T(8,128)(2,1)S(1)}, u32[]{:S(2)}, u32[]{:S(2)}) collective-permute-start(bf16[256,512]{1,0:T(8,128)(2,1)S(1)} %get-tuple-element.169), channel_id=1, source_target_pairs={{0,8},{4,12},{8,16},{12,20},{1,9},{5,13},{9,17},{13,21},{2,10},{6,... | collective-permute-start | bytes 786440 | tf_op jit(solution)/shard_map/ppermute | solution.py:1142
  469.1 17.5 %collective-permute-start.27 = (bf16[256,512]{1,0:T(8,128)(2,1)S(1)}, bf16[256,512]{1,0:T(8,128)(2,1)S(1)}, u32[]{:S(2)}, u32[]{:S(2)}) collective-permute-start(bf16[256,512]{1,0:T(8,128)(2,1)S(1)} %get-tuple-element.168), channel_id=1, source_target_pairs={{24,16},{28,20},{16,8},{20,12},{25,17},{29,21},{17,9},{21,13},{26,... | collective-permute-start | bytes 786440 | tf_op jit(solution)/shard_map/ppermute | solution.py:1142
  479.4 16.7 %collective-permute-start.24 = (bf16[256,512]{1,0:T(8,128)(2,1)S(1)}, bf16[256,512]{1,0:T(8,128)(2,1)S(1)}, u32[]{:S(2)}, u32[]{:S(2)}) collective-permute-start(bf16[256,512]{1,0:T(8,128)(2,1)S(1)} %get-tuple-element.171), channel_id=1, source_target_pairs={{0,8},{4,12},{8,16},{12,20},{1,9},{5,13},{9,17},{13,21},{2,10},{6,... | collective-permute-start | bytes 786440 | tf_op jit(solution)/shard_map/ppermute | solution.py:1142
  484.4 11.6 %collective-permute-start.25 = (bf16[256,512]{1,0:T(8,128)(2,1)S(1)}, bf16[256,512]{1,0:T(8,128)(2,1)S(1)}, u32[]{:S(2)}, u32[]{:S(2)}) collective-permute-start(bf16[256,512]{1,0:T(8,128)(2,1)S(1)} %get-tuple-element.170), channel_id=1, source_target_pairs={{24,16},{28,20},{16,8},{20,12},{25,17},{29,21},{17,9},{21,13},{26,... | collective-permute-start | bytes 786440 | tf_op jit(solution)/shard_map/ppermute | solution.py:1142
  487.5 16.9 %collective-permute-start.32 = (bf16[256,512]{1,0:T(8,128)(2,1)}, bf16[256,512]{1,0:T(8,128)(2,1)}, u32[]{:S(2)}, u32[]{:S(2)}) collective-permute-start(bf16[256,512]{1,0:T(8,128)(2,1)} %get-tuple-element.165), channel_id=1, source_target_pairs={{0,8},{4,12},{8,16},{12,20},{16,24},{20,28},{1,9},{5,13},{9,17},{1... | collective-permute-start | bytes 786440 | tf_op jit(solution)/shard_map/ppermute | solution.py:1142
  496.1 10.1 %collective-permute-start.33 = (bf16[256,512]{1,0:T(8,128)(2,1)}, bf16[256,512]{1,0:T(8,128)(2,1)}, u32[]{:S(2)}, u32[]{:S(2)}) collective-permute-start(bf16[256,512]{1,0:T(8,128)(2,1)} %get-tuple-element.164), channel_id=1, source_target_pairs={{24,16},{28,20},{16,8},{20,12},{8,0},{12,4},{25,17},{29,21},{17,9}... | collective-permute-start | bytes 786440 | tf_op jit(solution)/shard_map/ppermute | solution.py:1142
  498.3 12.4 %collective-permute-start.30 = (bf16[256,512]{1,0:T(8,128)(2,1)}, bf16[256,512]{1,0:T(8,128)(2,1)S(1)}, u32[]{:S(2)}, u32[]{:S(2)}) collective-permute-start(bf16[256,512]{1,0:T(8,128)(2,1)} %get-tuple-element.167), channel_id=1, source_target_pairs={{0,8},{4,12},{8,16},{12,20},{16,24},{20,28},{1,9},{5,13},{9,17},{1... | collective-permute-start | bytes 786440 | tf_op jit(solution)/shard_map/ppermute | solution.py:1142
  502.9 8.6 %collective-permute-start.31 = (bf16[256,512]{1,0:T(8,128)(2,1)}, bf16[256,512]{1,0:T(8,128)(2,1)}, u32[]{:S(2)}, u32[]{:S(2)}) collective-permute-start(bf16[256,512]{1,0:T(8,128)(2,1)} %get-tuple-element.166), channel_id=1, source_target_pairs={{24,16},{28,20},{16,8},{20,12},{8,0},{12,4},{25,17},{29,21},{17,9}... | collective-permute-start | bytes 786440 | tf_op jit(solution)/shard_map/ppermute | solution.py:1142
  504.4 28.7 %collective-permute-start.12 = (f32[256,2048]{1,0:T(8,128)}, f32[256,2048]{1,0:T(8,128)S(1)}, u32[]{:S(2)}, u32[]{:S(2)}) collective-permute-start(f32[256,2048]{1,0:T(8,128)} %get-tuple-element.121), channel_id=1, source_target_pairs={{0,1},{1,0},{2,3},{3,2},{4,5},{5,4},{6,7},{7,6},{8,9},{9,8},{10,11... | collective-permute-start | bytes 6291464 | tf_op jit(solution)/shard_map/ppermute | solution.py:1215
  506.2 24.1 %collective-permute-start.9 = (bf16[256,2048]{1,0:T(8,128)(2,1)}, bf16[256,2048]{1,0:T(8,128)(2,1)S(1)}, u32[]{:S(2)}, u32[]{:S(2)}) collective-permute-start(bf16[256,2048]{1,0:T(8,128)(2,1)} %add_convert_fusion.5), channel_id=1, source_target_pairs={{0,2},{1,3},{2,0},{3,1},{4,6},{5,7},{6,4},{7,5},{8,10},{9,11},{10,... | collective-permute-start | bytes 3145736 | tf_op jit(solution)/shard_map/ppermute | solution.py:1218
  516.7 14.2 %collective-permute-start.39 = (f32[2048]{0:T(1024)S(1)}, f32[2048]{0:T(1024)S(1)}, u32[]{:S(2)}, u32[]{:S(2)}) collective-permute-start(f32[2048]{0:T(1024)S(1)} %bitcast.35), channel_id=1, source_target_pairs={{0,1},{1,0},{2,3},{3,2},{4,5},{5,4},{6,7},{7,6},{8,9},{9,8},{10,11... | collective-permute-start | bytes 24584 | tf_op jit(solution)/shard_map/ppermute | solution.py:1240
  516.8 15.3 %collective-permute-start.34 = (f32[2304]{0:T(1024)S(1)}, f32[2304]{0:T(1024)S(1)}, u32[]{:S(2)}, u32[]{:S(2)}) collective-permute-start(f32[2304]{0:T(1024)S(1)} %pad_maximum_fusion.2), channel_id=1, source_target_pairs={{0,1},{1,0},{2,3},{3,2},{4,5},{5,4},{6,7},{7,6},{8,9},{9,8},{10,11... | collective-permute-start | bytes 27656 | tf_op jit(solution)/shard_map/ppermute | solution.py:1240
  530.8 21.6 %collective-permute-start.10 = (bf16[256,2048]{1,0:T(8,128)(2,1)S(1)}, bf16[256,2048]{1,0:T(8,128)(2,1)S(1)}, u32[]{:S(2)}, u32[]{:S(2)}) collective-permute-start(bf16[256,2048]{1,0:T(8,128)(2,1)S(1)} %add_convert_fusion.4), channel_id=1, source_target_pairs={{0,1},{1,0},{2,3},{3,2},{4,5},{5,4},{6,7},{7,6},{8,9},{9,8},{10,11... | collective-permute-start | bytes 3145736 | tf_op jit(solution)/shard_map/ppermute | solution.py:1215
  (52 other events, 445.9 us)

commit v4 on v3

--- a/solution.py
+++ b/solution.py
@@ -126,20 +126,115 @@
         self.over_core().wait_send()
 
 
+class LineSum:
+    def __init__(self, scratch, device, plane, planes):
+        self.stack, self.came = scratch[:2]
+        self.sems = scratch[2:]
+        self.device, self.plane, self.planes = device, plane, planes
+
+    @staticmethod
+    def scratch(planes, shape):
+        return [pltpu.VMEM((n,) + shape, BF16) for n in (planes, planes + 1)] + [
+            pltpu.SemaphoreType.DMA((planes,))
+        ] * 4
+
+    def up(self, j):
+        s = self.sems
+        peer = {"dp": self.device + 2}
+        return remote(self.stack.at[j], self.came.at[j], s[0].at[j], s[1].at[j], peer)
+
+    def down(self, j):
+        s = self.sems
+        slot = jnp.where(self.plane - 1 == j, self.planes, j)
+        peer = {"dp": self.device - 2}
+        return remote(self.stack.at[j], self.came.at[slot], s[2].at[j], s[3].at[j], peer)
+
+    def start(self):
+        last = self.planes - 1
+
+        @pl.when(self.plane == 0)
+        def _():
+            for j in range(last, 0, -1):
+                self.up(j).start()
+
+        @pl.when(self.plane == last)
+        def _():
+            for j in range(last):
+                self.down(j).start()
+
+    def wave(self, i):
+        last = self.planes - 1
+        j = last - i
+
+        @pl.when((self.plane > 0) & (self.plane < j))
+        def _():
+            self.up(j).wait_recv()
+            self.stack[j] += self.came[j]
+            self.up(j).start()
+
+        @pl.when((self.plane < last) & (self.plane > i))
+        def _():
+            self.down(i).wait_recv()
+            self.stack[i] += self.came[i]
+            self.down(i).start()
+
+    def finish(self, out):
+        plane, planes = self.plane, self.planes
+        out[...] = self.stack[plane].astype(F32)
+
+        @pl.when(plane > 0)
+        def _():
+            self.up(plane).wait_recv()
+            out[...] += self.came[plane].astype(F32)
+
+        @pl.when(plane < planes - 1)
+        def _():
+            self.down(plane).wait_recv()
+            out[...] += self.came[planes].astype(F32)
+
+        for j in range(planes):
+            pl.when(plane < j)(lambda j=j: self.up(j).wait_send())
+            pl.when(plane > j)(lambda j=j: self.down(j).wait_send())
+
+    def fill_rows(self, left, left_came, right, right_came):
+        shard = self.stack.shape[1]
+
+        def body(j, carry):
+            at = pl.ds(pl.multiple_of(j * shard, shard), shard)
+            self.stack[j] = (
+                dot(left[:, at], right[...], TN) + dot(left_came[:, at], right_came[...], TN)
+            ).astype(BF16)
+            return carry
+
+        lax.fori_loop(0, self.planes, body, 0)
+
+    def fill_columns(self, left, left_came, right, right_came):
+        shard = self.stack.shape[2]
+        tile = 256
+
+        def body(t, carry):
+            at = pl.ds(pl.multiple_of(t * tile, tile), tile)
+            term = dot(left[:, at], right[...], TN) + dot(left_came[:, at], right_came[...], TN)
+            for j in range(self.planes):
+                self.stack[j, at, :] = term[:, j * shard : (j + 1) * shard].astype(BF16)
+            return carry
+
+        lax.fori_loop(0, left.shape[1] // tile, body, 0)
+
+
 class TensorSum:
-    def __init__(self, scratch, core, core_peer, y_peer):
-        (self.away, self.core_came, self.both, self.y_came, self.mine) = scratch[:5]
-        self.sems = scratch[5:]
+    def __init__(self, scratch, mine, core, core_peer, y_peer):
+        self.away, self.core_came, self.both, self.y_came = scratch[:4]
+        self.sems = scratch[4:]
+        self.mine = mine
         self.core, self.core_peer, self.y_peer = core, core_peer, y_peer
         self.chunks, self.half, self.width = self.away.shape
 
     @staticmethod
     def scratch(chunks, half, width):
-        return (
-            [pltpu.VMEM((chunks, half, width), BF16)] * 4
-            + [pltpu.VMEM((2, 2 * half, width), F32)]
-            + [pltpu.SemaphoreType.DMA((chunks,))] * 4
-        )
+        return [pltpu.VMEM((chunks, half, width), BF16)] * 4 + [
+            pltpu.SemaphoreType.DMA((chunks,))
+        ] * 4
 
     def over_core(self, i):
         s = self.sems
@@ -224,39 +319,6 @@
         cost_estimate=COST,
         name=name,
     )(x, gain, *weights, *gains, cos, sin)
-
-
-def unproject_kernel(d_ref, raw_ref, gain_ref, cos_ref, sin_ref, out_ref, gain_out_ref, *, width, plain):
-    columns = d_ref.shape[1]
-    cos, sin = cos_ref[...], sin_ref[...]
-    gain = gain_ref[...]
-    total = jnp.zeros((1, width), F32)
-    for at in range(0, columns - plain, width):
-        d = d_ref[:, at : at + width].astype(F32)
-        c = d * cos - roll_half(d) * sin
-        v = raw_ref[:, at : at + width]
-        r = lax.rsqrt(jnp.mean(v * v, axis=1, keepdims=True) + EPS)
-        n = v * r
-        total = total + jnp.sum(c * n, axis=0, keepdims=True)
-        gc = gain * c
-        out_ref[:, at : at + width] = (r * (gc - n * jnp.mean(n * gc, axis=1, keepdims=True))).astype(BF16)
-    if plain:
-        out_ref[:, columns - plain :] = d_ref[:, columns - plain :].astype(BF16)
-    gain_out_ref[...] = total
-
-
-def unproject(d, raw, gain, cos, sin, plain, name):
-    rows, columns = d.shape
-    width = cos.shape[1]
-    return pl.pallas_call(
-        functools.partial(unproject_kernel, width=width, plain=plain),
-        out_shape=[jax.ShapeDtypeStruct((rows, columns), BF16), jax.ShapeDtypeStruct((1, width), F32)],
-        in_specs=vmem(5),
-        out_specs=vmem(2),
-        compiler_params=params(),
-        cost_estimate=COST,
-        name=name,
-    )(d, raw, gain, cos, sin)
 
 
 def visible(shape, key0, row0, prefix):
@@ -550,16 +612,15 @@
     send_x, recv_x, send_z, recv_z, send_first, recv_first = take(6)
     swap_sems = take(4)
     h_scratch, a_scratch = take(6), take(6)
-    if sums:
-        gate_came_ref, send_gate, recv_gate = take(3)
-        down_sum, gate_sum, out_sum = take(6), take(6), take(6)
-
     rows = qx_ref.shape[1]
     kv_width = kv_heads * width
     device = lax.axis_index("dp")
     member = device % group
     plane = member // 2
     last = planes - 1
+    if sums:
+        gate_came_ref, send_gate, recv_gate = take(3)
+        down_sum, gate_sum, out_sum = (LineSum(take(6), device, plane, planes) for _ in range(3))
     x_at = member % 2
     x_other = device + 1 - 2 * x_at
     inner = plane < last
@@ -584,93 +645,8 @@
     heads_swap = copy(heads_ref, heads_came_ref, swap_sems[0], swap_sems[1], x_other)
     up_swap = copy(up_ref, up_came_ref, swap_sems[2], swap_sems[3], x_other)
 
-    def up(parts, j):
-        stack, came, send_up, recv_up = parts[:4]
-        return copy(stack.at[j], came.at[j], send_up.at[j], recv_up.at[j], device + 2)
-
-    def down(parts, j):
-        stack, came, _, _, send_down, recv_down = parts
-        slot = jnp.where(plane - 1 == j, planes, j)
-        return copy(stack.at[j], came.at[slot], send_down.at[j], recv_down.at[j], device - 2)
-
-    def sum_start(parts):
-        @pl.when(plane == 0)
-        def _():
-            for j in range(last, 0, -1):
-                up(parts, j).start()
-
-        @pl.when(plane == last)
-        def _():
-            for j in range(last):
-                down(parts, j).start()
-
-    def sum_wave(parts, wave):
-        stack, came = parts[:2]
-        j = last - wave
-        i = wave
-
-        @pl.when((plane > 0) & (plane < j))
-        def _():
-            up(parts, j).wait_recv()
-            stack[j] += came[j]
-            up(parts, j).start()
-
-        @pl.when((plane < last) & (plane > i))
-        def _():
-            down(parts, i).wait_recv()
-            stack[i] += came[i]
-            down(parts, i).start()
-
-    def sum_finish(parts, out):
-        stack, came = parts[:2]
-        out[...] = stack[plane].astype(F32)
-
-        @pl.when(plane > 0)
-        def _():
-            up(parts, plane).wait_recv()
-            out[...] += came[plane].astype(F32)
-
-        @pl.when(plane < last)
-        def _():
-            down(parts, plane).wait_recv()
-            out[...] += came[planes].astype(F32)
-
-        for j in range(planes):
-            pl.when(plane < j)(lambda j=j: up(parts, j).wait_send())
-            pl.when(plane > j)(lambda j=j: down(parts, j).wait_send())
-
     def gate_swap():
         return copy(gate_ref, gate_came_ref, send_gate, recv_gate, x_other)
-
-    def column_terms(stack, left, left_came, right, right_came):
-        tile = 256
-
-        def body(t, carry):
-            at = pl.ds(pl.multiple_of(t * tile, tile), tile)
-            term = dot(left[:, at], right[...], TN) + dot(left_came[:, at], right_came[...], TN)
-            for j in range(planes):
-                stack[j, at, :] = term[:, j * shard : (j + 1) * shard].astype(BF16)
-            return carry
-
-        lax.fori_loop(0, left.shape[1] // tile, body, 0)
-
-    def down_terms():
-        column_terms(down_sum[0], hid_ref, hid_came_ref, og_ref, og_came_ref)
-
-    def out_terms():
-        column_terms(out_sum[0], heads_ref, heads_came_ref, a_ref, a_came_ref)
-
-    def gate_terms():
-        stack = gate_sum[0]
-
-        def body(j, carry):
-            at = pl.ds(pl.multiple_of(j * shard, shard), shard)
-            stack[j] = (
-                dot(h_ref[:, at], gate_ref[...], TN) + dot(h_came_ref[:, at], gate_came_ref[...], TN)
-            ).astype(BF16)
-            return carry
-
-        lax.fori_loop(0, planes, body, 0)
 
     lane = lax.broadcasted_iota(jnp.int32, (rows, width), 1)
     minus = jnp.where(lane < 3, -1.0, 0.0).astype(BF16)
@@ -756,8 +732,8 @@
     dq_ref[...] = jnp.zeros_like(dq_ref)
     if sums:
         gate_swap().start()
-        down_terms()
-        sum_start(down_sum)
+        down_sum.fill_columns(hid_ref, hid_came_ref, og_ref, og_came_ref)
+        down_sum.start()
     h_two.start()
     h_two.store()
     d_attn.store()
@@ -766,7 +742,7 @@
     for count, slot in enumerate(range(last, -1, -1)):
         attend(slot)
         if sums and count >= 1 and count - 1 < len(waves):
-            sum_wave(down_sum, waves[count - 1])
+            down_sum.wave(waves[count - 1])
         if count >= 1 and slot >= 1:
             pass_back(pending.pop(0))
         if slot == min(1, last):
@@ -776,8 +752,8 @@
             if sums:
                 gate_swap().wait_recv()
                 h_two.over_core().wait_recv()
-                gate_terms()
-                sum_start(gate_sum)
+                gate_sum.fill_rows(h_ref, h_came_ref, gate_ref, gate_came_ref)
+                gate_sum.start()
     up_swap.start()
     while pending:
         pass_back(pending.pop(0))
@@ -786,12 +762,12 @@
     heads_swap.wait_recv()
     d_attn.over_core().wait_recv()
     if sums:
-        out_terms()
-        sum_start(out_sum)
+        out_sum.fill_columns(heads_ref, heads_came_ref, a_ref, a_came_ref)
+        out_sum.start()
         for wave in waves:
-            sum_wave(gate_sum, wave)
+            gate_sum.wave(wave)
         for wave in waves:
-            sum_wave(out_sum, wave)
+            out_sum.wave(wave)
 
     far_swap(0).wait_recv()
     grad_ref[...] = own_ref[0].astype(F32) + xr_ref[0].astype(F32)
@@ -808,9 +784,9 @@
             grad_ref[...] += first_ref[...].astype(F32)
 
     if sums:
-        sum_finish(down_sum, w_down_ref)
-        sum_finish(gate_sum, w_gate_ref)
-        sum_finish(out_sum, w_out_ref)
+        down_sum.finish(w_down_ref)
+        gate_sum.finish(w_gate_ref)
+        out_sum.finish(w_out_ref)
         gate_swap().wait_send()
     up_swap.wait_recv()
     up_swap.wait_send()
@@ -854,8 +830,7 @@
         out_shape += [jax.ShapeDtypeStruct(s, F32) for s in shapes]
         scratch += [pltpu.VMEM((rows, units), BF16), dma, dma]
         for shape in shapes:
-            scratch += [pltpu.VMEM((n,) + shape, BF16) for n in (planes, planes + 1)]
-            scratch += [dma((planes,))] * 4
+            scratch += LineSum.scratch(planes, shape)
     return pl.pallas_call(
         functools.partial(
             back_kernel,
@@ -997,7 +972,6 @@
     add_ref,
     gain_ref,
     hid_came_ref,
-    d_ref,
     own_ref,
     far_ref,
     gain_out_ref,
@@ -1005,6 +979,7 @@
     up_buf,
     load_sems,
     c_ref,
+    mine_ref,
     hid_send,
     hid_recv,
     far_send,
@@ -1016,7 +991,7 @@
     core, core_peer, y_peer = tensor_peers()
     x_peer = {"dp": device + 1 - 2 * (device % 2)}
     half = middle_ref.shape[0]
-    total = TensorSum(scratch, core, core_peer, y_peer)
+    total = TensorSum(scratch, mine_ref, core, core_peer, y_peer)
     chunks, width = total.chunks, total.width
 
     def loads(i):
@@ -1056,7 +1031,6 @@
         gain_out_ref[...] += jnp.sum(c * n, axis=0, keepdims=True)
         gc = c * gain_ref[...]
         d = r * (gc - n * jnp.mean(n * gc, axis=1, keepdims=True)) + add_ref[add_at, :].astype(F32)
-        d_ref[at, :] = d
         own_ref[at, :] = d.astype(BF16)
         to_core(b).start()
     for b in range(blocks):
@@ -1078,15 +1052,16 @@
         functools.partial(d_middle_kernel, blocks=blocks),
         out_shape=[
             jax.ShapeDtypeStruct(hidden.shape, BF16),
-            jax.ShapeDtypeStruct((half, model), F32),
             jax.ShapeDtypeStruct((half, model), BF16),
             jax.ShapeDtypeStruct((half, model), BF16),
             jax.ShapeDtypeStruct((1, model), F32),
         ],
         in_specs=vmem(3) + [anywhere] * 2 + vmem(3),
-        out_specs=vmem(5),
+        out_specs=vmem(4),
         scratch_shapes=[pltpu.VMEM((chunks, width, units), BF16)] * 2
-        + [dma((2 * chunks,)), pltpu.VMEM((half, model), F32), dma, dma, dma((blocks,)), dma((blocks,))]
+        + [dma((2 * chunks,)), pltpu.VMEM((half, model), F32)]
+        + [pltpu.VMEM((2, 2 * half, width), F32)]
+        + [dma, dma, dma((blocks,)), dma((blocks,))]
         + TensorSum.scratch(chunks, half, width),
         compiler_params=pltpu.CompilerParams(
             vmem_limit_bytes=VMEM_LIMIT, collective_id=2, has_side_effects=True
@@ -1096,14 +1071,233 @@
     )(hidden, d_gate, d_up, w_gate, w_up, middle, out_grad, gain)
 
 
-def rms_parts(value):
-    r = lax.rsqrt(jnp.mean(value * value, axis=-1, keepdims=True) + EPS)
-    return r, value * r
-
-
-def rms_back(r, n, gain, c):
-    gc = gain * c
-    return r * (gc - n * jnp.mean(n * gc, axis=-1, keepdims=True))
+def through_rope(d_ref, raw_ref, gain, cos, sin, out_ref, width, plain):
+    columns = d_ref.shape[1]
+    total = jnp.zeros((1, width), F32)
+    for at in range(0, columns - plain, width):
+        d = d_ref[:, at : at + width]
+        c = d * cos - roll_half(d) * sin
+        v = raw_ref[:, at : at + width]
+        r = lax.rsqrt(jnp.mean(v * v, axis=1, keepdims=True) + EPS)
+        n = v * r
+        total = total + jnp.sum(c * n, axis=0, keepdims=True)
+        gc = gain * c
+        out_ref[:, at : at + width] = (r * (gc - n * jnp.mean(n * gc, axis=1, keepdims=True))).astype(BF16)
+    if plain:
+        out_ref[:, columns - plain :] = d_ref[:, columns - plain :].astype(BF16)
+    return total
+
+
+def front_kernel(*refs, dp_size, planes, chunks, sums):
+    refs = list(refs)
+
+    def take(count):
+        out = refs[:count]
+        del refs[:count]
+        return out
+
+    dq_in, dkv_in, q_raw, k_raw, q_gain, k_gain, cos_ref, sin_ref = take(8)
+    w_q, w_k, w_v, x_ref, mlp_gain_ref, middle_ref, hid_ref, w_down_ref = take(8)
+    if sums:
+        one_ref, one_came, two_ref, two_came, up_ref, up_came = take(6)
+    d_one, block_out, gains, dq_ref, dq_came, dkv_ref, dkv_came = take(7)
+    if sums:
+        w_up_out, w_q_out, w_kv_out = take(3)
+    mine, down_buf, down_sems, gain_came = take(4)
+    swap_sems, one_sems, block_sems, gain_sems = take(4), take(2), take(2), take(2)
+    one_sum_scratch, out_sum_scratch = take(8), take(8)
+    half = x_ref.shape[0] // 2
+    model = x_ref.shape[1]
+    width = model // chunks
+    head = cos_ref.shape[1]
+    kv_width = w_k.shape[1]
+
+    device = lax.axis_index("dp")
+    core, core_peer, y_peer = tensor_peers()
+    x_peer = {"dp": device + 1 - 2 * (device % 2)}
+    plane = device // 2
+    bits = [1 << i for i in range(dp_size.bit_length() - 1)]
+    dp_peers = [{"dp": device + bit - 2 * bit * ((device // bit) % 2)} for bit in bits]
+    gain_peers = [core_peer, y_peer] + dp_peers
+    meets = [(peer, True) for peer in gain_peers]
+    if sums:
+        up_sum, q_sum, kv_sum = (LineSum(take(6), device, plane, planes) for _ in range(3))
+        meets += [({"dp": device + 2}, plane < planes - 1), ({"dp": device - 2}, plane > 0)]
+
+    def load(i):
+        at = pl.ds(i * width, width)
+        return pltpu.make_async_copy(w_down_ref.at[:, at], down_buf.at[i % 2], down_sems.at[i])
+
+    load(0).start()
+    load(1).start()
+    greet(meets)
+    if sums:
+        up_sum.fill_rows(two_ref, two_came, up_ref, up_came)
+        up_sum.start()
+    cos, sin = cos_ref[...], sin_ref[...]
+    k_total = through_rope(dkv_in, k_raw, k_gain[...], cos, sin, dkv_ref, head, kv_width)
+    kv_swap = remote(dkv_ref, dkv_came, swap_sems[0], swap_sems[1], x_peer)
+    kv_swap.start()
+    q_total = through_rope(dq_in, q_raw, q_gain[...], cos, sin, dq_ref, head, 0)
+    q_swap = remote(dq_ref, dq_came, swap_sems[2], swap_sems[3], x_peer)
+    q_swap.start()
+
+    one_sum = TensorSum(one_sum_scratch, mine, core, core_peer, y_peer)
+    x = x_ref[...].astype(F32)
+    r = lax.rsqrt(jnp.mean(x * x, axis=1, keepdims=True) + EPS)
+    for i in range(chunks):
+        at = slice(i * width, (i + 1) * width)
+        part = (
+            dot(dq_ref[...], w_q[at, :], NT)
+            + dot(dkv_ref[:, :kv_width], w_k[at, :], NT)
+            + dot(dkv_ref[:, kv_width:], w_v[at, :], NT)
+        )
+        one_sum.add(i, part)
+        gains[0, :, at] = jnp.sum(part * (x_ref[:, at].astype(F32) * r), axis=0, keepdims=True)
+    gains[0, :, model : 2 * model] = mlp_gain_ref[...]
+    gains[0, :, 2 * model : 2 * model + head] = q_total
+    gains[0, :, 2 * model + head :] = k_total
+
+    def gain_swap(k):
+        return remote(
+            gains.at[k], gain_came.at[k], gain_sems[0].at[k], gain_sems[1].at[k], gain_peers[k]
+        )
+
+    def gain_add(k):
+        gain_swap(k).wait_recv()
+        gains[k + 1] = gains[k] + gain_came[k]
+        if k + 1 < len(gain_peers):
+            gain_swap(k + 1).start()
+
+    gain_swap(0).start()
+
+    out_sum = TensorSum(out_sum_scratch, mine, core, core_peer, y_peer)
+    for i in range(chunks):
+        load(i).wait()
+        out_sum.add(i, dot(hid_ref[...], down_buf[i % 2]))
+        if i + 2 < chunks:
+            load(i + 2).start()
+    gain_add(0)
+    if sums:
+        if planes > 2:
+            up_sum.wave(0)
+        kv_swap.wait_recv()
+        kv_sum.fill_rows(one_ref, one_came, dkv_ref, dkv_came)
+        kv_sum.start()
+    gain_add(1)
+    if sums:
+        q_swap.wait_recv()
+        q_sum.fill_rows(one_ref, one_came, dq_ref, dq_came)
+        q_sum.start()
+    gain_add(2)
+
+    mine_rows = rows_of(core, half)
+
+    def give(out, sems):
+        rows = out.at[mine_rows, :]
+        return remote(rows, rows, sems[0], sems[1], core_peer)
+
+    for i in range(chunks):
+        d_one[mine_rows, i * width : (i + 1) * width] = one_sum.total(i).astype(BF16)
+    give(d_one, one_sems).start()
+    if sums:
+        for wave in range(1, planes - 2):
+            up_sum.wave(wave)
+    for k in range(3, len(gain_peers)):
+        gain_add(k)
+    for i in range(chunks):
+        at = slice(i * width, (i + 1) * width)
+        block_out[mine_rows, at] = (middle_ref[:, at] + out_sum.total(i)).astype(BF16)
+    give(block_out, block_sems).start()
+    if sums:
+        for wave in range(planes - 2):
+            kv_sum.wave(wave)
+            q_sum.wave(wave)
+        up_sum.finish(w_up_out)
+        kv_sum.finish(w_kv_out)
+        q_sum.finish(w_q_out)
+    else:
+        kv_swap.wait_recv()
+        q_swap.wait_recv()
+    kv_swap.wait_send()
+    q_swap.wait_send()
+    for out, sems in ((d_one, one_sems), (block_out, block_sems)):
+        give(out, sems).wait_recv()
+        give(out, sems).wait_send()
+    for k in range(len(gain_peers)):
+        gain_swap(k).wait_send()
+    one_sum.finish()
+    out_sum.finish()
+
+
+def front(dq, dkv, q_raw, k_raw, q_gain, k_gain, cos, sin, weights, x, mlp_gain, middle, hidden, w_down, grads, dp_size, shard):
+    rows, model = x.shape
+    half = rows // 2
+    planes = dp_size // 2
+    chunks = 4
+    width = model // chunks
+    units = hidden.shape[1]
+    stages = dp_size.bit_length() + 1
+    dma = pltpu.SemaphoreType.DMA
+    gains = (2 * model + 2 * cos.shape[1],)
+    args = [dq, dkv, q_raw, k_raw, q_gain, k_gain, cos, sin, *weights, x, mlp_gain, middle, hidden, w_down]
+    whole = jax.ShapeDtypeStruct((rows, model), BF16)
+    q_shape, kv_shape = jax.ShapeDtypeStruct(dq.shape, BF16), jax.ShapeDtypeStruct(dkv.shape, BF16)
+    out_shape = [whole, whole, jax.ShapeDtypeStruct((stages + 1, 1) + gains, F32)]
+    out_shape += [q_shape, q_shape, kv_shape, kv_shape]
+    scratch = [pltpu.VMEM((2, rows, width), F32), pltpu.VMEM((2, units, width), BF16), dma((chunks,))]
+    scratch += [pltpu.VMEM((stages, 1) + gains, F32)]
+    scratch += [dma] * 8 + [dma((stages,))] * 2
+    scratch += TensorSum.scratch(chunks, half, width) * 2
+    if grads is not None:
+        args += grads
+        for columns in (units, dq.shape[1], dkv.shape[1]):
+            out_shape.append(jax.ShapeDtypeStruct((shard, columns), F32))
+            scratch += LineSum.scratch(planes, (shard, columns))
+    return pl.pallas_call(
+        functools.partial(
+            front_kernel, dp_size=dp_size, planes=planes, chunks=chunks, sums=grads is not None
+        ),
+        out_shape=out_shape,
+        in_specs=vmem(15) + [pl.BlockSpec(memory_space=pl.ANY)] + vmem(len(args) - 16),
+        out_specs=vmem(len(out_shape)),
+        scratch_shapes=scratch,
+        compiler_params=pltpu.CompilerParams(
+            vmem_limit_bytes=BACK_VMEM_LIMIT, collective_id=3, has_side_effects=True
+        ),
+        cost_estimate=COST,
+        name="front",
+    )(*args)
+
+
+def last_kernel(core_ref, d_ref, x_ref, gain_ref, own_ref, far_ref, out_ref, *, steps):
+    c = d_ref[...].astype(F32)
+    x = x_ref[...].astype(F32)
+    r = lax.rsqrt(jnp.mean(x * x, axis=1, keepdims=True) + EPS)
+    n = x * r
+    gc = c * gain_ref[...]
+    d = r * (gc - n * jnp.mean(n * gc, axis=1, keepdims=True))
+    mine = (pl.program_id(0) // steps) == core_ref[0]
+    out_ref[...] = d + jnp.where(mine, own_ref[...].astype(F32), far_ref[...].astype(F32))
+
+
+def tokens_grad_of(core, d_one, x, gain, own, far):
+    rows, model = x.shape
+    half = rows // 2
+    tile = math.gcd(half, 128)
+    steps = half // tile
+    row_spec = pl.BlockSpec((tile, model), lambda i: (i, 0))
+    half_spec = pl.BlockSpec((tile, model), lambda i: (i % steps, 0))
+    return pl.pallas_call(
+        functools.partial(last_kernel, steps=steps),
+        out_shape=jax.ShapeDtypeStruct((rows, model), F32),
+        grid=(2 * steps,),
+        in_specs=[smem(), row_spec, row_spec, pl.BlockSpec((1, model), lambda i: (0, 0))] + [half_spec] * 2,
+        out_specs=row_spec,
+        compiler_params=params(),
+        cost_estimate=COST,
+        name="tokens_grad",
+    )(core, d_one, x, gain, own, far)
 
 
 class Chain:
@@ -1234,18 +1428,6 @@
             core == 0, jnp.concatenate([mine, theirs], 0), jnp.concatenate([theirs, mine], 0)
         )
 
-    def sum_all(value, axes):
-        for axis, bit in axes:
-            size = dp_size if axis == "dp" else tensor_size
-            value = value + lax.ppermute(value, axis, [(d, d ^ bit) for d in range(size)])
-        return value
-
-    dp_bits = []
-    bit = 1
-    while bit < dp_size:
-        dp_bits.append(("dp", bit))
-        bit *= 2
-
     positions = (member * rows + jnp.arange(rows)).astype(F32)
     counter = jnp.arange(width // 2, dtype=F32)
     angles = positions[:, None] * (ROPE_BASE ** (-2.0 * counter / width))[None, :]
@@ -1297,7 +1479,7 @@
     hidden, d_gate, d_up = mlp(core_at, h_two_half, *chain(h_two_far), w_gate, w_up, d_hidden)
     chain.mark(hidden)
 
-    hidden_came, d_middle_half, d_attn_half, d_attn_far, norm_mlp_part = d_middle_of(
+    hidden_came, d_attn_half, d_attn_far, norm_mlp_part = d_middle_of(
         hidden, d_gate, d_up, w_gate, w_up, middle, out_grad, norm_mlp_row
     )
     chain.mark(d_attn_far)
@@ -1320,93 +1502,53 @@
         out_part = dot(heads_b, d_attn_keep, TN) + dot(heads_came, d_attn_came, TN)
         w_out_grad = ZSum(out_part.astype(BF16), 1, shard, planes, z_at).finish(chain)
 
-    d_middle_far = core_swap(chain(d_middle_half)[0])
-    dq_b, q_gain_part = unproject(chain(dq)[0], q_raw, q_gain_row, cos, sin, 0, "unproject_q")
-    chain.mark(dq_b)
-    dq_came = x_swap(chain(dq_b)[0])
-    up_part = (dot(h_two_keep, d_up, TN) + dot(h_two_came, *chain(up_came), TN)).astype(BF16)
-    chain.mark(up_part)
-    up = ZSum(up_part, 0, shard, planes, z_at)
-    up.start()
-
-    dkv_b, k_gain_part = unproject(
-        chain(kv_grad)[0], k_raw, k_gain_row, cos, sin, kv_heads * width, "unproject_kv"
+    up_grads = [h_one_keep, h_one_came, h_two_keep, h_two_came, d_up, up_came] if fused else None
+    outs = front(
+        *chain(dq),
+        kv_grad,
+        q_raw,
+        k_raw,
+        q_gain_row,
+        k_gain_row,
+        cos,
+        sin,
+        (w_query, key_weight, value_weight),
+        tokens,
+        0.5 * norm_mlp_part,
+        middle,
+        hidden,
+        w_down,
+        up_grads,
+        dp_size,
+        shard,
     )
+    d_h_one, block_out, gains, dq_b, dq_came, dkv_b, dkv_came = outs[:7]
+    if fused:
+        w_up_grad, w_query_grad, w_kv_grad = outs[7:]
+    else:
+        chain.mark(d_h_one)
+
+        def by_rows(left, left_came, right, right_came):
+            part = dot(left, right, TN) + dot(left_came, right_came, TN)
+            return ZSum(part.astype(BF16), 0, shard, planes, z_at).finish(chain)
+
+        w_up_grad = by_rows(h_two_keep, h_two_came, d_up, up_came)
+        w_query_grad = by_rows(h_one_keep, h_one_came, dq_b, dq_came)
+        w_kv_grad = by_rows(h_one_keep, h_one_came, dkv_b, dkv_came)
     kv_width = kv_heads * width
-    chain.mark(dkv_b)
-    dkv_came = x_swap(dkv_b)
-
-    def d_h_one_part(which):
-        dkv_rows = which(dkv_b)
-        return (
-            dot(which(dq_b), w_query, NT)
-            + dot(dkv_rows[:, :kv_width], key_weight, NT)
-            + dot(dkv_rows[:, kv_width:], value_weight, NT)
-        )
-
-    away = d_h_one_part(other_half)
-    came = core_swap(away.astype(BF16))
-    mine = d_h_one_part(own_half)
-    both = (mine + came.astype(F32)).astype(BF16)
-    chain.mark(both)
-    one_y = y_swap(both)
-    x_half = own_half(tokens).astype(F32)
-    x_other = other_half(tokens).astype(F32)
-    r_own, n_own = rms_parts(x_half)
-    r_other, n_other = rms_parts(x_other)
-    norm_attn_part = jnp.sum(away * n_other + mine * n_own, axis=0)
-
-    up.step(chain)
-    mlp_away = dot(other_half(chain(hidden)[0]), w_down).astype(BF16)
-    mlp_came = core_swap(mlp_away)
-    chain.mark(mlp_away)
-    mlp_both = (dot(own_half(chain(hidden)[0]), w_down) + mlp_came.astype(F32)).astype(BF16)
-    chain.mark(mlp_both)
-    mlp_y = y_swap(mlp_both)
-    (dq_came,) = chain(dq_came)
-    q_part = (dot(h_one_keep, dq_b, TN) + dot(h_one_came, dq_came, TN)).astype(BF16)
-    chain.mark(q_part)
-    query = ZSum(q_part, 0, shard, planes, z_at)
-    query.start()
-    (dkv_came,) = chain(dkv_came)
-    kv_part = (dot(h_one_keep, dkv_b, TN) + dot(h_one_came, dkv_came, TN)).astype(BF16)
-    chain.mark(kv_part)
-    key_value = ZSum(kv_part, 0, shard, planes, z_at)
-    key_value.start()
-    up.step(chain)
-    query.step(chain)
-    key_value.step(chain)
-    w_up_grad = up.finish(chain)
-    query.step(chain)
-    key_value.step(chain)
-
-    d_h_one = (both.astype(F32) + one_y.astype(F32)).astype(BF16)
-    d_h_one_other = core_swap(d_h_one)
-    grad_own = d_middle_half + rms_back(r_own, n_own, norm_attn_row, d_h_one.astype(F32))
-    grad_other = d_middle_far + rms_back(r_other, n_other, norm_attn_row, d_h_one_other.astype(F32))
-    tokens_grad = join(grad_own, grad_other)
-    block_half = (middle + (mlp_both.astype(F32) + mlp_y.astype(F32))).astype(BF16)
-    block_out = join(block_half, core_swap(block_half))
-    w_query_grad = query.finish(chain)
-    w_kv_grad = key_value.finish(chain)
-
-    small = jnp.concatenate([norm_attn_part, q_gain_part[0], k_gain_part[0]])
-    norm_mlp_part, small = chain(norm_mlp_part[0], small)
-    norm_mlp_sum = sum_all(norm_mlp_part, [("tensor", 1)] + dp_bits)
-    small = sum_all(small, [("tensor", 1), ("tensor", 2)] + dp_bits)
-    norm_mlp_grad = lax.dynamic_slice_in_dim(norm_mlp_sum, device * shard, shard, 0)
-    norm_attn_grad = lax.dynamic_slice_in_dim(small, device * shard, shard, 0)
+    tokens_grad = tokens_grad_of(core_at, d_h_one, tokens, norm_attn_row, d_attn_half, d_attn_far)
+    gains = gains[-1, 0]
     return (
         block_out,
         tokens_grad,
-        norm_attn_grad,
+        lax.dynamic_slice_in_dim(gains, device * shard, shard, 0),
         w_query_grad,
         w_kv_grad[:, :kv_width],
         w_kv_grad[:, kv_width:],
-        small[model : model + width],
-        small[model + width :],
+        gains[2 * model : 2 * model + width],
+        gains[2 * model + width :],
         w_out_grad,
-        norm_mlp_grad,
+        lax.dynamic_slice_in_dim(gains, model + device * shard, shard, 0),
         w_gate_grad,
         w_up_grad,
         w_down_grad,

time: 567 us -> 522 us (0.921)
  Pallas kernels: 327 us -> 460 us
  starting transfers between devices: 70.5 us -> 4.2 us
  waiting for transfers between devices: 74.9 us -> 13.1 us
  matrix products: 44.2 us -> 12.5 us
  other arithmetic: 27.3 us -> 6.19 us
    pallas_call x2, Pallas kernels: 6.74 us -> 141 us  [the longest x1 134 us: front(): pl.pallas_call(functools.partial(front_kernel, dp_size=dp_size, planes=pl...]
    ppermute x27 -> x0, starting transfers between devices: 59.4 us -> none  [the longest x9 39.9 us: send(): lax.ppermute(up, 'dp', up_pairs)]
    dot_general x17 -> x3, matrix products: 44.2 us -> 12.5 us  [dot(): return lax.dot_general(left, right, dims, preferred_element_type=F32)]
    ppermute x27 -> x0, waiting for transfers between devices: 26.5 us -> none  [the longest x9 20.4 us: send(): lax.ppermute(up, 'dp', up_pairs)]
    ppermute x3 -> x1, waiting for transfers between devices: 31.8 us -> 7.23 us  [y_swap(): return lax.ppermute(value, 'tensor', y_pairs)]
    add x19 -> x0, other arithmetic: 11.9 us -> none  [the longest x3 4.55 us: finish(): total = self.term(self.z_at).astype(F32) + up.astype(F32) + down.astype(F32)]
    ppermute x4 -> x2, waiting for transfers between devices: 10.5 us -> 0.01 us  [x_swap(): return lax.ppermute(value, 'dp', x_pairs)]
  transfers between devices with their start and end apart: 43 -> 7, of which waited for: 12 -> 3; matrix products, arithmetic and copies ran while one was open for 10% -> 2% of each run, Pallas kernels for 2% -> 2%
where the time goes in v4:
time: 522 us; the launch traced here: 513 us
  Pallas kernels  460 us (88%)
  local copies, waits for them, and re-layouts  15 us (3%)
  waiting for transfers between devices  13.1 us (3%)
  matrix products  12.5 us (2%)
  other arithmetic  6.19 us (1%)
    pallas_call x1, Pallas kernels, back(): pl.pallas_call(functools.partial(back_kernel, group=group, planes=planes,...  202 us
    pallas_call x1, Pallas kernels, front(): pl.pallas_call(functools.partial(front_kernel, dp_size=dp_size, planes=pl...  134 us
    pallas_call x1, Pallas kernels, d_middle_of(): pl.pallas_call(functools.partial(d_middle_kernel, blocks=blocks), out_sha...  43.2 us
    pallas_call x1, Pallas kernels, attn_fwd(): pl.pallas_call(functools.partial(attn_fwd_kernel, group=group, kv_heads=k...  35.4 us
    pallas_call x1, Pallas kernels, mlp(): pl.pallas_call(mlp_kernel, out_shape=[jax.ShapeDtypeStruct((2 * half, uni...  13.9 us
    dot_general x3, matrix products, dot(): return lax.dot_general(left, right, dims, preferred_element_type=F32)  12.5 us
  transfers between devices with their start and end apart: 7, of which 3 were waited for; matrix products, arithmetic and copies ran while one was open for 2% of the time, Pallas kernels for 2%

profile of v4, /device:TPU:0, one launch (start us, length us, event | category | flops | bytes accessed | tf_op | source)
XLA Modules:
  0.0 512.5 jit_solution(12879586307668346456)
XLA Ops:
  0.7 1.0 fusion.5
  1.7 1.0 pad_maximum_fusion
  2.7 8.2 %project.1 = (bf16[512,2048]{1,0:T(8,128)(2,1)}, bf16[512,1024]{1,0:T(8,128)(2,1)}, f32[512,512]{1,0:T(8,128)}, f32[512,256]{1,0:T(8,128)}) custom-call(bf16[512,2048]{1,0:T(8,128)(2,1)} %x_ref.5, f32[1,2048]{1,0:T(1,128)} %bitcast.19, bf16[2048,512]{1,0:T(8,128)(2,1)} %refs_8_.1, bf16[2048,256]{1,0:T(8,128)(2,1)} %refs_9_.1, bf16[2048,256]{1,0:T(8,128)(2,1)} %refs_10_.1, ...), custom_call_target="tpu_custom_call" | custom-call | flops 1000 | bytes 1000 | tf_op jit(solution)/shard_map/project/pallas_call | solution.py:309
  10.9 2.4 fusion.8
  14.0 35.4 %attn_fwd.1 = (bf16[512,512]{1,0:T(8,128)(2,1)}, f32[512,512]{1,0:T(8,128)}, bf16[8,512,512]{2,1,0:T(8,128)(2,1)}) custom-call(s32[1]{0:T(128)S(6)} %select_n.48.prefix_ref.refs_0_, bf16[512,512]{1,0:T(8,128)(2,1)} %get-tuple-element.96.q_ref, bf16[512,512]{1,0:T(8,128)(2,1)} %get-tuple-element.95.kv_ref), custom_call_target="tpu_custom_call" | custom-call | flops 1000 | bytes 1000 | tf_op jit(solution)/shard_map/attn_fwd/pallas_call | solution.py:523
  49.4 2.7 convolution_convert_fusion
  52.1 3.0 collective-permute-done
  55.1 1.9 add_convert_fusion.both_ref
  57.1 1.6 collective-permute-start.1
  59.2 3.0 cut.2
  62.2 1.5 collective-permute-start.3
  63.7 7.9 %fusion.10.d_ref = f32[512,1536]{1,0:T(8,128)} fusion(bf16[512,2048]{1,0:T(8,128)(2,1)S(1)} %copy-done.1, bf16[1536,2048]{1,0:T(8,128)(2,1)} %refs_15_.1), kind=kOutput, calls=%fused_computation.24 | convolution fusion | flops 3221225472 | bytes 11534336 | tf_op jit(solution)/shard_map/dot_general | solution.py:27
  71.6 3.0 cut.3
  75.1 7.2 %collective-permute-done.1.y_ref = bf16[256,2048]{1,0:T(8,128)(2,1)S(1)} collective-permute-done((bf16[256,2048]{1,0:T(8,128)(2,1)S(1)}, bf16[256,2048]{1,0:T(8,128)(2,1)S(1)}, u32[]{:S(2)}, u32[]{:S(2)}) %collective-permute-start.1) | collective-permute-done | bytes 1048608 | tf_op jit(solution)/shard_map/ppermute | solution.py:1412
  82.3 1.0 copy-done.9
  83.3 4.4 norm_forward.1
  88.3 2.8 collective-permute-done.4
  91.1 1.5 maximum_select_fusion.refs_13_
  92.6 1.5 maximum_select_fusion.1.refs_17_
  94.1 1.0 copy-done.3
  95.1 13.9 %mlp.1 = (bf16[512,1536]{1,0:T(8,128)(2,1)}, bf16[512,1536]{1,0:T(8,128)(2,1)}, bf16[512,1536]{1,0:T(8,128)(2,1)}) custom-call(s32[1]{0:T(128)} %bitcast.1.core_ref, bf16[256,2048]{1,0:T(8,128)(2,1)} %get-tuple-element.63.own_ref.refs_4_, bf16[256,2048]{1,0:T(8,128)(2,1)} %copy-done.3, bf16[2048,1536]{1,0:T(8,128)(2,1)} %w_gate_ref.1, ...), custom_call_target="tpu_custom_call" | custom-call | flops 1000 | bytes 1000 | tf_op jit(solution)/shard_map/mlp/pallas_call | solution.py:953
  109.0 43.2 %d_middle.1 = (bf16[512,1536]{1,0:T(8,128)(2,1)}, bf16[256,2048]{1,0:T(8,128)(2,1)}, bf16[256,2048]{1,0:T(8,128)(2,1)}, f32[1,2048]{1,0:T(1,128)}) custom-call(bf16[512,1536]{1,0:T(8,128)(2,1)} %get-tuple-element.65.hid_ref.refs_10_.refs_14_, bf16[512,1536]{1,0:T(8,128)(2,1)} %get-tuple-element.66.d_gate_ref.refs_14_, ...), custom_call_target="tpu_custom_call" | custom-call | flops 1000 | bytes 1000 | tf_op jit(solution)/shard_map/d_middle/pallas_call | solution.py:1051
  152.2 5.8 %attn_prep.1 = (bf16[4,512,256]{2,1,0:T(8,128)(2,1)}, bf16[4,512,256]{2,1,0:T(8,128)(2,1)}) custom-call(s32[1]{0:T(128)} %bitcast.1.core_ref, bf16[256,2048]{1,0:T(8,128)(2,1)} %get-tuple-element.69.own_ref.refs_6_, bf16[256,2048]{1,0:T(8,128)(2,1)} %get-tuple-element.70.far_ref.refs_7_, bf16[512,2048]{1,0:T(8,128)(2,1)} %w_ref.1, ...), custom_call_target="tpu_custom_call" | custom-call | flops 1000 | bytes 1000 | tf_op jit(solution)/shard_map/attn_prep/pallas_call | solution.py:583
  158.0 201.5 %back.1 = (f32[512,512]{1,0:T(8,128)}, f32[512,512]{1,0:T(8,128)}, bf16[512,1024]{1,0:T(8,128)(2,1)}, bf16[512,1024]{1,0:T(8,128)(2,1)}, bf16[512,1024]{1,0:T(8,...) custom-call(s32[1]{0:T(128)S(6)} %select_n.48.prefix_ref.refs_0_, ...), custom_call_target="tpu_custom_call" | custom-call | flops 1000 | bytes 1000 | tf_op jit(solution)/shard_map/back/pallas_call | solution.py:834
  360.1 134.0 %front.1 = (bf16[512,2048]{1,0:T(8,128)(2,1)}, bf16[512,2048]{1,0:T(8,128)(2,1)}, f32[6,1,4352]{2,1,0:T(1,128)}, bf16[512,512]{1,0:T(8,128)(2,1)}, bf16[512,512]...) custom-call(f32[512,512]{1,0:T(8,128)} %get-tuple-element.77.refs_0_, ...), custom_call_target="tpu_custom_call" | custom-call | flops 1000 | bytes 1000 | tf_op jit(solution)/shard_map/front/pallas_call | solution.py:1257
  494.9 1.2 slice_bitcast_fusion
  496.1 7.3 %tokens_grad.1 = f32[512,2048]{1,0:T(8,128)} custom-call(s32[1]{0:T(128)} %bitcast.1.core_ref, bf16[512,2048]{1,0:T(8,128)(2,1)} %get-tuple-element.87.d_ref, bf16[512,2048]{1,0:T(8,128)(2,1)} %x_ref.5, f32[1,2048]{1,0:T(1,128)} %bitcast.20, bf16[256,2048]{1,0:T(8,128)(2,1)} %get-tuple-element.69.own_ref.refs_6_, ...), custom_call_target="tpu_custom_call" | custom-call | flops 1000 | bytes 1000 | tf_op jit(solution)/shard_map/tokens_grad/pallas_call | solution.py:1291
  504.8 1.3 copy.34
  507.8 1.1 copy.37
  509.0 1.1 copy.38
  510.1 0.8 copy-done.6
  510.9 1.1 copy.39
  (43 shorter events, 6.2 us)
Async XLA Ops:
  10.9 38.5 %copy-start = (bf16[512,2048]{1,0:T(8,128)(2,1)S(1)}, bf16[512,2048]{1,0:T(8,128)(2,1)}, u32[]{:S(2)}) copy-start(bf16[512,2048]{1,0:T(8,128)(2,1)} %w_ref.1) | copy-start | bytes 6291460
  49.4 5.7 %copy-start.2 = (bf16[512,512]{1,0:T(8,128)(2,1)S(1)}, bf16[512,512]{1,0:T(8,128)(2,1)}, u32[]{:S(2)}) copy-start(bf16[512,512]{1,0:T(8,128)(2,1)} %get-tuple-element.55.o_ref.refs_8_) | copy-start | bytes 1572868
  52.1 3.0 collective-permute-start
  57.0 14.6 %copy-start.4 = (bf16[256,2048]{1,0:T(8,128)(2,1)}, bf16[256,2048]{1,0:T(8,128)(2,1)S(1)}, u32[]{:S(2)}) copy-start(bf16[256,2048]{1,0:T(8,128)(2,1)S(1)} %add_convert_fusion.both_ref) | copy-start | bytes 3145732
  57.0 6.6 %copy-start.1 = (bf16[512,2048]{1,0:T(8,128)(2,1)S(1)}, bf16[512,2048]{1,0:T(8,128)(2,1)}, u32[]{:S(2)}) copy-start(bf16[512,2048]{1,0:T(8,128)(2,1)} %add_ref.1) | copy-start | bytes 6291460
  57.1 25.3 %collective-permute-start.1 = (bf16[256,2048]{1,0:T(8,128)(2,1)S(1)}, bf16[256,2048]{1,0:T(8,128)(2,1)S(1)}, u32[]{:S(2)}, u32[]{:S(2)}) collective-permute-start(bf16[256,2048]{1,0:T(8,128)(2,1)S(1)} %add_convert_fusion.both_ref), channel_id=1, source_target_pairs={{0,2},{1,3},{2,0},{3,1},{4,6},{5,7},{6,4},{7,5},{8,10},{9,11},{10,... | collective-permute-start | bytes 3145736 | tf_op jit(solution)/shard_map/ppermute | solution.py:1412
  62.2 25.5 %collective-permute-start.3 = (bf16[256,1024]{1,0:T(8,128)(2,1)}, bf16[256,1024]{1,0:T(8,128)(2,1)S(1)}, u32[]{:S(2)}, u32[]{:S(2)}) collective-permute-start(bf16[256,1024]{1,0:T(8,128)(2,1)} %get-tuple-element.76), channel_id=1, source_target_pairs={{0,4},{4,0},{8,12},{12,8},{16,20},{20,16},{24,28},{28,24},{1,5},{5... | collective-permute-start | bytes 1572872 | tf_op jit(solution)/shard_map/ppermute | solution.py:1415
  74.5 13.7 %collective-permute-start.5 = (bf16[256,1024]{1,0:T(8,128)(2,1)}, bf16[256,1024]{1,0:T(8,128)(2,1)S(1)}, u32[]{:S(2)}, u32[]{:S(2)}) collective-permute-start(bf16[256,1024]{1,0:T(8,128)(2,1)} %get-tuple-element.82), channel_id=1, source_target_pairs={{0,4},{4,0},{8,12},{12,8},{16,20},{20,16},{24,28},{28,24},{1,5},{5... | collective-permute-start | bytes 1572872 | tf_op jit(solution)/shard_map/ppermute | solution.py:1415
  82.3 1.0 copy-start.9
  87.7 6.4 %collective-permute-start.2 = (bf16[256,2048]{1,0:T(8,128)(2,1)}, bf16[256,2048]{1,0:T(8,128)(2,1)S(1)}, u32[]{:S(2)}, u32[]{:S(2)}) collective-permute-start(bf16[256,2048]{1,0:T(8,128)(2,1)} %get-tuple-element.63.own_ref.refs_4_), channel_id=1, source_target_pairs={{0,1},{1,0},{2,3},{3,2},{4,5},{5,4},{6,7},{7,6},{8,9},{9,8},{10,11... | collective-permute-start | bytes 3145736 | tf_op jit(solution)/shard_map/ppermute | solution.py:1409
  87.7 3.4 collective-permute-start.4
  88.2 4.4 collective-permute-start.6
  94.1 1.0 copy-start.3
  158.0 201.5 %copy-start.13 = (f32[1,2048]{1,0:T(1,128)S(1)}, f32[1,2048]{1,0:T(1,128)}, u32[]{:S(2)}) copy-start(f32[1,2048]{1,0:T(1,128)} %get-tuple-element.81) | copy-start | bytes 24580
  496.1 7.3 %copy-start.12 = (f32[256,512]{1,0:T(8,128)S(1)}, f32[256,512]{1,0:T(8,128)}, u32[]{:S(2)}) copy-start(f32[256,512]{1,0:T(8,128)} %get-tuple-element.90) | copy-start | bytes 1572868
  496.1 8.7 %copy-start.5 = (bf16[512,2048]{1,0:T(8,128)(2,1)S(1)}, bf16[512,2048]{1,0:T(8,128)(2,1)}, u32[]{:S(2)}) copy-start(bf16[512,2048]{1,0:T(8,128)(2,1)} %get-tuple-element.121) | copy-start | bytes 6291460
  504.8 1.4 copy-start.11
  504.8 2.2 copy-start.10
  506.2 1.6 copy-start.7
  507.0 2.0 copy-start.8
  509.0 2.0 copy-start.6

commit v5 on v4

--- a/solution.py
+++ b/solution.py
@@ -61,6 +61,31 @@
         device_id=peer,
         device_id_type=pl.DeviceIdType.MESH,
     )
+
+
+class Staged:
+    def __init__(self, arrays, buffers, sems, out=False):
+        self.copies = []
+        for i, (array, buffer) in enumerate(zip(arrays, buffers)):
+            ends = (buffer, array) if out else (array, buffer)
+            self.copies.append((buffer, pltpu.make_async_copy(*ends, sems.at[i])))
+
+    @staticmethod
+    def scratch(shapes):
+        return [pltpu.VMEM(s.shape, s.dtype) for s in shapes] + [pltpu.SemaphoreType.DMA((len(shapes),))]
+
+    def start(self, *buffers):
+        for buffer, copy in self.copies:
+            if not buffers or any(buffer is b for b in buffers):
+                copy.start()
+
+    def wait(self, *buffers):
+        for buffer, copy in self.copies:
+            if not buffers or any(buffer is b for b in buffers):
+                copy.wait()
+
+
+ANYWHERE = pl.BlockSpec(memory_space=pl.ANY)
 
 
 def tensor_peers():
@@ -87,12 +112,12 @@
 
 
 class Columns:
-    def __init__(self, own, far, keep, came, scratch, x_at, core, x_peer, core_peer, planes, shard):
-        self.own, self.far, self.keep, self.came = own, far, keep, came
+    def __init__(self, whole, keep, came, scratch, x_at, core, x_peer, core_peer, planes, shard):
+        self.whole, self.keep, self.came = whole, keep, came
         self.send_ref, self.recv_ref, self.sems = scratch[0], scratch[1], scratch[2:]
         self.x_at, self.core, self.cut = x_at, core, (planes, shard)
         self.x_peer, self.core_peer = x_peer, core_peer
-        self.half = own.shape[0]
+        self.half = whole.shape[0] // 2
 
     @staticmethod
     def scratch(half, columns):
@@ -106,14 +131,12 @@
         return remote(self.recv_ref, there, self.sems[2], self.sems[3], self.core_peer)
 
     def start(self):
-        every = slice(None)
-        cut_into(self.send_ref, every, self.own, every, 1 - self.x_at, *self.cut)
+        mine = rows_of(self.core, self.half)
+        cut_into(self.send_ref, slice(None), self.whole, mine, 1 - self.x_at, *self.cut)
         self.over_x().start()
 
     def store(self):
-        every = slice(None)
-        for ref, core in ((self.own, self.core), (self.far, 1 - self.core)):
-            cut_into(self.keep, rows_of(core, self.half), ref, every, self.x_at, *self.cut)
+        cut_into(self.keep, slice(None), self.whole, slice(None), self.x_at, *self.cut)
 
     def forward(self):
         self.over_x().wait_recv()
@@ -278,8 +301,8 @@
     w_refs = refs[:count]
     gain_refs = refs[count : 2 * count]
     cos_ref, sin_ref = refs[2 * count : 2 * count + 2]
-    h_ref, out_ref = refs[2 * count + 2 : 2 * count + 4]
-    raw_refs = refs[2 * count + 4 :]
+    h_ref, q_ref, kv_ref = refs[2 * count + 2 : 2 * count + 5]
+    raw_refs = refs[2 * count + 5 :]
     x = x_ref[...].astype(F32)
     h = (x * lax.rsqrt(jnp.mean(x * x, axis=1, keepdims=True) + EPS) * g_ref[...]).astype(BF16)
     h_ref[...] = h
@@ -287,6 +310,8 @@
     column = 0
     raw_at = 0
     for i in range(count):
+        out_ref = q_ref if i == 0 else kv_ref
+        column = 0 if i < 2 else column
         product = dot(h, w_refs[i][...])
         if normed[i]:
             raw_refs[raw_at][...] = product
@@ -310,11 +335,12 @@
         functools.partial(project_kernel, heads=heads, normed=normed, width=width),
         out_shape=[
             jax.ShapeDtypeStruct((rows, model), BF16),
-            jax.ShapeDtypeStruct((rows, columns), BF16),
+            jax.ShapeDtypeStruct((rows, weights[0].shape[1]), BF16),
+            jax.ShapeDtypeStruct((rows, columns - weights[0].shape[1]), BF16),
         ]
         + [jax.ShapeDtypeStruct((rows, w.shape[1]), F32) for w in raws],
         in_specs=vmem(4 + 2 * len(weights)),
-        out_specs=vmem(2 + len(raws)),
+        out_specs=vmem(3 + len(raws)),
         compiler_params=params(),
         cost_estimate=COST,
         name=name,
@@ -555,42 +581,6 @@
     return high.astype(F32), mid.astype(F32), (left - mid.astype(F32)).astype(BF16).astype(F32)
 
 
-def attn_prep_kernel(core_ref, own_ref, far_ref, w_ref, q_ref, o_ref, lse_ref, qx_ref, dox_ref, *, heads, width):
-    half = own_ref.shape[0]
-    core = core_ref[0]
-    lane = lax.broadcasted_iota(jnp.int32, (half, width), 1)
-
-    def extra(value):
-        a, b, c = split_three(value)
-        return jnp.where(lane == 0, a, jnp.where(lane == 1, b, jnp.where(lane == 2, c, 0.0))).astype(BF16)
-
-    for ref, at_core in ((own_ref, core), (far_ref, 1 - core)):
-        at_rows = pl.ds(pl.multiple_of(at_core * half, half), half)
-        d_heads = dot(ref[...], w_ref[...], NT)
-        for head in range(heads):
-            at = slice(head * width, (head + 1) * width)
-            qx_ref[head, at_rows, :width] = q_ref[at_rows, at]
-            qx_ref[head, at_rows, width:] = extra(lse_ref[at_rows, at])
-            d = d_heads[:, at].astype(BF16)
-            delta = jnp.sum(d.astype(F32) * o_ref[at_rows, at].astype(F32), axis=1, keepdims=True)
-            dox_ref[head, at_rows, :width] = d
-            dox_ref[head, at_rows, width:] = extra(jnp.broadcast_to(delta, (half, width)))
-
-
-def attn_prep(core, d_own, d_far, w_out, q, out, lse, width):
-    rows, columns = q.shape
-    heads = columns // width
-    return pl.pallas_call(
-        functools.partial(attn_prep_kernel, heads=heads, width=width),
-        out_shape=[jax.ShapeDtypeStruct((heads, rows, 2 * width), BF16)] * 2,
-        in_specs=[pl.BlockSpec(memory_space=pltpu.SMEM)] + vmem(6),
-        out_specs=vmem(2),
-        compiler_params=params(),
-        cost_estimate=COST,
-        name="attn_prep",
-    )(core, d_own, d_far, w_out, q, out, lse)
-
-
 def back_kernel(
     *refs, group, planes, all_planes, shard, kv_heads, repeat, width, coef, scale, sums
 ):
@@ -601,26 +591,41 @@
         del refs[:count]
         return out
 
-    prefix_ref, qx_ref, dox_ref, kv_ref = take(4)
-    h_own_ref, h_far_ref, a_own_ref, a_far_ref, heads_ref, up_ref = take(6)
-    if sums:
-        hid_ref, hid_came_ref, og_ref, og_came_ref, gate_ref = take(5)
-    dq_ref, grad_ref, h_ref, h_came_ref, a_ref, a_came_ref, heads_came_ref, up_came_ref = take(8)
-    if sums:
-        w_down_ref, w_gate_ref, w_out_ref = take(3)
-    own_ref, far_ref, xr_ref, zr_ref, first_ref = take(5)
-    send_x, recv_x, send_z, recv_z, send_first, recv_first = take(6)
-    swap_sems = take(4)
-    h_scratch, a_scratch = take(6), take(6)
-    rows = qx_ref.shape[1]
-    kv_width = kv_heads * width
     device = lax.axis_index("dp")
     member = device % group
     plane = member // 2
     last = planes - 1
+    prefix_ref, up_ref = take(2)
+    if sums:
+        hid_arrays = take(2)
+    count = 11 if sums else 4
+    arrays = take(count)
+    dq_ref, grad_ref, a_ref, a_came_ref, up_came_ref = take(5)
+    if sums:
+        w_down_ref, w_gate_ref, w_out_ref = take(3)
+    if sums:
+        hid_ref, hid_came_ref = hid_buffers = take(2)
+        hid_sems = take(1)[0]
+    buffers = take(count)
+    inputs = Staged(arrays, buffers, *take(1))
+    a_all_ref, qx_ref, dox_ref, kv_ref = buffers[:4]
+    if sums:
+        og_ref, og_came_ref, gate_ref, h_ref, h_came_ref, heads_ref, heads_came_ref = buffers[4:]
+    own_ref, far_ref, xr_ref, zr_ref, first_ref = take(5)
+    send_x, recv_x, send_z, recv_z, send_first, recv_first = take(6)
+    swap_sems = take(2)
+    a_scratch = take(6)
+    rows = qx_ref.shape[1]
+    kv_width = kv_heads * width
     if sums:
         gate_came_ref, send_gate, recv_gate = take(3)
-        down_sum, gate_sum, out_sum = (LineSum(take(6), device, plane, planes) for _ in range(3))
+        left = w_down_ref.shape[0]
+        rest = pl.ds(hid_arrays[0].shape[1] - left, left)
+        hid_inputs = Staged([h.at[:, rest] for h in hid_arrays], hid_buffers, hid_sems)
+        down_sum, out_sum = (LineSum(take(6), device, plane, planes) for _ in range(2))
+        piece = gate_came_ref.shape[2]
+        pieces = gate_ref.shape[1] // piece
+        gate_sums = [LineSum(take(6), device, plane, planes) for _ in range(pieces)]
     x_at = member % 2
     x_other = device + 1 - 2 * x_at
     inner = plane < last
@@ -628,6 +633,13 @@
 
     core, core_peer, _ = tensor_peers()
     x_peer = {"dp": x_other}
+    inputs.start(a_all_ref)
+    if sums:
+        hid_inputs.start()
+        inputs.start(*buffers[4:6])
+    inputs.start(*buffers[1:4])
+    if sums:
+        inputs.start(*buffers[6:])
     greet(
         [(x_peer, True), (core_peer, True), ({"dp": device + 2}, inner), ({"dp": device - 2}, plane > 0)]
     )
@@ -635,18 +647,19 @@
     def copy(src, dst, send, recv, there):
         return remote(src, dst, send, recv, {"dp": there})
 
-    def columns(own, far, keep, came, scratch):
-        return Columns(
-            own, far, keep, came, scratch, x_at, core, x_peer, core_peer, all_planes, shard
-        )
-
-    h_two = columns(h_own_ref, h_far_ref, h_ref, h_came_ref, h_scratch)
-    d_attn = columns(a_own_ref, a_far_ref, a_ref, a_came_ref, a_scratch)
-    heads_swap = copy(heads_ref, heads_came_ref, swap_sems[0], swap_sems[1], x_other)
-    up_swap = copy(up_ref, up_came_ref, swap_sems[2], swap_sems[3], x_other)
-
-    def gate_swap():
-        return copy(gate_ref, gate_came_ref, send_gate, recv_gate, x_other)
+    place = (x_at, core, x_peer, core_peer, all_planes, shard)
+    d_attn = Columns(a_all_ref, a_ref, a_came_ref, a_scratch, *place)
+    up_swap = copy(up_ref, up_came_ref, swap_sems[0], swap_sems[1], x_other)
+
+    def gate_swap(k):
+        part = gate_ref.at[:, pl.ds(k * piece, piece)]
+        return copy(part, gate_came_ref.at[k], send_gate.at[k], recv_gate.at[k], x_other)
+
+    def gate_start(k):
+        gate_swap(k).wait_recv()
+        part = gate_ref.at[:, pl.ds(k * piece, piece)]
+        gate_sums[k].fill_rows(h_ref, h_came_ref, part, gate_came_ref.at[k])
+        gate_sums[k].start()
 
     lane = lax.broadcasted_iota(jnp.int32, (rows, width), 1)
     minus = jnp.where(lane < 3, -1.0, 0.0).astype(BF16)
@@ -730,44 +743,56 @@
             pl.when(plane >= slot)(go)
 
     dq_ref[...] = jnp.zeros_like(dq_ref)
-    if sums:
-        gate_swap().start()
+    inputs.wait(a_all_ref)
+    d_attn.start()
+    if sums:
+        hid_inputs.wait()
+        inputs.wait(og_ref, og_came_ref)
         down_sum.fill_columns(hid_ref, hid_came_ref, og_ref, og_came_ref)
         down_sum.start()
-    h_two.start()
-    h_two.store()
+    inputs.wait(*buffers[1:4])
+    attend(last)
+    d_attn.forward()
+    if sums:
+        inputs.wait(*buffers[6:])
+        gate_swap(0).start()
     d_attn.store()
     pending = list(range(last, 0, -1))
-    waves = list(range(max(last - 1, 0)))
-    for count, slot in enumerate(range(last, -1, -1)):
+    waves = range(max(last - 1, 0))
+    for slot in range(last - 1, -1, -1):
         attend(slot)
-        if sums and count >= 1 and count - 1 < len(waves):
-            down_sum.wave(waves[count - 1])
-        if count >= 1 and slot >= 1:
+        if slot == last - 1:
+            if sums:
+                d_attn.over_core().wait_recv()
+                out_sum.fill_columns(heads_ref, heads_came_ref, a_ref, a_came_ref)
+                out_sum.start()
+                down_sum.wave(0)
+                gate_start(0)
+                gate_swap(1).start()
             pass_back(pending.pop(0))
-        if slot == min(1, last):
-            h_two.forward()
-            d_attn.start()
-            heads_swap.start()
+        if slot == last - 2:
             if sums:
-                gate_swap().wait_recv()
-                h_two.over_core().wait_recv()
-                gate_sum.fill_rows(h_ref, h_came_ref, gate_ref, gate_came_ref)
-                gate_sum.start()
-    up_swap.start()
+                for wave in waves[1:]:
+                    down_sum.wave(wave)
+                out_sum.wave(0)
+                gate_start(1)
+                gate_swap(2).start()
+                gate_sums[0].wave(0)
+            pass_back(pending.pop(0))
+    if sums:
+        for wave in waves[1:]:
+            out_sum.wave(wave)
+            gate_sums[0].wave(wave)
     while pending:
         pass_back(pending.pop(0))
+    if sums:
+        gate_start(2)
+    up_swap.start()
+    if sums:
+        for k in (1, 2):
+            for wave in waves:
+                gate_sums[k].wave(wave)
     dq_ref[...] = dq_ref[...] * scale
-    d_attn.forward()
-    heads_swap.wait_recv()
-    d_attn.over_core().wait_recv()
-    if sums:
-        out_sum.fill_columns(heads_ref, heads_came_ref, a_ref, a_came_ref)
-        out_sum.start()
-        for wave in waves:
-            gate_sum.wave(wave)
-        for wave in waves:
-            out_sum.wave(wave)
 
     far_swap(0).wait_recv()
     grad_ref[...] = own_ref[0].astype(F32) + xr_ref[0].astype(F32)
@@ -785,17 +810,16 @@
 
     if sums:
         down_sum.finish(w_down_ref)
-        gate_sum.finish(w_gate_ref)
         out_sum.finish(w_out_ref)
-        gate_swap().wait_send()
+        for k in range(pieces):
+            gate_sums[k].finish(w_gate_ref.at[:, pl.ds(k * piece, piece)])
+            gate_swap(k).wait_send()
+    else:
+        d_attn.over_core().wait_recv()
     up_swap.wait_recv()
     up_swap.wait_send()
-    heads_swap.wait_send()
-    for part in (h_two, d_attn):
-        part.over_x().wait_send()
-        part.over_core().wait_send()
-    if not sums:
-        h_two.over_core().wait_recv()
+    d_attn.over_x().wait_send()
+    d_attn.over_core().wait_send()
     for slot in range(planes):
         if slot <= 1:
             far_swap(slot).wait_send()
@@ -807,29 +831,37 @@
         pl.when(plane == 0)(lambda: from_first().wait_send())
 
 
-def back(prefix, qx, dox, kv_all, shared, grads, group, all_planes, shard, dims):
+def back(prefix, qx, dox, kv_all, shared, grads, group, all_planes, shard, pieces, dims):
     kv_heads, repeat, width = dims
     rows = qx.shape[1]
     columns = kv_heads * repeat * width
     planes = group // 2
     block = kv_all.shape[1:]
     dma = pltpu.SemaphoreType.DMA
-    heads, d_up = shared[4:]
+    d_up = shared[1]
     units = d_up.shape[1]
     cut_shape = jax.ShapeDtypeStruct((rows, all_planes * shard), BF16)
     out_shape = [jax.ShapeDtypeStruct((rows, columns), F32), jax.ShapeDtypeStruct(block, F32)]
-    out_shape += [cut_shape] * 4
-    out_shape += [jax.ShapeDtypeStruct(heads.shape, BF16), jax.ShapeDtypeStruct(d_up.shape, BF16)]
+    out_shape += [cut_shape] * 2 + [jax.ShapeDtypeStruct(d_up.shape, BF16)]
     scratch = [pltpu.VMEM((planes,) + block, BF16)] * 4 + [pltpu.VMEM(block, BF16)]
-    scratch += [dma((planes,))] * 4 + [dma, dma] + [dma] * 4
-    scratch += Columns.scratch(rows // 2, all_planes * shard) * 2
-    args = [prefix, qx, dox, kv_all, *shared]
+    scratch += [dma((planes,))] * 4 + [dma, dma] + [dma] * 2
+    scratch += Columns.scratch(rows // 2, all_planes * shard)
+    d_attn, d_up = shared
+    staged = [d_attn, qx, dox, kv_all]
+    args = [prefix, d_up]
+    first = []
     if grads is not None:
-        args += grads
-        shapes = (units, shard), (shard, units), (heads.shape[1], shard)
+        args += grads[:2]
+        staged += grads[2:]
+        first = [pltpu.VMEM((rows, units // pieces), BF16)] * 2 + [dma((2,))]
+    args += staged
+    scratch = first + Staged.scratch(staged) + scratch
+    if grads is not None:
+        piece = units // pieces
+        shapes = (piece, shard), (shard, units), (columns, shard)
         out_shape += [jax.ShapeDtypeStruct(s, F32) for s in shapes]
-        scratch += [pltpu.VMEM((rows, units), BF16), dma, dma]
-        for shape in shapes:
+        scratch += [pltpu.VMEM((pieces, rows, piece), BF16)] + [dma((pieces,))] * 2
+        for shape in [(piece, shard), (columns, shard)] + [(shard, piece)] * pieces:
             scratch += LineSum.scratch(planes, shape)
     return pl.pallas_call(
         functools.partial(
@@ -846,8 +878,8 @@
             sums=grads is not None,
         ),
         out_shape=out_shape,
-        in_specs=[smem()] + vmem(8) + [pl.BlockSpec(memory_space=pl.ANY)] + vmem(len(args) - 10),
-        out_specs=vmem(7) + [pl.BlockSpec(memory_space=pl.ANY)] + vmem(len(out_shape) - 8),
+        in_specs=[smem()] + [ANYWHERE] * (len(args) - 1),
+        out_specs=vmem(4) + [pl.BlockSpec(memory_space=pl.ANY)] + vmem(len(out_shape) - 5),
         scratch_shapes=scratch,
         compiler_params=pltpu.CompilerParams(
             vmem_limit_bytes=BACK_VMEM_LIMIT, collective_id=1, has_side_effects=True
@@ -861,214 +893,336 @@
     return pl.BlockSpec(memory_space=pltpu.SMEM)
 
 
-def cut_kernel(at_ref, *refs, halves, planes, shard):
-    x_at, core = at_ref[0], at_ref[1]
-    keep_ref, send_ref = refs[-2:]
-    half = send_ref.shape[0]
-    for z in range(planes):
-        to = slice(z * shard, (z + 1) * shard)
-        keep = pl.ds(pl.multiple_of((2 * z + x_at) * shard, shard), shard)
-        send = pl.ds(pl.multiple_of((2 * z + 1 - x_at) * shard, shard), shard)
-        if halves:
-            own_ref, far_ref = refs[:2]
-            keep_ref[pl.ds(pl.multiple_of(core * half, half), half), to] = own_ref[:, keep]
-            keep_ref[pl.ds(pl.multiple_of((1 - core) * half, half), half), to] = far_ref[:, keep]
-            send_ref[:, to] = own_ref[:, send]
-        else:
-            keep_ref[:, to] = refs[0][:, keep]
-            send_ref[:, to] = refs[0][pl.ds(pl.multiple_of(core * half, half), half), send]
-
-
-def cut(x_at, core, parts, planes, shard, join):
-    halves = len(parts) == 2
-    half = parts[0].shape[0] // (1 if halves else 2)
-    if shard % 128:
-        whole = join(*parts) if halves else parts[0]
-        own = parts[0] if halves else lax.dynamic_slice_in_dim(whole, core * half, half, 0)
-
-        def columns(value, side):
-            view = value.reshape(value.shape[0], planes, 2, shard)
-            return lax.dynamic_index_in_dim(view, side, 2, keepdims=False).reshape(
-                value.shape[0], planes * shard
-            )
-
-        return columns(whole, x_at), columns(own, 1 - x_at)
+def out_kernel(*refs, planes, shard, blocks):
+    refs = list(refs)
+
+    def take(count):
+        out = refs[:count]
+        del refs[:count]
+        return out
+
+    arrays = take(4)
+    gain_ref, w_down_ref = take(2)
+    middle_ref, h_ref, d_hidden_out, og_keep, og_came, heads_came = take(6)
+    buffers = take(4)
+    heads_ref, w_ref, og_ref, x_ref = buffers
+    inputs = Staged(arrays, buffers, *take(1))
+    d_hidden_ref, d_hidden_sem = take(2)
+    down_buf, down_sems, mine_ref, h_send, h_recv, heads_send, heads_recv = take(7)
+    scratch = refs
+    device = lax.axis_index("dp")
+    core, core_peer, y_peer = tensor_peers()
+    x_at = device % 2
+    x_peer = {"dp": device + 1 - 2 * x_at}
+    half = middle_ref.shape[0]
+    total = TensorSum(scratch[:8], mine_ref, core, core_peer, y_peer)
+    chunks, width = total.chunks, total.width
+    place = (x_at, core, x_peer, core_peer, planes, shard)
+    og = Columns(og_ref, og_keep, og_came, scratch[8:14], *place)
+    tiles = down_sems.shape[0]
+    tile = down_buf.shape[0] // tiles
+
+    def load(t):
+        at = pl.ds(t * tile, tile)
+        return pltpu.make_async_copy(w_down_ref.at[at, :], down_buf.at[at, :], down_sems.at[t])
+
+    inputs.start()
+    for t in range(tiles):
+        load(t).start()
+    greet([(x_peer, True), (core_peer, True), (y_peer, True)])
+    heads_swap = remote(heads_ref, heads_came, heads_send, heads_recv, x_peer)
+    inputs.wait(heads_ref, w_ref)
+    heads_swap.start()
+    for i in range(chunks):
+        total.add(i, dot(heads_ref[...], w_ref[:, i * width : (i + 1) * width]))
+    inputs.wait(og_ref)
+    og.start()
+    og.store()
+    for t in range(tiles):
+        at = slice(t * tile, (t + 1) * tile)
+        load(t).wait()
+        d_hidden_ref[:, at] = dot(og_ref[...], down_buf[at, :], NT)
+    d_hidden_copy = pltpu.make_async_copy(d_hidden_ref, d_hidden_out, d_hidden_sem)
+    d_hidden_copy.start()
+    mine = rows_of(core, half)
+    inputs.wait(x_ref)
+    for i in range(chunks):
+        at = slice(i * width, (i + 1) * width)
+        middle_ref[:, at] = x_ref[mine, at].astype(F32) + total.total(i)
+    step = half // blocks
+
+    def to_core(b):
+        rows = h_ref.at[pl.ds(pl.multiple_of(core * half + b * step, step), step), :]
+        return remote(rows, rows, h_send.at[b], h_recv.at[b], core_peer)
+
+    for b in range(blocks):
+        v = middle_ref[b * step : (b + 1) * step, :]
+        r = lax.rsqrt(jnp.mean(v * v, axis=1, keepdims=True) + EPS)
+        at = pl.ds(pl.multiple_of(core * half + b * step, step), step)
+        h_ref[at, :] = (v * r * gain_ref[...]).astype(BF16)
+        to_core(b).start()
+    og.forward()
+    og.finish()
+    d_hidden_copy.wait()
+    heads_swap.wait_recv()
+    heads_swap.wait_send()
+    for b in range(blocks):
+        to_core(b).wait_recv()
+        to_core(b).wait_send()
+    total.finish()
+
+
+def attention_out(heads, w_out, x, gain, out_grad, w_down, planes, shard):
+    rows, model = x.shape
+    half = rows // 2
+    units = w_down.shape[0]
+    chunks, blocks = 4, 4
+    tiles = units // math.gcd(units, 256)
+    dma = pltpu.SemaphoreType.DMA
+    cut_shape = jax.ShapeDtypeStruct((rows, planes * shard), BF16)
     return pl.pallas_call(
-        functools.partial(cut_kernel, halves=halves, planes=planes, shard=shard),
+        functools.partial(out_kernel, planes=planes, shard=shard, blocks=blocks),
         out_shape=[
-            jax.ShapeDtypeStruct((2 * half, planes * shard), BF16),
-            jax.ShapeDtypeStruct((half, planes * shard), BF16),
-        ],
-        in_specs=[smem()] + vmem(len(parts)),
-        out_specs=vmem(2),
-        compiler_params=params(),
+            jax.ShapeDtypeStruct((half, model), F32),
+            jax.ShapeDtypeStruct((rows, model), BF16),
+            jax.ShapeDtypeStruct((rows, units), F32),
+        ]
+        + [cut_shape] * 2
+        + [jax.ShapeDtypeStruct(heads.shape, BF16)],
+        in_specs=[ANYWHERE] * 4 + vmem(1) + [ANYWHERE],
+        out_specs=vmem(2) + [ANYWHERE] + vmem(3),
+        scratch_shapes=Staged.scratch([heads, w_out, out_grad, x])
+        + [pltpu.VMEM((rows, units), F32), dma]
+        + [pltpu.VMEM((units, model), BF16), dma((tiles,))]
+        + [pltpu.VMEM((2, rows, model // chunks), F32), dma((blocks,)), dma((blocks,)), dma, dma]
+        + TensorSum.scratch(chunks, half, model // chunks)
+        + Columns.scratch(half, planes * shard),
+        compiler_params=pltpu.CompilerParams(
+            vmem_limit_bytes=VMEM_LIMIT, collective_id=4, has_side_effects=True
+        ),
         cost_estimate=COST,
-        name="cut",
-    )(jnp.stack([x_at, core]).astype(jnp.int32), *parts)
-
-
-def norm_kernel(core_ref, both_ref, y_ref, x_ref, gain_ref, middle_ref, h_ref):
-    half = both_ref.shape[0]
-    x = x_ref[pl.ds(pl.multiple_of(core_ref[0] * half, half), half), :].astype(F32)
-    middle = x + both_ref[...].astype(F32) + y_ref[...].astype(F32)
-    middle_ref[...] = middle
-    r = lax.rsqrt(jnp.mean(middle * middle, axis=1, keepdims=True) + EPS)
-    h_ref[...] = (middle * r * gain_ref[...]).astype(BF16)
-
-
-def norm_forward(core, both, came, x, gain):
-    return pl.pallas_call(
-        norm_kernel,
-        out_shape=[jax.ShapeDtypeStruct(both.shape, F32), jax.ShapeDtypeStruct(both.shape, BF16)],
-        in_specs=[smem()] + vmem(4),
-        out_specs=vmem(2),
-        compiler_params=params(),
-        cost_estimate=COST,
-        name="norm_forward",
-    )(core, both, came, x, gain)
-
-
-def mlp_kernel(core_ref, own_ref, far_ref, gate_ref, up_ref, d_ref, hidden_ref, d_gate_ref, d_up_ref):
-    half = own_ref.shape[0]
-    core = core_ref[0]
-    for ref, at_core in ((own_ref, core), (far_ref, 1 - core)):
-        at = pl.ds(pl.multiple_of(at_core * half, half), half)
-        gate = dot(ref[...], gate_ref[...])
-        up = dot(ref[...], up_ref[...])
+        name="attention_out",
+    )(heads, w_out, out_grad, x, gain, w_down)
+
+
+def middle_kernel(*refs, planes, shard, heads, width, pieces, blocks, sums):
+    refs = list(refs)
+
+    def take(count):
+        out = refs[:count]
+        del refs[:count]
+        return out
+
+    w_gate_ref, w_up_ref, gain_ref = take(3)
+    count = 10 if sums else 8
+    arrays = take(count)
+    outs = take(3)
+    hid_came_ref, a_ref, gain_out_ref, qx_ref, dox_ref, h_keep, h_came = take(7)
+    if sums:
+        down_outs = take(pieces - 1)
+    buffers = take(count)
+    inputs = Staged(arrays, buffers, *take(1))
+    h_ref, d_ref, middle_ref, og_ref, w_out_ref, q_ref, o_ref, lse_ref = buffers[:8]
+    if sums:
+        og_keep, og_came = buffers[8:]
+    out_buffers = take(3)
+    hid_ref, gate_ref, up_ref = out_buffers
+    outputs = Staged(outs, out_buffers, *take(1), out=True)
+    gate_buf, up_buf, load_sems, c_ref, mine_ref = take(5)
+    hid_send, hid_recv, a_send, a_recv = take(4)
+    sum_scratch, h_scratch = take(8), take(6)
+    device = lax.axis_index("dp")
+    core, core_peer, y_peer = tensor_peers()
+    plane = device // 2
+    x_at = device % 2
+    x_peer = {"dp": device + 1 - 2 * x_at}
+    meets = [(x_peer, True), (core_peer, True), (y_peer, True)]
+    h_two = Columns(h_ref, h_keep, h_came, h_scratch, x_at, core, x_peer, core_peer, planes, shard)
+    half = middle_ref.shape[0]
+    total = TensorSum(sum_scratch, mine_ref, core, core_peer, y_peer)
+    chunks, columns = total.chunks, total.width
+    units = hid_ref.shape[1]
+    piece = units // pieces
+    tile = 256
+    tiles = units // tile
+    if sums:
+        downs = [LineSum(take(6), device, plane, planes) for _ in range(pieces - 1)]
+        meets += [({"dp": device + 2}, plane < planes - 1), ({"dp": device - 2}, plane > 0)]
+
+    def loads(t):
+        at = pl.ds(t * tile, tile)
+        return (
+            pltpu.make_async_copy(w_gate_ref.at[:, at], gate_buf.at[:, at], load_sems.at[2 * t]),
+            pltpu.make_async_copy(w_up_ref.at[:, at], up_buf.at[:, at], load_sems.at[2 * t + 1]),
+        )
+
+    inputs.start(h_ref)
+    for t in range(tiles):
+        for load in loads(t):
+            load.start()
+        if t == 0:
+            inputs.start(d_ref)
+    inputs.start(*buffers[2:])
+    greet(meets)
+    inputs.wait(h_ref)
+
+    def swap(k):
+        at = pl.ds(k * piece, piece)
+        return remote(hid_ref.at[:, at], hid_came_ref.at[:, at], hid_send.at[k], hid_recv.at[k], x_peer)
+
+    for t in range(tiles):
+        for load in loads(t):
+            load.wait()
+        if t == 0:
+            inputs.wait(d_ref)
+        at = slice(t * tile, (t + 1) * tile)
+        gate = dot(h_ref[...], gate_buf[:, at])
+        up = dot(h_ref[...], up_buf[:, at])
         sig = 1.0 / (1.0 + jnp.exp(-gate))
         silu = gate * sig
-        d = d_ref[at, :]
-        hidden_ref[at, :] = (silu * up).astype(BF16)
-        d_up_ref[at, :] = (d * silu).astype(BF16)
-        d_gate_ref[at, :] = (d * up * (sig * (1.0 + gate * (1.0 - sig)))).astype(BF16)
-
-
-def mlp(core, own, far, w_gate, w_up, d_hidden):
-    half, model = own.shape
-    units = w_gate.shape[1]
-    tile = math.gcd(units, 256)
-    rows_spec = pl.BlockSpec((half, model), lambda i: (0, 0))
-    weight_spec = pl.BlockSpec((model, tile), lambda i: (0, i))
-    unit_spec = pl.BlockSpec((2 * half, tile), lambda i: (0, i))
-    return pl.pallas_call(
-        mlp_kernel,
-        out_shape=[jax.ShapeDtypeStruct((2 * half, units), BF16)] * 3,
-        grid=(units // tile,),
-        in_specs=[smem(), rows_spec, rows_spec, weight_spec, weight_spec, unit_spec],
-        out_specs=[unit_spec] * 3,
-        compiler_params=params(),
-        cost_estimate=COST,
-        name="mlp",
-    )(core, own, far, w_gate, w_up, d_hidden)
-
-
-def d_middle_kernel(
-    hid_ref,
-    d_gate_ref,
-    d_up_ref,
-    w_gate_ref,
-    w_up_ref,
-    middle_ref,
-    add_ref,
-    gain_ref,
-    hid_came_ref,
-    own_ref,
-    far_ref,
-    gain_out_ref,
-    gate_buf,
-    up_buf,
-    load_sems,
-    c_ref,
-    mine_ref,
-    hid_send,
-    hid_recv,
-    far_send,
-    far_recv,
-    *scratch,
-    blocks,
-):
-    device = lax.axis_index("dp")
-    core, core_peer, y_peer = tensor_peers()
-    x_peer = {"dp": device + 1 - 2 * (device % 2)}
-    half = middle_ref.shape[0]
-    total = TensorSum(scratch, mine_ref, core, core_peer, y_peer)
-    chunks, width = total.chunks, total.width
-
-    def loads(i):
-        at = pl.ds(i * width, width)
-        return (
-            pltpu.make_async_copy(w_gate_ref.at[at, :], gate_buf.at[i], load_sems.at[2 * i]),
-            pltpu.make_async_copy(w_up_ref.at[at, :], up_buf.at[i], load_sems.at[2 * i + 1]),
-        )
+        d = d_ref[:, at]
+        hid_ref[:, at] = (silu * up).astype(BF16)
+        up_ref[:, at] = (d * silu).astype(BF16)
+        gate_ref[:, at] = (d * up * (sig * (1.0 + gate * (1.0 - sig)))).astype(BF16)
+        if (t + 1) * tile % piece == 0:
+            swap((t + 1) * tile // piece - 1).start()
+
+    outputs.start()
+    inputs.wait(*buffers[2:])
+
+    def down_start(k):
+        if sums:
+            at = pl.ds(k * piece, piece)
+            swap(k).wait_recv()
+            downs[k].fill_columns(hid_ref.at[:, at], hid_came_ref.at[:, at], og_keep, og_came)
+            downs[k].start()
+
+    def down_wave(k, wave):
+        if sums and wave < planes - 2:
+            downs[k].wave(wave)
 
     for i in range(chunks):
-        for load in loads(i):
-            load.start()
-    greet([(x_peer, True), (core_peer, True), (y_peer, True)])
-    swap = remote(hid_ref, hid_came_ref, hid_send, hid_recv, x_peer)
-    swap.start()
+        at = slice(i * columns, (i + 1) * columns)
+        total.add(i, dot(gate_ref[...], gate_buf[at, :], NT) + dot(up_ref[...], up_buf[at, :], NT))
+        if i == chunks - 2:
+            down_start(0)
     for i in range(chunks):
-        for load in loads(i):
-            load.wait()
-        total.add(i, dot(d_gate_ref[...], gate_buf[i], NT) + dot(d_up_ref[...], up_buf[i], NT))
-    for i in range(chunks):
-        c_ref[:, i * width : (i + 1) * width] = total.total(i)
+        if i == 1:
+            down_start(1)
+            h_two.start()
+        if i == 2:
+            down_wave(0, 0)
+        c_ref[:, i * columns : (i + 1) * columns] = total.total(i)
+    down_wave(0, 1)
 
     step = half // blocks
 
     def to_core(b):
-        at = slice(b * step, (b + 1) * step)
-        return remote(own_ref.at[at, :], far_ref.at[at, :], far_send.at[b], far_recv.at[b], core_peer)
+        rows = a_ref.at[pl.ds(pl.multiple_of(core * half + b * step, step), step), :]
+        return remote(rows, rows, a_send.at[b], a_recv.at[b], core_peer)
 
     gain_out_ref[...] = jnp.zeros_like(gain_out_ref)
     for b in range(blocks):
         at = slice(b * step, (b + 1) * step)
-        add_at = pl.ds(pl.multiple_of(core * half + b * step, step), step)
+        whole_at = pl.ds(pl.multiple_of(core * half + b * step, step), step)
         c = c_ref[at, :]
         v = middle_ref[at, :]
         r = lax.rsqrt(jnp.mean(v * v, axis=1, keepdims=True) + EPS)
         n = v * r
         gain_out_ref[...] += jnp.sum(c * n, axis=0, keepdims=True)
         gc = c * gain_ref[...]
-        d = r * (gc - n * jnp.mean(n * gc, axis=1, keepdims=True)) + add_ref[add_at, :].astype(F32)
-        own_ref[at, :] = d.astype(BF16)
+        d = r * (gc - n * jnp.mean(n * gc, axis=1, keepdims=True)) + og_ref[whole_at, :].astype(F32)
+        a_ref[whole_at, :] = d.astype(BF16)
         to_core(b).start()
+
+    lane = lax.broadcasted_iota(jnp.int32, (half, width), 1)
+
+    def extra(value):
+        a, b, c = split_three(value)
+        return jnp.where(lane == 0, a, jnp.where(lane == 1, b, jnp.where(lane == 2, c, 0.0))).astype(BF16)
+
+    def prepare(which):
+        at_rows = rows_of(which, half)
+        d_heads = dot(a_ref[at_rows, :], w_out_ref[...], NT)
+        for head in range(heads):
+            at = slice(head * width, (head + 1) * width)
+            qx_ref[head, at_rows, :width] = q_ref[at_rows, at]
+            qx_ref[head, at_rows, width:] = extra(lse_ref[at_rows, at])
+            d = d_heads[:, at].astype(BF16)
+            delta = jnp.sum(d.astype(F32) * o_ref[at_rows, at].astype(F32), axis=1, keepdims=True)
+            dox_ref[head, at_rows, :width] = d
+            dox_ref[head, at_rows, width:] = extra(jnp.broadcast_to(delta, (half, width)))
+
+    down_wave(1, 0)
+    h_two.store()
+    prepare(core)
+    h_two.forward()
     for b in range(blocks):
         to_core(b).wait_recv()
+    prepare(1 - core)
+    down_wave(1, 1)
+    for b in range(blocks):
         to_core(b).wait_send()
     total.finish()
-    swap.wait_recv()
-    swap.wait_send()
-
-
-def d_middle_of(hidden, d_gate, d_up, w_gate, w_up, middle, out_grad, gain):
+    h_two.finish()
+    outputs.wait()
+    for k in range(pieces):
+        if k == pieces - 1 or not sums:
+            swap(k).wait_recv()
+        swap(k).wait_send()
+    if sums:
+        for k in range(pieces - 1):
+            for wave in range(2, planes - 2):
+                downs[k].wave(wave)
+            downs[k].finish(down_outs[k])
+
+
+def middle_of(w_gate, w_up, h_two, d_hidden, middle, out_grad, gain, w_out, q, out, lse, cuts, pieces, planes, shard, width):
     half, model = middle.shape
-    units = hidden.shape[1]
+    rows, units = d_hidden.shape
+    columns = q.shape[1]
+    heads = columns // width
     chunks, blocks = 4, 4
-    width = model // chunks
     dma = pltpu.SemaphoreType.DMA
-    anywhere = pl.BlockSpec(memory_space=pl.ANY)
+    staged = [h_two, d_hidden, middle, out_grad, w_out, q, out, lse] + ([] if cuts is None else cuts)
+    args = [w_gate, w_up, gain, *staged]
+    unit_shape = jax.ShapeDtypeStruct((rows, units), BF16)
+    out_shape = [unit_shape] * 4 + [
+        jax.ShapeDtypeStruct((rows, model), BF16),
+        jax.ShapeDtypeStruct((1, model), F32),
+    ]
+    out_shape += [jax.ShapeDtypeStruct((heads, rows, 2 * width), BF16)] * 2
+    out_shape += [jax.ShapeDtypeStruct((rows, planes * shard), BF16)] * 2
+    scratch = Staged.scratch(staged) + Staged.scratch([unit_shape] * 3)
+    scratch += [pltpu.VMEM((model, units), BF16)] * 2 + [dma((2 * units // 256,))]
+    scratch += [pltpu.VMEM((half, model), F32), pltpu.VMEM((2, rows, model // chunks), F32)]
+    scratch += [dma((pieces,))] * 2 + [dma((blocks,))] * 2
+    scratch += TensorSum.scratch(chunks, half, model // chunks)
+    scratch += Columns.scratch(half, planes * shard)
+    if cuts is not None:
+        out_shape += [jax.ShapeDtypeStruct((units // pieces, shard), F32)] * (pieces - 1)
+        scratch += LineSum.scratch(planes, (units // pieces, shard)) * (pieces - 1)
     return pl.pallas_call(
-        functools.partial(d_middle_kernel, blocks=blocks),
-        out_shape=[
-            jax.ShapeDtypeStruct(hidden.shape, BF16),
-            jax.ShapeDtypeStruct((half, model), BF16),
-            jax.ShapeDtypeStruct((half, model), BF16),
-            jax.ShapeDtypeStruct((1, model), F32),
-        ],
-        in_specs=vmem(3) + [anywhere] * 2 + vmem(3),
-        out_specs=vmem(4),
-        scratch_shapes=[pltpu.VMEM((chunks, width, units), BF16)] * 2
-        + [dma((2 * chunks,)), pltpu.VMEM((half, model), F32)]
-        + [pltpu.VMEM((2, 2 * half, width), F32)]
-        + [dma, dma, dma((blocks,)), dma((blocks,))]
-        + TensorSum.scratch(chunks, half, width),
+        functools.partial(
+            middle_kernel,
+            planes=planes,
+            shard=shard,
+            heads=heads,
+            width=width,
+            pieces=pieces,
+            blocks=blocks,
+            sums=cuts is not None,
+        ),
+        out_shape=out_shape,
+        in_specs=[ANYWHERE] * 2 + vmem(1) + [ANYWHERE] * len(staged),
+        out_specs=[ANYWHERE] * 3 + vmem(len(out_shape) - 3),
+        scratch_shapes=scratch,
         compiler_params=pltpu.CompilerParams(
-            vmem_limit_bytes=VMEM_LIMIT, collective_id=2, has_side_effects=True
+            vmem_limit_bytes=BACK_VMEM_LIMIT, collective_id=2, has_side_effects=True
         ),
         cost_estimate=COST,
-        name="d_middle",
-    )(hidden, d_gate, d_up, w_gate, w_up, middle, out_grad, gain)
+        name="middle",
+    )(*args)
 
 
 def through_rope(d_ref, raw_ref, gain, cos, sin, out_ref, width, plain):
@@ -1088,7 +1242,7 @@
     return total
 
 
-def front_kernel(*refs, dp_size, planes, chunks, sums):
+def front_kernel(*refs, dp_size, planes, shard, chunks, sums):
     refs = list(refs)
 
     def take(count):
@@ -1096,16 +1250,21 @@
         del refs[:count]
         return out
 
-    dq_in, dkv_in, q_raw, k_raw, q_gain, k_gain, cos_ref, sin_ref = take(8)
-    w_q, w_k, w_v, x_ref, mlp_gain_ref, middle_ref, hid_ref, w_down_ref = take(8)
-    if sums:
-        one_ref, one_came, two_ref, two_came, up_ref, up_came = take(6)
-    d_one, block_out, gains, dq_ref, dq_came, dkv_ref, dkv_came = take(7)
+    q_gain, k_gain, mlp_gain_ref, w_down_ref = take(4)
+    count = 17 if sums else 13
+    arrays = take(count)
+    d_one, block_out, gains, dq_ref, dq_came, dkv_ref, dkv_came, one_ref, one_came = take(9)
     if sums:
         w_up_out, w_q_out, w_kv_out = take(3)
+    buffers = take(count)
+    inputs = Staged(arrays, buffers, *take(1))
+    dkv_in, k_raw, cos_ref, sin_ref, dq_in, q_raw, one_all = buffers[:7]
+    x_ref, w_q, w_k, w_v, hid_ref, middle_ref = buffers[7:13]
+    if sums:
+        two_ref, two_came, up_ref, up_came = buffers[13:]
     mine, down_buf, down_sems, gain_came = take(4)
     swap_sems, one_sems, block_sems, gain_sems = take(4), take(2), take(2), take(2)
-    one_sum_scratch, out_sum_scratch = take(8), take(8)
+    one_sum_scratch, out_sum_scratch, one_scratch = take(8), take(8), take(6)
     half = x_ref.shape[0] // 2
     model = x_ref.shape[1]
     width = model // chunks
@@ -1114,8 +1273,10 @@
 
     device = lax.axis_index("dp")
     core, core_peer, y_peer = tensor_peers()
-    x_peer = {"dp": device + 1 - 2 * (device % 2)}
+    x_at = device % 2
+    x_peer = {"dp": device + 1 - 2 * x_at}
     plane = device // 2
+    one = Columns(one_all, one_ref, one_came, one_scratch, x_at, core, x_peer, core_peer, planes, shard)
     bits = [1 << i for i in range(dp_size.bit_length() - 1)]
     dp_peers = [{"dp": device + bit - 2 * bit * ((device // bit) % 2)} for bit in bits]
     gain_peers = [core_peer, y_peer] + dp_peers
@@ -1124,16 +1285,24 @@
         up_sum, q_sum, kv_sum = (LineSum(take(6), device, plane, planes) for _ in range(3))
         meets += [({"dp": device + 2}, plane < planes - 1), ({"dp": device - 2}, plane > 0)]
 
+    narrow = down_buf.shape[2]
+    parts = model // narrow
+
     def load(i):
-        at = pl.ds(i * width, width)
+        at = pl.ds(i * narrow, narrow)
         return pltpu.make_async_copy(w_down_ref.at[:, at], down_buf.at[i % 2], down_sems.at[i])
 
+    if sums:
+        inputs.start(*buffers[13:])
+    inputs.start(*buffers[:13])
     load(0).start()
     load(1).start()
     greet(meets)
     if sums:
+        inputs.wait(*buffers[13:])
         up_sum.fill_rows(two_ref, two_came, up_ref, up_came)
         up_sum.start()
+    inputs.wait(*buffers[:7])
     cos, sin = cos_ref[...], sin_ref[...]
     k_total = through_rope(dkv_in, k_raw, k_gain[...], cos, sin, dkv_ref, head, kv_width)
     kv_swap = remote(dkv_ref, dkv_came, swap_sems[0], swap_sems[1], x_peer)
@@ -1141,6 +1310,8 @@
     q_total = through_rope(dq_in, q_raw, q_gain[...], cos, sin, dq_ref, head, 0)
     q_swap = remote(dq_ref, dq_came, swap_sems[2], swap_sems[3], x_peer)
     q_swap.start()
+    one.start()
+    inputs.wait(*buffers[7:13])
 
     one_sum = TensorSum(one_sum_scratch, mine, core, core_peer, y_peer)
     x = x_ref[...].astype(F32)
@@ -1171,17 +1342,20 @@
 
     gain_swap(0).start()
 
-    out_sum = TensorSum(out_sum_scratch, mine, core, core_peer, y_peer)
-    for i in range(chunks):
+    out_sum = TensorSum(out_sum_scratch, mine.at[:, :, pl.ds(0, narrow)], core, core_peer, y_peer)
+    for i in range(parts):
         load(i).wait()
         out_sum.add(i, dot(hid_ref[...], down_buf[i % 2]))
-        if i + 2 < chunks:
+        if i + 2 < parts:
             load(i + 2).start()
     gain_add(0)
+    one.store()
+    one.forward()
     if sums:
         if planes > 2:
             up_sum.wave(0)
         kv_swap.wait_recv()
+        one.over_core().wait_recv()
         kv_sum.fill_rows(one_ref, one_came, dkv_ref, dkv_came)
         kv_sum.start()
     gain_add(1)
@@ -1205,8 +1379,8 @@
             up_sum.wave(wave)
     for k in range(3, len(gain_peers)):
         gain_add(k)
-    for i in range(chunks):
-        at = slice(i * width, (i + 1) * width)
+    for i in range(parts):
+        at = slice(i * narrow, (i + 1) * narrow)
         block_out[mine_rows, at] = (middle_ref[:, at] + out_sum.total(i)).astype(BF16)
     give(block_out, block_sems).start()
     if sums:
@@ -1219,6 +1393,9 @@
     else:
         kv_swap.wait_recv()
         q_swap.wait_recv()
+        one.over_core().wait_recv()
+    one.over_x().wait_send()
+    one.over_core().wait_send()
     kv_swap.wait_send()
     q_swap.wait_send()
     for out, sems in ((d_one, one_sems), (block_out, block_sems)):
@@ -1230,7 +1407,7 @@
     out_sum.finish()
 
 
-def front(dq, dkv, q_raw, k_raw, q_gain, k_gain, cos, sin, weights, x, mlp_gain, middle, hidden, w_down, grads, dp_size, shard):
+def front(dq, dkv, q_raw, k_raw, q_gain, k_gain, cos, sin, h_one, weights, x, mlp_gain, middle, hidden, w_down, grads, dp_size, shard):
     rows, model = x.shape
     half = rows // 2
     planes = dp_size // 2
@@ -1240,26 +1417,37 @@
     stages = dp_size.bit_length() + 1
     dma = pltpu.SemaphoreType.DMA
     gains = (2 * model + 2 * cos.shape[1],)
-    args = [dq, dkv, q_raw, k_raw, q_gain, k_gain, cos, sin, *weights, x, mlp_gain, middle, hidden, w_down]
+    staged = [dkv, k_raw, cos, sin, dq, q_raw, h_one, x, *weights, hidden, middle]
+    if grads is not None:
+        staged += grads
+    args = [q_gain, k_gain, mlp_gain, w_down, *staged]
+    cut_shape = jax.ShapeDtypeStruct((rows, planes * shard), BF16)
     whole = jax.ShapeDtypeStruct((rows, model), BF16)
     q_shape, kv_shape = jax.ShapeDtypeStruct(dq.shape, BF16), jax.ShapeDtypeStruct(dkv.shape, BF16)
     out_shape = [whole, whole, jax.ShapeDtypeStruct((stages + 1, 1) + gains, F32)]
-    out_shape += [q_shape, q_shape, kv_shape, kv_shape]
-    scratch = [pltpu.VMEM((2, rows, width), F32), pltpu.VMEM((2, units, width), BF16), dma((chunks,))]
+    out_shape += [q_shape, q_shape, kv_shape, kv_shape, cut_shape, cut_shape]
+    scratch = Staged.scratch(staged)
+    scratch += [pltpu.VMEM((2, rows, width), F32)]
+    scratch += [pltpu.VMEM((2, units, width // 2), BF16), dma((2 * chunks,))]
     scratch += [pltpu.VMEM((stages, 1) + gains, F32)]
     scratch += [dma] * 8 + [dma((stages,))] * 2
-    scratch += TensorSum.scratch(chunks, half, width) * 2
+    scratch += TensorSum.scratch(chunks, half, width) + TensorSum.scratch(2 * chunks, half, width // 2)
+    scratch += Columns.scratch(half, planes * shard)
     if grads is not None:
-        args += grads
         for columns in (units, dq.shape[1], dkv.shape[1]):
             out_shape.append(jax.ShapeDtypeStruct((shard, columns), F32))
             scratch += LineSum.scratch(planes, (shard, columns))
     return pl.pallas_call(
         functools.partial(
-            front_kernel, dp_size=dp_size, planes=planes, chunks=chunks, sums=grads is not None
+            front_kernel,
+            dp_size=dp_size,
+            planes=planes,
+            shard=shard,
+            chunks=chunks,
+            sums=grads is not None,
         ),
         out_shape=out_shape,
-        in_specs=vmem(15) + [pl.BlockSpec(memory_space=pl.ANY)] + vmem(len(args) - 16),
+        in_specs=vmem(3) + [ANYWHERE] * (len(args) - 3),
         out_specs=vmem(len(out_shape)),
         scratch_shapes=scratch,
         compiler_params=pltpu.CompilerParams(
@@ -1270,34 +1458,29 @@
     )(*args)
 
 
-def last_kernel(core_ref, d_ref, x_ref, gain_ref, own_ref, far_ref, out_ref, *, steps):
+def last_kernel(d_ref, x_ref, gain_ref, add_ref, out_ref):
     c = d_ref[...].astype(F32)
     x = x_ref[...].astype(F32)
     r = lax.rsqrt(jnp.mean(x * x, axis=1, keepdims=True) + EPS)
     n = x * r
     gc = c * gain_ref[...]
-    d = r * (gc - n * jnp.mean(n * gc, axis=1, keepdims=True))
-    mine = (pl.program_id(0) // steps) == core_ref[0]
-    out_ref[...] = d + jnp.where(mine, own_ref[...].astype(F32), far_ref[...].astype(F32))
-
-
-def tokens_grad_of(core, d_one, x, gain, own, far):
+    out_ref[...] = add_ref[...].astype(F32) + r * (gc - n * jnp.mean(n * gc, axis=1, keepdims=True))
+
+
+def tokens_grad_of(d_one, x, gain, add):
     rows, model = x.shape
-    half = rows // 2
-    tile = math.gcd(half, 128)
-    steps = half // tile
+    tile = math.gcd(rows, 128)
     row_spec = pl.BlockSpec((tile, model), lambda i: (i, 0))
-    half_spec = pl.BlockSpec((tile, model), lambda i: (i % steps, 0))
     return pl.pallas_call(
-        functools.partial(last_kernel, steps=steps),
+        last_kernel,
         out_shape=jax.ShapeDtypeStruct((rows, model), F32),
-        grid=(2 * steps,),
-        in_specs=[smem(), row_spec, row_spec, pl.BlockSpec((1, model), lambda i: (0, 0))] + [half_spec] * 2,
+        grid=(rows // tile,),
+        in_specs=[row_spec, row_spec, pl.BlockSpec((1, model), lambda i: (0, 0)), row_spec],
         out_specs=row_spec,
         compiler_params=params(),
         cost_estimate=COST,
         name="tokens_grad",
-    )(core, d_one, x, gain, own, far)
+    )(d_one, x, gain, add)
 
 
 class Chain:
@@ -1393,7 +1576,6 @@
     assert tensor_size == 4 and MAX_PREFIX <= 4 * rows
 
     device = lax.axis_index("dp")
-    core = lax.axis_index("tensor") % 2
     x_at = device % 2
     z_at = device // 2
     sequence = device // group
@@ -1401,32 +1583,10 @@
     plane = member // 2
     prefix = jnp.sum(jnp.where(jnp.arange(prefix_len.shape[0]) == sequence, prefix_len, 0))
 
-    core_pairs = [(t, t ^ 1) for t in range(tensor_size)]
-    y_pairs = [(t, t ^ 2) for t in range(tensor_size)]
     x_pairs = [(d, d ^ 1) for d in range(dp_size)]
-
-    def core_swap(value):
-        return lax.ppermute(value, "tensor", core_pairs)
-
-    def y_swap(value):
-        return lax.ppermute(value, "tensor", y_pairs)
 
     def x_swap(value):
         return lax.ppermute(value, "dp", x_pairs)
-
-    def plane_of(d):
-        return (d % group) // 2
-
-    def own_half(value):
-        return lax.dynamic_slice_in_dim(value, core * half, half, 0)
-
-    def other_half(value):
-        return lax.dynamic_slice_in_dim(value, (1 - core) * half, half, 0)
-
-    def join(mine, theirs):
-        return jnp.where(
-            core == 0, jnp.concatenate([mine, theirs], 0), jnp.concatenate([theirs, mine], 0)
-        )
 
     positions = (member * rows + jnp.arange(rows)).astype(F32)
     counter = jnp.arange(width // 2, dtype=F32)
@@ -1439,9 +1599,7 @@
     q_gain_row = query_gain[None, :]
     k_gain_row = key_gain[None, :]
 
-    core_at = core[None].astype(jnp.int32)
-    core_not = 1 - core_at
-    h_one, qkv, q_raw, k_raw = project(
+    h_one, q, kv, q_raw, k_raw = project(
         tokens,
         norm_attn_row,
         (w_query, key_weight, value_weight),
@@ -1451,49 +1609,45 @@
         sin,
         "project",
     )
-    q = qkv[:, : w_query.shape[1]]
-    kv = qkv[:, w_query.shape[1] :]
     prefix_at = prefix[None].astype(jnp.int32)
     heads_b, lse, kv_all = attn_fwd(prefix_at, q, kv, group, dims)
+    fused = planes == group_planes and shard % 128 == 0
+    pieces = 3
+    middle, h_two, d_hidden, og_keep, og_came, heads_came = attention_out(
+        heads_b, w_out, tokens, norm_mlp_row, out_grad, w_down, planes, shard
+    )
+    outs = middle_of(
+        w_gate,
+        w_up,
+        h_two,
+        d_hidden,
+        middle,
+        out_grad,
+        norm_mlp_row,
+        w_out,
+        q,
+        heads_b,
+        lse,
+        [og_keep, og_came] if fused else None,
+        pieces,
+        planes,
+        shard,
+        width,
+    )
+    hidden, d_gate, d_up, hidden_came, d_attn, norm_mlp_part, qx, dox, h_two_keep, h_two_came = outs[:10]
+
+    grads = None
+    if fused:
+        grads = [hidden, hidden_came, og_keep, og_came, d_gate, h_two_keep, h_two_came]
+        grads += [heads_b, heads_came]
+        w_down_parts = outs[10:]
+    outs = back(prefix_at, qx, dox, kv_all, [d_attn, d_up], grads, group, planes, shard, pieces, dims)
+    dq, kv_grad, d_attn_keep, d_attn_came, up_came = outs[:5]
     chain = Chain()
-
-    away = dot(other_half(heads_b), w_out).astype(BF16)
-    came = core_swap(away)
-    both = (dot(own_half(heads_b), w_out) + came.astype(F32)).astype(BF16)
-    chain.mark(both)
-    y_came = y_swap(both)
-    (og,) = chain(out_grad)
-    og_keep, og_send = cut(x_at, core, [og], planes, shard, join)
-    og_came = x_swap(og_send)
-    chain.mark(og_keep)
-    d_hidden = dot(chain(out_grad)[0], w_down, NT)
-    chain.mark(d_hidden)
-    h_one_keep, h_one_send = cut(x_at, core, chain(h_one), planes, shard, join)
-    h_one_came = x_swap(h_one_send)
-    chain.mark(h_one_keep)
-    middle, h_two_half = norm_forward(core_at, both, *chain(y_came), tokens, norm_mlp_row)
-    chain.mark(h_two_half)
-    h_two_far = core_swap(h_two_half)
-    og_came = join(og_came, core_swap(og_came))
-    h_one_came = join(h_one_came, core_swap(h_one_came))
-    hidden, d_gate, d_up = mlp(core_at, h_two_half, *chain(h_two_far), w_gate, w_up, d_hidden)
-    chain.mark(hidden)
-
-    hidden_came, d_attn_half, d_attn_far, norm_mlp_part = d_middle_of(
-        hidden, d_gate, d_up, w_gate, w_up, middle, out_grad, norm_mlp_row
-    )
-    chain.mark(d_attn_far)
-    qx, dox = attn_prep(core_at, d_attn_half, d_attn_far, w_out, q, heads_b, lse, width)
-    chain.mark(dox)
-
-    fused = planes == group_planes and shard % 128 == 0
-    shared = [h_two_half, h_two_far, d_attn_half, d_attn_far, heads_b, d_up]
-    grads = [hidden, hidden_came, og_keep, og_came, d_gate] if fused else None
-    outs = back(prefix_at, qx, *chain(dox), kv_all, shared, grads, group, planes, shard, dims)
-    dq, kv_grad, h_two_keep, h_two_came, d_attn_keep, d_attn_came, heads_came, up_came = outs[:8]
     chain.mark(dq)
     if fused:
-        w_down_grad, w_gate_grad, w_out_grad = outs[8:]
+        w_down_grad = jnp.concatenate([*w_down_parts, outs[5]], axis=0)
+        w_gate_grad, w_out_grad = outs[6:]
     else:
         down_part = (dot(hidden, og_keep, TN) + dot(hidden_came, og_came, TN)).astype(BF16)
         w_down_grad = ZSum(down_part, 1, shard, planes, z_at).finish(chain)
@@ -1502,7 +1656,7 @@
         out_part = dot(heads_b, d_attn_keep, TN) + dot(heads_came, d_attn_came, TN)
         w_out_grad = ZSum(out_part.astype(BF16), 1, shard, planes, z_at).finish(chain)
 
-    up_grads = [h_one_keep, h_one_came, h_two_keep, h_two_came, d_up, up_came] if fused else None
+    up_grads = [h_two_keep, h_two_came, d_up, up_came] if fused else None
     outs = front(
         *chain(dq),
         kv_grad,
@@ -1512,6 +1666,7 @@
         k_gain_row,
         cos,
         sin,
+        h_one,
         (w_query, key_weight, value_weight),
         tokens,
         0.5 * norm_mlp_part,
@@ -1522,9 +1677,9 @@
         dp_size,
         shard,
     )
-    d_h_one, block_out, gains, dq_b, dq_came, dkv_b, dkv_came = outs[:7]
+    d_h_one, block_out, gains, dq_b, dq_came, dkv_b, dkv_came, h_one_keep, h_one_came = outs[:9]
     if fused:
-        w_up_grad, w_query_grad, w_kv_grad = outs[7:]
+        w_up_grad, w_query_grad, w_kv_grad = outs[9:]
     else:
         chain.mark(d_h_one)
 
@@ -1536,7 +1691,7 @@
         w_query_grad = by_rows(h_one_keep, h_one_came, dq_b, dq_came)
         w_kv_grad = by_rows(h_one_keep, h_one_came, dkv_b, dkv_came)
     kv_width = kv_heads * width
-    tokens_grad = tokens_grad_of(core_at, d_h_one, tokens, norm_attn_row, d_attn_half, d_attn_far)
+    tokens_grad = tokens_grad_of(d_h_one, tokens, norm_attn_row, d_attn)
     gains = gains[-1, 0]
     return (
         block_out,

time: 522 us -> 474 us (0.908)
  waiting for transfers between devices: 13.1 us -> 0 us
  matrix products: 12.5 us -> 0 us
  Pallas kernels: 460 us -> 450 us
  local copies, waits for them, and re-layouts: 15 us -> 8.63 us
    pallas_call x1, Pallas kernels: 202 us -> 144 us  [back(): pl.pallas_call(functools.partial(back_kernel, group=group, planes=planes,...]
    pallas_call x7 -> x3, Pallas kernels: 80.6 us -> 134 us  [the longest x1 91.6 us: middle_of(): pl.pallas_call(functools.partial(middle_kernel, planes=planes, shard=shar...]
    ppermute x7 -> x0, waiting for transfers between devices: 13.1 us -> none  [the longest x1 7.23 us: y_swap(): return lax.ppermute(value, 'tensor', y_pairs)]
    dot_general x3 -> x0, matrix products: 12.5 us -> none  [dot(): return lax.dot_general(left, right, dims, preferred_element_type=F32)]
    pallas_call x1, Pallas kernels: 134 us -> 129 us  [front(): pl.pallas_call(functools.partial(front_kernel, dp_size=dp_size, planes=pl...]
  transfers between devices with their start and end apart: 7 -> 0, of which waited for: 3 -> 0; matrix products, arithmetic and copies ran while one was open for 2% -> 0% of each run, Pallas kernels for 2% -> 0%
where the time goes in v5:
time: 474 us; the launch traced here: 465 us
  Pallas kernels  450 us (95%)
  local copies, waits for them, and re-layouts  8.63 us (2%)
  other arithmetic  4.9 us (1%)
    pallas_call x1, Pallas kernels, back(): pl.pallas_call(functools.partial(back_kernel, group=group, planes=planes,...  144 us
    pallas_call x1, Pallas kernels, front(): pl.pallas_call(functools.partial(front_kernel, dp_size=dp_size, planes=pl...  129 us
    pallas_call x1, Pallas kernels, middle_of(): pl.pallas_call(functools.partial(middle_kernel, planes=planes, shard=shar...  91.6 us
    pallas_call x1, Pallas kernels, attention_out(): pl.pallas_call(functools.partial(out_kernel, planes=planes, shard=shard,...  36.3 us
    pallas_call x1, Pallas kernels, attn_fwd(): pl.pallas_call(functools.partial(attn_fwd_kernel, group=group, kv_heads=k...  35.5 us

profile of v5, /device:TPU:0, one launch (start us, length us, event | category | flops | bytes accessed | tf_op | source)
XLA Modules:
  0.0 464.9 jit_solution(16554519465525827484)
XLA Ops:
  0.7 1.0 fusion
  1.7 1.0 pad_maximum_fusion.1
  2.7 7.6 %project.1 = (bf16[512,2048]{1,0:T(8,128)(2,1)}, bf16[512,512]{1,0:T(8,128)(2,1)}, bf16[512,512]{1,0:T(8,128)(2,1)}, f32[512,512]{1,0:T(8,128)}, f32[512,256]{1,0:T(8,128)}) custom-call(bf16[512,2048]{1,0:T(8,128)(2,1)} %x_ref.3, f32[1,2048]{1,0:T(1,128)} %bitcast.11, bf16[2048,512]{1,0:T(8,128)(2,1)} %refs_12_.1, bf16[2048,256]{1,0:T(8,128)(2,1)} %refs_13_.1, ...), custom_call_target="tpu_custom_call" | custom-call | flops 1000 | bytes 1000 | tf_op jit(solution)/shard_map/project/pallas_call | solution.py:334
  11.0 35.5 %attn_fwd.1 = (bf16[512,512]{1,0:T(8,128)(2,1)}, f32[512,512]{1,0:T(8,128)}, bf16[8,512,512]{2,1,0:T(8,128)(2,1)}) custom-call(s32[1]{0:T(128)S(6)} %select_n.22.prefix_ref.refs_0_, bf16[512,512]{1,0:T(8,128)(2,1)} %get-tuple-element.51.q_ref.refs_8_, bf16[512,512]{1,0:T(8,128)(2,1)} %get-tuple-element.52.kv_ref), custom_call_target="tpu_custom_call" | custom-call | flops 1000 | bytes 1000 | tf_op jit(solution)/shard_map/attn_fwd/pallas_call | solution.py:549
  46.4 36.3 %attention_out.1 = (f32[256,2048]{1,0:T(8,128)}, bf16[512,2048]{1,0:T(8,128)(2,1)}, f32[512,1536]{1,0:T(8,128)}, bf16[512,1024]{1,0:T(8,128)(2,1)}, bf16[512,1024]{1,0:T(8,128)(2,1)}, /*index=5*/bf16[512,512]{1,0:T(8,128)(2,1)}) custom-call(bf16[512,512]{1,0:T(8,128)(2,1)} %get-tuple-element.53.refs_0_.refs_9_.refs_13_, bf16[512,2048]{1,0:T(8,128)(2,1)} %refs_7_.1, ...), custom_call_target="tpu_custom_call" | custom-call | flops 1000 | bytes 1000 | tf_op jit(solution)/shard_map/attention_out/pallas_call | solution.py:983
  82.7 91.6 %middle.1 = (bf16[512,1536]{1,0:T(8,128)(2,1)}, bf16[512,1536]{1,0:T(8,128)(2,1)}, bf16[512,1536]{1,0:T(8,128)(2,1)}, bf16[512,1536]{1,0:T(8,128)(2,1)}, bf16[51...) custom-call(bf16[2048,1536]{1,0:T(8,128)(2,1)} %refs_0_.3, ...), custom_call_target="tpu_custom_call" | custom-call | flops 1000 | bytes 1000 | tf_op jit(solution)/shard_map/middle/pallas_call | solution.py:1205
  174.3 0.0 copy-start.6
  174.3 0.0 copy-start.7
  174.4 143.9 %back.1 = (f32[512,512]{1,0:T(8,128)}, f32[512,512]{1,0:T(8,128)}, bf16[512,1024]{1,0:T(8,128)(2,1)}, bf16[512,1024]{1,0:T(8,128)(2,1)}, bf16[512,1536]{1,0:T(8,...) custom-call(s32[1]{0:T(128)S(6)} %select_n.22.prefix_ref.refs_0_, ...), custom_call_target="tpu_custom_call" | custom-call | flops 1000 | bytes 1000 | tf_op jit(solution)/shard_map/back/pallas_call | solution.py:866
  318.3 0.0 copy-start.8
  318.3 0.0 copy-done.6
  318.3 0.0 copy-done.7
  318.3 2.3 pad_maximum_fusion
  320.6 0.0 copy-done.8
  320.6 0.6 broadcast_multiply_fusion.refs_2_
  321.2 128.6 %front.1 = (bf16[512,2048]{1,0:T(8,128)(2,1)}, bf16[512,2048]{1,0:T(8,128)(2,1)}, f32[6,1,4352]{2,1,0:T(1,128)}, bf16[512,512]{1,0:T(8,128)(2,1)}, bf16[512,512]...) custom-call(f32[1,128]{1,0:T(1,128)} %bitcast.19, ...), custom_call_target="tpu_custom_call" | custom-call | flops 1000 | bytes 1000 | tf_op jit(solution)/shard_map/front/pallas_call | solution.py:1440
  449.8 0.0 copy-start.5
  449.8 0.0 copy-start
  449.8 6.2 %tokens_grad.1 = f32[512,2048]{1,0:T(8,128)} custom-call(bf16[512,2048]{1,0:T(8,128)(2,1)} %get-tuple-element.79.d_ref, bf16[512,2048]{1,0:T(8,128)(2,1)} %x_ref.3, f32[1,2048]{1,0:T(1,128)} %bitcast.12, bf16[512,2048]{1,0:T(8,128)(2,1)} %get-tuple-element.64.refs_4_.add_ref), custom_call_target="tpu_custom_call" | custom-call | flops 1000 | bytes 1000 | tf_op jit(solution)/shard_map/tokens_grad/pallas_call | solution.py:1474
  456.1 0.0 copy-done.5
  456.1 0.8 fusion.1
  456.9 0.7 slice.23
  457.6 0.6 constant_dynamic-slice_fusion
  458.2 1.2 slice_bitcast_fusion
  459.4 0.0 copy-done
  459.4 1.3 copy.33
  460.7 0.0 copy-done.4
  460.8 0.8 copy.34
  461.6 0.8 copy.35
  462.4 0.0 copy-done.1
  462.4 1.1 copy.36
  463.5 1.1 copy.37
  (8 shorter events, 0.0 us)
Async XLA Ops:
  174.3 143.9 %copy-start.6 = (f32[512,256]{1,0:T(8,128)S(1)}, f32[512,256]{1,0:T(8,128)}, u32[]{:S(2)}) copy-start(f32[512,256]{1,0:T(8,128)} %get-tuple-element.86) | copy-start | bytes 1572868
  174.3 143.9 %copy-start.7 = (f32[512,256]{1,0:T(8,128)S(1)}, f32[512,256]{1,0:T(8,128)}, u32[]{:S(2)}) copy-start(f32[512,256]{1,0:T(8,128)} %get-tuple-element.87) | copy-start | bytes 1572868
  318.3 2.3 copy-start.8
  449.8 6.3 %copy-start.5 = (f32[256,512]{1,0:T(8,128)S(1)}, f32[256,512]{1,0:T(8,128)}, u32[]{:S(2)}) copy-start(f32[256,512]{1,0:T(8,128)} %get-tuple-element.82) | copy-start | bytes 1572868
  449.8 9.6 %copy-start = (bf16[512,2048]{1,0:T(8,128)(2,1)S(1)}, bf16[512,2048]{1,0:T(8,128)(2,1)}, u32[]{:S(2)}) copy-start(bf16[512,2048]{1,0:T(8,128)(2,1)} %get-tuple-element.113) | copy-start | bytes 6291460
  459.4 1.4 copy-start.4
  459.4 2.2 copy-start.3
  460.8 1.6 copy-start.1
  461.6 2.0 copy-start.2
